TPU v7x, 32 devices: a whole 2x2x4 slice. The times are simulated.
32 devices in a mesh: dp: 16 (over z, x, core), tensor: 2 (over y).
Axes of the slice: x: 2, y: 2, z: 4, core: 2. Of those that a mesh axis runs over, the one named last changes fastest.
Arguments:
- inputs: bfloat16 [131072, 512], P(('dp', 'tensor')), may hold values from -6 to 6
- cotangent: bfloat16 [131072, 512], P(('dp', 'tensor')), may hold values from -6 to 6
- lengths: int32 [128], P('dp'), may hold values from 256 to 1024, as said below
- time_span: int32 [128, 2], P('dp'), may hold values from 0 to 1024, as said below
- freq_span: int32 [128, 2], P('dp'), may hold values from 0 to 512, as said below
- gain_one: float32 [512], replicated, may hold values from 0.1 to 1.9
- shift_one: float32 [512], replicated, may hold values from -3 to 3
- qkv_weight: bfloat16 [512, 3, 512], P(None, None, 'tensor'), may hold values from -0.25 to 0.25
- qkv_bias: float32 [2, 512], P(None, 'tensor'), may hold values from -3 to 3
- out_weight: bfloat16 [512, 512], P('tensor'), may hold values from -0.5 to 0.5
- out_bias: float32 [512], replicated, may hold values from -2 to 2
- gain_two: float32 [512], replicated, may hold values from 0.1 to 1.9
- shift_two: float32 [512], replicated, may hold values from -3 to 3
- up_weight: bfloat16 [512, 2048], P(None, 'tensor'), may hold values from -0.25 to 0.25
- up_bias: float32 [2048], P('tensor'), may hold values from -3 to 3
- down_weight: bfloat16 [2048, 512], P('tensor'), may hold values from -0.1875 to 0.1875
- down_bias: float32 [512], replicated, may hold values from -2 to 2
Outputs:
- layer_out: bfloat16 [131072, 512], P(('dp', 'tensor'))
- input_grad: float32 [131072, 512], P(('dp', 'tensor'))
- grad_gain_one: float32 [512], replicated
- grad_shift_one: float32 [512], replicated
- grad_qkv_weight: float32 [512, 3, 512], P(None, None, 'tensor')
- grad_qkv_bias: float32 [2, 512], P(None, 'tensor')
- grad_out_weight: float32 [512, 512], P('tensor')
- grad_out_bias: float32 [512], replicated
- grad_gain_two: float32 [512], replicated
- grad_shift_two: float32 [512], replicated
- grad_up_weight: float32 [512, 2048], P(None, 'tensor')
- grad_up_bias: float32 [2048], P('tensor')
- grad_down_weight: float32 [2048, 512], P('tensor')
- grad_down_bias: float32 [512], replicated
Inputs may be any that keep to these rules, and one draw needn't show every extreme that they name: `lengths`: each length is at least 256, and some sequence has all 1024 frames. `time_span`: in each row the second entry minus the first lies between 0 and 40, and in some row it is exactly 40. `freq_span`: in each row the second entry minus the first lies between 0 and 27, and in some row it is exactly 27.
All inputs are finite; a program needn't handle non-finite values.
Results may differ from a plain program's by a relative error of at most 0.02.
Values may be sent and summed in bfloat16 or wider, within the bound.
No kernel may reach another device: no remote copies, remote signals or barrier semaphores. Data moves between devices by JAX's collectives and lax.ppermute only.
A program may use at most 320 MiB of HBM per device.

v0:
```python
import jax
import jax.numpy as jnp
from jax import lax
from jax.sharding import PartitionSpec as P

HEAD_DIM = 64
SEQ_LEN = 1024
LEFT = 10
RIGHT = 2
BLOCK = 512


epsilon = 1e-05
key_margin = 16


def layer_norm(values, norm_gain, norm_shift):
    centre = jnp.mean(values, axis=-1, keepdims=True)
    offset = values - centre
    variance = jnp.mean(offset * offset, axis=-1, keepdims=True)
    return offset * lax.rsqrt(variance + epsilon) * norm_gain + norm_shift


def inner_rows(left_side, right_side):
    return lax.dot_general(
        left_side, right_side, (((0,), (0,)), ((), ())), preferred_element_type=jnp.float32
    )


def times_transposed(left_side, right_side):
    return lax.dot_general(
        left_side, right_side, (((1,), (1,)), ((), ())), preferred_element_type=jnp.float32
    )


def block_scores(query_blk, key_blk, first_row, seq_length):
    query_pos = first_row + jnp.arange(BLOCK, dtype=jnp.int32)
    key_pos = first_row - key_margin + jnp.arange(BLOCK + 2 * key_margin, dtype=jnp.int32)
    relative = key_pos[None, :] - query_pos[:, None]
    inside = (relative >= -LEFT) & (relative <= RIGHT) & (key_pos[None, :] >= 0)
    allowed = inside & ((key_pos[None, :] < seq_length) | (relative == 0))
    scores = jnp.einsum(
        "qhe,khe->hqk", query_blk, key_blk, preferred_element_type=jnp.float32
    ) * HEAD_DIM ** (-0.5)
    return jnp.where(allowed[None], scores, -1000000000.0)


def block_slices(arrays, block_index, seq_lengths):
    queries, keys_pad, values_pad = arrays
    per_seq = SEQ_LEN // BLOCK
    seq_index = block_index // per_seq
    first_row = block_index % per_seq * BLOCK
    query_blk = lax.dynamic_slice_in_dim(
        lax.dynamic_index_in_dim(queries, seq_index, 0, False), first_row, BLOCK, 0
    )
    key_blk = lax.dynamic_slice_in_dim(
        lax.dynamic_index_in_dim(keys_pad, seq_index, 0, False),
        first_row,
        BLOCK + 2 * key_margin,
        0,
    )
    value_blk = lax.dynamic_slice_in_dim(
        lax.dynamic_index_in_dim(values_pad, seq_index, 0, False),
        first_row,
        BLOCK + 2 * key_margin,
        0,
    )
    seq_length = lax.dynamic_index_in_dim(seq_lengths, seq_index, 0, False)
    return (seq_index, first_row, query_blk, key_blk, value_blk, seq_length)


def attend_forward(arrays, seq_lengths):
    block_total = arrays[0].shape[0] * (SEQ_LEN // BLOCK)

    def one_block(block_index):
        seq_index, first_row, query_blk, key_blk, value_blk, seq_length = block_slices(
            arrays, block_index, seq_lengths
        )
        scores = block_scores(query_blk, key_blk, first_row, seq_length)
        top_score = jnp.max(scores, axis=-1, keepdims=True)
        weights = jnp.exp(scores - top_score)
        row_total = jnp.sum(weights, axis=-1, keepdims=True)
        probabilities = (weights / row_total).astype(jnp.bfloat16)
        context = jnp.einsum(
            "hqk,khe->qhe", probabilities, value_blk, preferred_element_type=jnp.float32
        )
        return (context.astype(jnp.bfloat16), (top_score + jnp.log(row_total))[..., 0])

    return lax.map(one_block, jnp.arange(block_total, dtype=jnp.int32))


def attend_backward(arrays, seq_lengths, log_totals, grad_context):
    queries, keys_pad, values_pad = arrays
    block_total = queries.shape[0] * (SEQ_LEN // BLOCK)
    width = BLOCK + 2 * key_margin
    local_heads = queries.shape[2]
    score_scale = HEAD_DIM ** (-0.5)

    def one_block(carry, block_index):
        key_grads, value_grads = carry
        seq_index, first_row, query_blk, key_blk, value_blk, seq_length = block_slices(
            arrays, block_index, seq_lengths
        )
        grad_blk = lax.dynamic_slice_in_dim(
            lax.dynamic_index_in_dim(grad_context, seq_index, 0, False), first_row, BLOCK, 0
        )
        scores = block_scores(query_blk, key_blk, first_row, seq_length)
        probabilities = jnp.exp(
            scores - lax.dynamic_index_in_dim(log_totals, block_index, 0, False)[..., None]
        )
        grad_prob = jnp.einsum(
            "qhe,khe->hqk", grad_blk, value_blk, preferred_element_type=jnp.float32
        )
        inner = jnp.sum(probabilities * grad_prob, axis=-1, keepdims=True)
        grad_score = (probabilities * (grad_prob - inner)).astype(jnp.bfloat16)
        query_grad = (
            jnp.einsum("hqk,khe->qhe", grad_score, key_blk, preferred_element_type=jnp.float32)
            * score_scale
        )
        key_term = (
            jnp.einsum("hqk,qhe->khe", grad_score, query_blk, preferred_element_type=jnp.float32)
            * score_scale
        )
        value_term = jnp.einsum(
            "hqk,qhe->khe",
            probabilities.astype(jnp.bfloat16),
            grad_blk,
            preferred_element_type=jnp.float32,
        )
        corner = (seq_index, first_row, 0, 0)
        extent = (1, width, local_heads, HEAD_DIM)
        key_grads = lax.dynamic_update_slice(
            key_grads, lax.dynamic_slice(key_grads, corner, extent) + key_term[None], corner
        )
        value_grads = lax.dynamic_update_slice(
            value_grads, lax.dynamic_slice(value_grads, corner, extent) + value_term[None], corner
        )
        return ((key_grads, value_grads), query_grad)

    empty = jnp.zeros(keys_pad.shape, jnp.float32)
    (key_grads, value_grads), query_grads = lax.scan(
        one_block, (empty, empty), jnp.arange(block_total, dtype=jnp.int32)
    )
    return (query_grads, key_grads, value_grads)


def attend_rows(row_values, weight_flat, bias_pair, seq_lengths):
    row_count = row_values.shape[0]
    width_here = weight_flat.shape[1] // 3
    heads_here = width_here // HEAD_DIM
    seq_count = row_count // SEQ_LEN
    bias_rows = jnp.concatenate(
        [bias_pair[0:1], jnp.zeros((1, width_here), jnp.float32), bias_pair[1:2]], axis=0
    )
    projected = (
        jnp.dot(row_values, weight_flat, preferred_element_type=jnp.float32)
        + bias_rows.reshape(3 * width_here)
    ).astype(jnp.bfloat16)
    shaped = projected.reshape(seq_count, SEQ_LEN, 3, heads_here, HEAD_DIM)
    pad_widths = ((0, 0), (key_margin, key_margin), (0, 0), (0, 0))
    arrays = (
        shaped[:, :, 0],
        jnp.pad(shaped[:, :, 1], pad_widths),
        jnp.pad(shaped[:, :, 2], pad_widths),
    )
    context, log_totals = attend_forward(arrays, seq_lengths)
    return (arrays, context.reshape(row_count, width_here), log_totals)


def attend_grads(arrays, seq_lengths, log_totals, grad_context):
    queries = arrays[0]
    seq_count = queries.shape[0]
    heads_here = queries.shape[2]
    row_count = seq_count * SEQ_LEN
    width_here = heads_here * HEAD_DIM
    grad_context = grad_context.reshape(seq_count, SEQ_LEN, heads_here, HEAD_DIM)
    query_grads, key_grads, value_grads = attend_backward(
        arrays, seq_lengths, log_totals, grad_context
    )
    return (
        jnp.stack(
            [
                query_grads.reshape(row_count, width_here),
                key_grads[:, key_margin : key_margin + SEQ_LEN].reshape(row_count, width_here),
                value_grads[:, key_margin : key_margin + SEQ_LEN].reshape(row_count, width_here),
            ],
            axis=1,
        )
        .astype(jnp.bfloat16)
        .reshape(row_count, 3 * width_here)
    )


def body(
    inputs,
    cotangent,
    lengths,
    time_span,
    freq_span,
    gain_one,
    shift_one,
    qkv_weight,
    qkv_bias,
    out_weight,
    out_bias,
    gain_two,
    shift_two,
    up_weight,
    up_bias,
    down_weight,
    down_bias,
):
    tok_rows = inputs.shape[0]
    model_width = inputs.shape[1]
    seq_count = lengths.shape[0]
    local_width = qkv_weight.shape[2]
    row_global = lax.axis_index("tensor") * tok_rows + jnp.arange(tok_rows, dtype=jnp.int32)
    row_seq = row_global // SEQ_LEN
    row_pos = row_global % SEQ_LEN
    chooser = row_seq[:, None] == jnp.arange(seq_count, dtype=jnp.int32)[None, :]

    def lookup(small_table):
        return jnp.sum(jnp.where(chooser, small_table[None, :], 0), axis=1)

    time_cut = (row_pos >= lookup(time_span[:, 0])) & (row_pos < lookup(time_span[:, 1]))
    column = jnp.arange(model_width, dtype=jnp.int32)
    freq_cut = (column[None, :] >= lookup(freq_span[:, 0])[:, None]) & (
        column[None, :] < lookup(freq_span[:, 1])[:, None]
    )
    keep_mask = ((~time_cut)[:, None] & ~freq_cut).astype(jnp.float32)
    masked = inputs.astype(jnp.float32) * keep_mask
    normed_one, norm_one_back = jax.vjp(layer_norm, masked, gain_one, shift_one)
    normed_one_low = normed_one.astype(jnp.bfloat16)
    rows_one = lax.all_gather(normed_one_low, "tensor", axis=0, tiled=True)
    weight_flat = qkv_weight.reshape(model_width, 3 * local_width)
    arrays, context, log_totals = attend_rows(rows_one, weight_flat, qkv_bias, lengths)
    branch = lax.psum_scatter(
        jnp.dot(context, out_weight, preferred_element_type=jnp.float32).astype(jnp.bfloat16),
        "tensor",
        scatter_dimension=0,
        tiled=True,
    ).astype(jnp.float32)
    middle = masked + branch + out_bias
    normed_two, norm_two_back = jax.vjp(layer_norm, middle, gain_two, shift_two)
    normed_low = normed_two.astype(jnp.bfloat16)
    rows_two = lax.all_gather(normed_low, "tensor", axis=0, tiled=True)
    hidden_pre = jnp.dot(rows_two, up_weight, preferred_element_type=jnp.float32) + up_bias
    hidden_act, gelu_back = jax.vjp(jax.nn.gelu, hidden_pre)
    hidden_low = hidden_act.astype(jnp.bfloat16)
    feed_out = lax.psum_scatter(
        jnp.dot(hidden_low, down_weight, preferred_element_type=jnp.float32).astype(jnp.bfloat16),
        "tensor",
        scatter_dimension=0,
        tiled=True,
    ).astype(jnp.float32)
    layer_out = (middle + feed_out + down_bias).astype(jnp.bfloat16)
    grad_out = cotangent.astype(jnp.float32)
    grad_rows = lax.all_gather(cotangent, "tensor", axis=0, tiled=True)
    grad_hidden = times_transposed(grad_rows, down_weight)
    down_grad = inner_rows(hidden_low, grad_rows)
    grad_pre = gelu_back(grad_hidden)[0].astype(jnp.bfloat16)
    up_grad = inner_rows(rows_two, grad_pre)
    up_bias_grad = jnp.sum(grad_pre.astype(jnp.float32), axis=0)
    grad_normed_two = lax.psum_scatter(
        times_transposed(grad_pre, up_weight).astype(jnp.bfloat16),
        "tensor",
        scatter_dimension=0,
        tiled=True,
    ).astype(jnp.float32)
    grad_middle_norm, gain_two_grad, shift_two_grad = norm_two_back(grad_normed_two)
    grad_middle = grad_out + grad_middle_norm
    grad_middle_low = grad_middle.astype(jnp.bfloat16)
    attn_grad_full = lax.all_gather(grad_middle_low, "tensor", axis=0, tiled=True)
    grad_context = times_transposed(attn_grad_full, out_weight).astype(jnp.bfloat16)
    out_grad = inner_rows(context, attn_grad_full)
    grad_projected = attend_grads(arrays, lengths, log_totals, grad_context)
    qkv_grad = inner_rows(rows_one, grad_projected).reshape(model_width, 3, local_width)
    bias_sums = jnp.sum(grad_projected.astype(jnp.float32), axis=0).reshape(3, local_width)
    qkv_bias_grad = jnp.stack([bias_sums[0], bias_sums[2]], axis=0)
    grad_normed_one = lax.psum_scatter(
        times_transposed(grad_projected, weight_flat).astype(jnp.bfloat16),
        "tensor",
        scatter_dimension=0,
        tiled=True,
    ).astype(jnp.float32)
    grad_masked_norm, gain_one_grad, shift_one_grad = norm_one_back(grad_normed_one)
    input_grad = (grad_middle + grad_masked_norm) * keep_mask
    shared = lax.psum(
        (
            gain_one_grad,
            shift_one_grad,
            jnp.sum(grad_middle, axis=0),
            gain_two_grad,
            shift_two_grad,
            jnp.sum(grad_out, axis=0),
        ),
        ("dp", "tensor"),
    )
    sharded = (
        lax.psum(qkv_grad.astype(jnp.bfloat16), "dp").astype(jnp.float32),
        lax.psum(qkv_bias_grad.astype(jnp.bfloat16), "dp").astype(jnp.float32),
        lax.psum(out_grad.astype(jnp.bfloat16), "dp").astype(jnp.float32),
        lax.psum(up_grad.astype(jnp.bfloat16), "dp").astype(jnp.float32),
        lax.psum(up_bias_grad.astype(jnp.bfloat16), "dp").astype(jnp.float32),
        lax.psum(down_grad.astype(jnp.bfloat16), "dp").astype(jnp.float32),
    )
    return (
        layer_out,
        input_grad,
        shared[0],
        shared[1],
        sharded[0],
        sharded[1],
        sharded[2],
        shared[2],
        shared[3],
        shared[4],
        sharded[3],
        sharded[4],
        sharded[5],
        shared[5],
    )


def solution(mesh):
    in_specs = (
        P(("dp", "tensor"), None),
        P(("dp", "tensor"), None),
        P("dp"),
        P("dp", None),
        P("dp", None),
        P(),
        P(),
        P(None, None, "tensor"),
        P(None, "tensor"),
        P("tensor", None),
        P(),
        P(),
        P(),
        P(None, "tensor"),
        P("tensor"),
        P("tensor", None),
        P(),
    )
    out_specs = (
        P(("dp", "tensor"), None),
        P(("dp", "tensor"), None),
        P(),
        P(),
        P(None, None, "tensor"),
        P(None, "tensor"),
        P("tensor", None),
        P(),
        P(),
        P(),
        P(None, "tensor"),
        P("tensor"),
        P("tensor", None),
        P(),
    )
    return jax.shard_map(body, mesh=mesh, in_specs=in_specs, out_specs=out_specs, check_vma=False)
```

profile of v0, /device:TPU:0, one launch (start us, length us, event | category | flops | bytes accessed | tf_op | source)
XLA Modules:
  0.0 2027.4 jit_solution(2315542039182934936)
XLA Ops:
  30.5 106.3 %all-gather.5.cloned.1.call-done = bf16[8192,512]{1,0:T(8,128)(2,1)} async-done(((bf16[4096,512]{1,0:T(8,128)(2,1)}), bf16[8192,512]{1,0:T(8,128)(2,1)}) %all-gather.5.cloned.1.call-update) | async-done | bytes 8388624 | tf_op jit(solution)/shard_map/all_gather | solution.py:234
  149.5 16.1 copy.59
  194.8 17.0 pad.7.clone
  211.9 194.1 %while.32 = (s32[]{:T(128)}, bf16[16,512,4,64]{1,3,2,0:T(8,128)(2,1)}, f32[16,4,512]{2,1,0:T(4,128)}, s32[16]{0:T(128)S(1)}, bf16[8,1056,4,64]{1,3,2,0:T(8,128)(...) while((s32[]{:T(128)}, ...), condition=%wide.region_9.10_spmd, body=%wide.region_6.9_spmd.sunk | while | flops 300941984 | bytes 15741893 | solution.py:89
  422.7 99.3 %reduce-scatter.5.cloned.1.call-done = bf16[4096,512]{1,0:T(8,128)(2,1)} async-done(((bf16[8192,512]{1,0:T(8,128)(2,1)}), bf16[4096,512]{1,0:T(8,128)(2,1)}) %reduce-scatter.5.cloned.1.call-update) | async-done | bytes 4194320 | tf_op jit(solution)/shard_map/reduce_scatter | solution.py:237
  547.5 103.5 %all-gather.7.cloned.1.call-done = bf16[8192,512]{1,0:T(8,128)(2,1)} async-done(((bf16[4096,512]{1,0:T(8,128)(2,1)}), bf16[8192,512]{1,0:T(8,128)(2,1)}) %all-gather.7.cloned.1.call-update) | async-done | bytes 8388624 | tf_op jit(solution)/shard_map/all_gather | solution.py:246
  651.0 26.9 %multiply_convert_fusion.1 = (bf16[8192,1024]{1,0:T(8,128)(2,1)}, f32[8192,1024]{1,0:T(8,128)}) fusion(f32[1024]{0:T(1024)S(1)} %copy-done.43, bf16[8192,512]{1,0:T(8,128)(2,1)} %all-gather.7.cloned.1.call-done, bf16[512,1024]{1,0:T(8,128)(2,1)S(1)} %copy-done), kind=kOutput, calls=%fused_computation.90 | convolution fusion | flops 8673820672 | bytes 59772928 | tf_op jit(solution)/shard_map/dot_general | solution.py:247
  678.0 78.6 %all-gather.9.cloned.1.call-done = bf16[8192,512]{1,0:T(8,128)(2,1)} async-done(((bf16[4096,512]{1,0:T(8,128)(2,1)}), bf16[8192,512]{1,0:T(8,128)(2,1)}) %all-gather.9.cloned.1.call-update) | async-done | bytes 8388624 | tf_op jit(solution)/shard_map/all_gather | solution.py:258
  756.5 36.4 %fusion.106 = (bf16[1024]{0:T(1024)(128)(2,1)}, bf16[8192,1024]{1,0:T(8,128)(2,1)}) fusion(f32[8192,1024]{1,0:T(8,128)} %get-tuple-element.490, f32[1024]{0:T(1024)S(1)} %copy-done.43, bf16[8192,512]{1,0:T(8,128)(2,1)} %all-gather.9.cloned.1.call-done, bf16[1024,512]{1,0:T(8,128)(2,1)S(1)} %copy-done.42), kind=kOutput, calls=%fused_computation.180 | convolution fusion | flops 8774482944 | bytes 59774976 | tf_op jit(solution)/shard_map/dot_general | solution.py:31
  793.0 17.1 convolution_convert_fusion
  810.1 16.9 convolution_convert_fusion.1
  827.1 82.3 %reduce-scatter.9.cloned.1.call-done = bf16[4096,512]{1,0:T(8,128)(2,1)} async-done(((bf16[8192,512]{1,0:T(8,128)(2,1)}), bf16[4096,512]{1,0:T(8,128)(2,1)}) %reduce-scatter.9.cloned.1.call-update) | async-done | bytes 4194320 | tf_op jit(solution)/shard_map/reduce_scatter | solution.py:264
  921.3 89.6 %reduce-scatter.7.cloned.1.call-done = bf16[4096,512]{1,0:T(8,128)(2,1)} async-done(((bf16[8192,512]{1,0:T(8,128)(2,1)}), bf16[4096,512]{1,0:T(8,128)(2,1)}) %reduce-scatter.7.cloned.1.call-update) | async-done | bytes 4194320 | tf_op jit(solution)/shard_map/reduce_scatter | solution.py:250
  1029.8 15.9 convolution_convert_fusion.4
  1045.6 16.4 convolution_convert_fusion.5
  1062.0 71.8 %all-gather.11.cloned.1.call-done = bf16[8192,512]{1,0:T(8,128)(2,1)} async-done(((bf16[4096,512]{1,0:T(8,128)(2,1)}), bf16[8192,512]{1,0:T(8,128)(2,1)}) %all-gather.11.cloned.1.call-update) | async-done | bytes 8388624 | tf_op jit(solution)/shard_map/all_gather | solution.py:273
  1176.8 426.5 %while.33 = (s32[]{:T(128)}, f32[8,1056,4,64]{1,3,2,0:T(8,128)}, f32[8,1056,4,64]{1,3,2,0:T(8,128)}, bf16[16,512,4,64]{1,3,2,0:T(8,128)(2,1)}, s32[16]{0:T(128)S...) while((s32[]{:T(128)}, f32[8,1056,4,64]{1,3,2,0:T(8,128)}, ...), condition=%wide.region_19.20_spmd, body=%wide.region_17.19_spmd.sunk | while | flops 732521088 | bytes 41819172 | solution.py:141
  1705.5 16.7 copy.75
  1729.9 13.6 fusion.91
  1743.6 13.8 bitcast_convert_fusion
  1758.1 33.6 %all-reduce.3 = (bf16[2,256]{1,0:T(2,128)(2,1)S(1)}, bf16[1024]{0:T(1024)(128)(2,1)S(1)}) all-reduce(bf16[2,256]{1,0:T(2,128)(2,1)S(1)} %pad_maximum_fusion.1, bf16[1024]{0:T(1024)(128)(2,1)S(1)} %copy-done.40), channel_id=1, replica_groups=mesh['dp'=16,'tensor'=2] {'dp'}, use_global_device_ids=true, to_apply=%region_29.30 | all-reduce | flops 1536 | bytes 6144 | tf_op jit(solution)/shard_map/psum | solution.py:301
  1792.9 55.1 %all-reduce.7.cloned.1.call-done = (bf16[512,3,256]{2,0,1:T(8,128)(2,1)}, bf16[256,512]{1,0:T(8,128)(2,1)}, bf16[512,1024]{1,0:T(8,128)(2,1)}, bf16[1024,512]{1,0:T(8,128)(2,1)}) async-done(((bf16[512,3,256]{2,0,1:T(8,128)(2,1)}, bf16[256,512]{1,0:T(8,128)(2,1)}, bf16[512,1024]{1,0:T(8,128)(2,1)}, bf16[1024,512]{1,0:T(8,128)(2,1)}), (bf16[512,3,256]{2,0,1:T(8,128)(2,1)}, bf16[256,512]{1,0:T(8,128)(2,1)}, ...) | async-done | bytes 3145744 | tf_op jit(solution)/shard_map/psum | solution.py:300
  1858.0 90.3 %reduce-scatter.11.cloned.1.call-done = bf16[4096,512]{1,0:T(8,128)(2,1)} async-done(((bf16[8192,512]{1,0:T(8,128)(2,1)}), bf16[4096,512]{1,0:T(8,128)(2,1)}) %reduce-scatter.11.cloned.1.call-update) | async-done | bytes 4194320 | tf_op jit(solution)/shard_map/reduce_scatter | solution.py:280
  1981.1 39.6 %all-reduce.2 = (f32[512]{0:T(512)}, f32[512]{0:T(512)}, f32[512]{0:T(512)}, f32[512]{0:T(512)}, f32[512]{0:T(512)}, /*index=5*/f32[512]{0:T(512)}) all-reduce(f32[512]{0:T(512)S(1)} %get-tuple-element.401, f32[512]{0:T(512)S(1)} %get-tuple-element.406, ...), channel_id=1, replica_groups=mesh['dp'=16,'tensor'=2] {'dp','tensor'}, use_global_device_ids=true, to_apply=%region_24.25 | all-reduce | flops 3072 | bytes 24576 | tf_op jit(solution)/shard_map/psum | solution.py:288
  (577 shorter events, 849.2 us)
Async XLA Ops:
  7.2 643.9 %copy-start = (bf16[512,1024]{1,0:T(8,128)(2,1)S(1)}, bf16[512,1024]{1,0:T(8,128)(2,1)}, u32[]{:S(2)}) copy-start(bf16[512,1024]{1,0:T(8,128)(2,1)} %param.34) | copy-start | bytes 3145732
  7.2 129.6 %all-gather.5.cloned.1.call-start = ((), (), s32[]{:S(2)}) async-start(), calls=%async_computation.4 | async-start | bytes 12582912 | tf_op jit(solution)/shard_map/all_gather | solution.py:234
  8.4 1002.5 %copy-start.11 = (s32[4096]{0:T(1024)}, s32[4096]{0:T(1024)S(1)}, u32[]{:S(2)}) copy-start(s32[4096]{0:T(1024)S(1)} %get-tuple-element.409) | copy-start | bytes 49156
  8.4 1002.5 %copy-start.13 = (s32[4096]{0:T(1024)}, s32[4096]{0:T(1024)S(1)}, u32[]{:S(2)}) copy-start(s32[4096]{0:T(1024)S(1)} %get-tuple-element.410) | copy-start | bytes 49156
  8.5 1002.5 %copy-start.17 = (pred[4096]{0:T(1024)(128)(4,1)}, pred[4096]{0:T(1024)(128)(4,1)S(1)}, u32[]{:S(2)}) copy-start(pred[4096]{0:T(1024)(128)(4,1)S(1)} %and_not_fusion) | copy-start | bytes 12292
  23.8 125.8 %copy-start.27 = (f32[4096]{0:T(1024)}, f32[4096]{0:T(1024)S(1)}, u32[]{:S(2)}) copy-start(f32[4096]{0:T(1024)S(1)} %multiply_reduce_fusion.2) | copy-start | bytes 49156
  23.8 125.7 %copy-start.23 = (f32[4096]{0:T(1024)}, f32[4096]{0:T(1024)S(1)}, u32[]{:S(2)}) copy-start(f32[4096]{0:T(1024)S(1)} %fusion.101) | copy-start | bytes 49156
  30.0 492.1 %reduce-scatter.5.cloned.1.call-start = ((), (), s32[]{:S(2)}) async-start(), calls=%async_computation.5 | async-start | bytes 12582912 | tf_op jit(solution)/shard_map/reduce_scatter | solution.py:237
  422.7 117.3 %copy-start.34 = (f32[512]{0:T(512)S(1)}, f32[512]{0:T(512)}, u32[]{:S(2)}) copy-start(f32[512]{0:T(512)} %param.32) | copy-start | bytes 6148
  422.7 117.3 %copy-start.38 = (f32[512]{0:T(512)S(1)}, f32[512]{0:T(512)}, u32[]{:S(2)}) copy-start(f32[512]{0:T(512)} %param.33) | copy-start | bytes 6148
  422.7 228.4 %all-gather.7.cloned.1.call-start = ((), (), s32[]{:S(2)}) async-start(), calls=%async_computation.6 | async-start | bytes 12582912 | tf_op jit(solution)/shard_map/all_gather | solution.py:246
  546.9 209.7 %all-gather.9.cloned.1.call-start = ((), (), s32[]{:S(2)}) async-start(), calls=%async_computation.8 | async-start | bytes 12582912 | tf_op jit(solution)/shard_map/all_gather | solution.py:258
  547.4 209.1 %copy-start.42 = (bf16[1024,512]{1,0:T(8,128)(2,1)S(1)}, bf16[1024,512]{1,0:T(8,128)(2,1)}, u32[]{:S(2)}) copy-start(bf16[1024,512]{1,0:T(8,128)(2,1)} %param.36) | copy-start | bytes 3145732
  547.5 362.0 %reduce-scatter.9.cloned.1.call-start = ((), (), s32[]{:S(2)}) async-start(), calls=%async_computation.9 | async-start | bytes 12582912 | tf_op jit(solution)/shard_map/reduce_scatter | solution.py:264
  810.1 200.8 %reduce-scatter.7.cloned.1.call-start = ((), (), s32[]{:S(2)}) async-start(), calls=%async_computation.7 | async-start | bytes 12582912 | tf_op jit(solution)/shard_map/reduce_scatter | solution.py:250
  827.1 183.8 %copy-start.39 = (f32[512]{0:T(512)S(1)}, f32[512]{0:T(512)}, u32[]{:S(2)}) copy-start(f32[512]{0:T(512)} %param.37) | copy-start | bytes 6148
  827.1 306.8 %all-gather.11.cloned.1.call-start = ((), (), s32[]{:S(2)}) async-start(), calls=%async_computation.10 | async-start | bytes 12582912 | tf_op jit(solution)/shard_map/all_gather | solution.py:273
  1029.7 818.3 %all-reduce.7.cloned.1.call-start = ((), (), s32[]{:S(2)}) async-start(), calls=%async_computation.12 | async-start | bytes 6291456 | tf_op jit(solution)/shard_map/psum | solution.py:300
  1743.6 204.8 %reduce-scatter.11.cloned.1.call-start = ((), (), s32[]{:S(2)}) async-start(), calls=%async_computation.11 | async-start | bytes 12582912 | tf_op jit(solution)/shard_map/reduce_scatter | solution.py:280
  1757.4 191.0 %copy-start.12 = (s32[4096]{0:T(1024)S(1)}, s32[4096]{0:T(1024)}, u32[]{:S(2)}) copy-start(s32[4096]{0:T(1024)} %copy-done.11) | copy-start | bytes 49156
  1757.4 191.0 %copy-start.14 = (s32[4096]{0:T(1024)S(1)}, s32[4096]{0:T(1024)}, u32[]{:S(2)}) copy-start(s32[4096]{0:T(1024)} %copy-done.13) | copy-start | bytes 49156
  1757.4 191.0 %copy-start.18 = (pred[4096]{0:T(1024)(128)(4,1)S(1)}, pred[4096]{0:T(1024)(128)(4,1)}, u32[]{:S(2)}) copy-start(pred[4096]{0:T(1024)(128)(4,1)} %copy-done.17) | copy-start | bytes 12292
  1757.4 191.0 %copy-start.20 = (f32[4096]{0:T(1024)S(1)}, f32[4096]{0:T(1024)}, u32[]{:S(2)}) copy-start(f32[4096]{0:T(1024)} %copy-done.19) | copy-start | bytes 49156
  1757.4 190.9 %copy-start.33 = (f32[512]{0:T(512)S(1)}, f32[512]{0:T(512)}, u32[]{:S(2)}) copy-start(f32[512]{0:T(512)} %param.26) | copy-start | bytes 6148
  (31 other events, 1060.4 us)
Sparse Core Ops, SparseCore 0:
  30.1 106.6 all-gather.4
  422.8 99.2 reduce-scatter.4
  547.0 104.0 all-gather.6
  652.5 103.9 all-gather.8
  810.2 99.2 reduce-scatter.8
  911.6 99.2 reduce-scatter.6
  1029.8 104.0 all-gather.10
  1743.7 104.2 all-reduce.6
  1850.4 97.9 reduce-scatter.10
where the time goes:
time: 2040 us; the launch traced here: 2030 us
  waiting for transfers between devices  778 us (38%)
  matrix products  470 us (23%)
  local copies, waits for them, and re-layouts  373 us (18%)
  other arithmetic  212 us (10%)
  loops' own time  107 us (5%)
  blocking collectives  73.2 us (4%)
    all_gather x1, waiting for transfers between devices, body(): rows_one = lax.all_gather(normed_one_low, 'tensor', axis=0, tiled=True)  106 us
    all_gather x1, waiting for transfers between devices, body(): rows_two = lax.all_gather(normed_low, 'tensor', axis=0, tiled=True)  104 us
    reduce_scatter x1, waiting for transfers between devices, body(): lax.psum_scatter(jnp.dot(context, out_weight, preferred_element_type=jnp....  99.3 us
    reduce_scatter x1, waiting for transfers between devices, body(): lax.psum_scatter(times_transposed(grad_projected, weight_flat).astype(jnp...  90.3 us
    reduce_scatter x1, waiting for transfers between devices, body(): lax.psum_scatter(jnp.dot(hidden_low, down_weight, preferred_element_type=...  89.6 us
    reduce_scatter x1, waiting for transfers between devices, body(): lax.psum_scatter(times_transposed(grad_pre, up_weight).astype(jnp.bfloat1...  82.3 us
    all_gather x1, waiting for transfers between devices, body(): grad_rows = lax.all_gather(cotangent, 'tensor', axis=0, tiled=True)  78.6 us
    another operation x6, local copies, waits for them, and re-layouts, attend_grads(): jnp.stack([query_grads.reshape(row_count, width_here), key_grads[:, key_m...  76.4 us
  transfers between devices with their start and end apart: 9, of which 9 were waited for; matrix products, arithmetic and copies ran while one was open for 6% of the time, Pallas kernels for 0%

commit v1 on v0

v1 whole, which is shorter than its diff:
```python
import jax
import jax.numpy as jnp
from jax import lax
from jax.experimental import pallas as pl
from jax.experimental.pallas import tpu as pltpu
from jax.sharding import PartitionSpec as P

HEAD_DIM = 64
SEQ_LEN = 1024
LEFT = 10
RIGHT = 2
QB = 64
MARGIN = 16
WIN = QB + 2 * MARGIN
NBLK = SEQ_LEN // QB
EPS = 1e-05
NEG = -1000000000.0
VMEM = 60 * 1024 * 1024
F32 = jnp.float32
BF16 = jnp.bfloat16


def dot_nn(a, b):
    return jnp.dot(a, b, preferred_element_type=F32)


def dot_nt(a, b):
    return lax.dot_general(a, b, (((1,), (1,)), ((), ())), preferred_element_type=F32)


def dot_tn(a, b):
    return lax.dot_general(a, b, (((0,), (0,)), ((), ())), preferred_element_type=F32)


def keep_of(shape, first_pos, seq, tspan, fspan):
    pos = first_pos + lax.broadcasted_iota(jnp.int32, (shape[0], 1), 0)
    col = lax.broadcasted_iota(jnp.int32, (1, shape[1]), 1)
    rows = jnp.where((pos >= tspan[seq, 0]) & (pos < tspan[seq, 1]), 0.0, 1.0)
    cols = jnp.where((col >= fspan[seq, 0]) & (col < fspan[seq, 1]), 0.0, 1.0)
    return rows * cols


def normalize(v):
    off = v - jnp.mean(v, axis=-1, keepdims=True)
    r = lax.rsqrt(jnp.mean(off * off, axis=-1, keepdims=True) + EPS)
    return off * r, r


def head_mask(scale, heads):
    row = lax.broadcasted_iota(jnp.int32, (heads * QB, heads * HEAD_DIM), 0)
    col = lax.broadcasted_iota(jnp.int32, (heads * QB, heads * HEAD_DIM), 1)
    return jnp.where(row // QB == col // HEAD_DIM, scale, 0.0).astype(BF16)


def spread(block, mask, heads):
    return jnp.concatenate([block] * heads, axis=0) * mask


def pair_rows(probs, window, heads):
    out = []
    low = lax.broadcasted_iota(jnp.int32, (QB, 2 * HEAD_DIM), 1) < HEAD_DIM
    for p in range(heads // 2):
        both = dot_tn(
            probs[:, p * 2 * QB : (p + 1) * 2 * QB],
            window[:, p * 2 * HEAD_DIM : (p + 1) * 2 * HEAD_DIM],
        )
        out.append(jnp.where(low, both[:QB], both[QB:]))
    return jnp.concatenate(out, axis=1)


def attend(length, proj, kpad, vpad, ctx, probs_out, heads):
    width = heads * HEAD_DIM
    edge = jnp.zeros((MARGIN, width), BF16)
    for pad, j in ((kpad, 1), (vpad, 2)):
        pad[0:MARGIN, :] = edge
        pad[MARGIN + SEQ_LEN :, :] = edge
        pad[MARGIN : MARGIN + SEQ_LEN, :] = proj[:, j * width : (j + 1) * width]
    mask = head_mask(HEAD_DIM**-0.5, heads)
    key = lax.broadcasted_iota(jnp.int32, (WIN, heads * QB), 0)
    query = lax.broadcasted_iota(jnp.int32, (WIN, heads * QB), 1) % QB
    rel = key - MARGIN - query
    band = jnp.where((rel >= -LEFT) & (rel <= RIGHT), 0.0, NEG)
    diagonal = jnp.where(rel == 0, 0.0, NEG)

    def block(b, carry):
        first = pl.multiple_of(b * QB, QB)
        k_win = kpad[pl.ds(first, WIN), :]
        v_win = vpad[pl.ds(first, WIN), :]
        q_all = spread(proj[pl.ds(first, QB), 0:width], mask, heads)
        pos = key + (first - MARGIN)
        live = (pos >= 0) & (pos < length)
        scores = dot_nt(k_win, q_all) + jnp.where(live, band, diagonal)
        weights = jnp.exp(scores - jnp.max(scores, axis=0, keepdims=True))
        probs = (weights / jnp.sum(weights, axis=0, keepdims=True)).astype(BF16)
        probs_out[pl.ds(pl.multiple_of(b * WIN, WIN), WIN), :] = probs
        ctx[pl.ds(first, QB), :] = pair_rows(probs, v_win, heads).astype(BF16)
        return carry

    lax.fori_loop(0, NBLK, block, 0, unroll=4)


def first_kernel(heads, length, tspan, fspan, x, w, bias, gain, shift, n1, proj, ctx, probs, kpad, vpad):
    s = pl.program_id(0)
    masked = x[...].astype(F32) * keep_of(x.shape, 0, s, tspan, fspan)
    n1[...] = (normalize(masked)[0] * gain[...] + shift[...]).astype(BF16)
    proj[...] = (dot_nn(n1[...], w[...]) + bias[...]).astype(BF16)
    attend(length[s], proj, kpad, vpad, ctx, probs, heads)


def second_kernel(heads, length, n1, w, bias, proj, ctx, probs, kpad, vpad):
    s = pl.program_id(0)
    proj[...] = (dot_nn(n1[...], w[...]) + bias[...]).astype(BF16)
    attend(length[s], proj, kpad, vpad, ctx, probs, heads)


def const_spec(shape):
    return pl.BlockSpec(shape, lambda *_: (0,) * len(shape), pipeline_mode=pl.Buffered(1))


def rows_spec(rows, cols):
    return pl.BlockSpec((rows, cols), lambda i, *_: (i, 0))


def params():
    return pltpu.CompilerParams(vmem_limit_bytes=VMEM, dimension_semantics=("arbitrary",))


def attention_forward(first, length, tspan, fspan, rows, w, bias, gain, shift):
    total, width_in = rows.shape
    seqs = total // SEQ_LEN
    width = w.shape[1] // 3
    heads = width // HEAD_DIM
    outs = [
        jax.ShapeDtypeStruct((total, 3 * width), BF16),
        jax.ShapeDtypeStruct((total, width), BF16),
        jax.ShapeDtypeStruct((seqs * NBLK * WIN, heads * QB), BF16),
    ]
    out_specs = [
        rows_spec(SEQ_LEN, 3 * width),
        rows_spec(SEQ_LEN, width),
        rows_spec(NBLK * WIN, heads * QB),
    ]
    scratch = [pltpu.VMEM((SEQ_LEN + 2 * MARGIN, width), BF16)] * 2
    flops = 2 * total * width_in * 3 * width + 8 * total * WIN * width
    cost = pl.CostEstimate(flops=flops, bytes_accessed=total * (width_in + 6 * width) * 2, transcendentals=0)
    in_specs = [rows_spec(SEQ_LEN, width_in), const_spec(w.shape), const_spec(bias.shape)]
    if first:
        in_specs += [const_spec(gain.shape), const_spec(shift.shape)]
        outs = [jax.ShapeDtypeStruct(rows.shape, BF16)] + outs
        out_specs = [rows_spec(SEQ_LEN, width_in)] + out_specs
        scalars = (length, tspan, fspan)
        args = (rows, w, bias, gain, shift)
    else:
        scalars = (length,)
        args = (rows, w, bias)

    def body(*refs):
        (first_kernel if first else second_kernel)(heads, *refs)

    return pl.pallas_call(
        body,
        grid_spec=pltpu.PrefetchScalarGridSpec(
            num_scalar_prefetch=len(scalars),
            grid=(seqs,),
            in_specs=in_specs,
            out_specs=out_specs,
            scratch_shapes=scratch,
        ),
        out_shape=outs,
        compiler_params=params(),
        cost_estimate=cost,
        name="attend_first" if first else "attend_second",
    )(*scalars, *args)


TM = 512
FC = 512
GELU_A = 0.7978845608028654
GELU_B = 0.7978845608028654 * 0.044715


def middle_kernel(
    per_seq, tspan, fspan,
    x, cot, ctx_a, ctx_b, wo_a, wo_b, wu_a, wu_b, wd_a, wd_b,
    bo, gain, shift, bu_a, bu_b, bd,
    layer_out, gmid_out, gctx_a, gctx_b, gwo_a, gwo_b, gwu_a, gwu_b, gwd_a, gwd_b, gbu_a, gbu_b, small,
    acc_o, acc_u, acc_d, acc_bu, acc_small, n2_s, gn2_s, out_s,
):
    i = pl.program_id(0)

    @pl.when(i == 0)
    def _():
        acc_o[...] = jnp.zeros_like(acc_o)
        acc_u[...] = jnp.zeros_like(acc_u)
        acc_d[...] = jnp.zeros_like(acc_d)
        acc_bu[...] = jnp.zeros_like(acc_bu)
        acc_small[...] = jnp.zeros_like(acc_small)

    rows = x.shape[0]
    keep = keep_of(x.shape, (i % per_seq) * rows, i // per_seq, tspan, fspan)
    mid = x[...].astype(F32) * keep + dot_nn(ctx_a[...], wo_a[...]) + dot_nn(ctx_b[...], wo_b[...]) + bo[...]
    nn, r = normalize(mid)
    n2_s[...] = (nn * gain[...] + shift[...]).astype(BF16)
    out_s[...] = mid + bd[...]
    n2 = n2_s[...]
    g = cot[...]
    n2_t = n2.T
    g_t = g.T
    half = wu_a.shape[1]
    for part, (wu, wd, bu) in enumerate(((wu_a, wd_a, bu_a), (wu_b, wd_b, bu_b))):
        for c in range(half // FC):
            cs = slice(c * FC, (c + 1) * FC)
            ts = slice(part * half + c * FC, part * half + (c + 1) * FC)
            v = dot_nn(n2, wu[:, cs]) + bu[:, cs]
            v2 = v * v
            t = jnp.tanh(v * (GELU_A + GELU_B * v2))
            p = 0.5 + 0.5 * t
            hidden = (v * p).astype(BF16)
            slope = p + (v * (0.5 - 0.5 * (t * t))) * (GELU_A + (3 * GELU_B) * v2)
            gpre = (slope * dot_nt(g, wd[cs, :])).astype(BF16)
            out_s[...] += dot_nn(hidden, wd[cs, :])
            acc_d[:, ts] += dot_nn(g_t, hidden)
            acc_u[:, ts] += dot_nn(n2_t, gpre)
            acc_bu[:, ts] += jnp.sum(gpre.astype(F32), axis=0, keepdims=True)
            back = dot_nt(gpre, wu[:, cs])
            if part == 0 and c == 0:
                gn2_s[...] = back
            else:
                gn2_s[...] += back
    layer_out[...] = out_s[...].astype(BF16)
    gn2 = gn2_s[...]
    gf = g.astype(F32)
    u = gn2 * gain[...]
    un = u * nn
    gm = gf + r * (u - jnp.mean(u, axis=-1, keepdims=True) - nn * jnp.mean(un, axis=-1, keepdims=True))
    gmid_out[...] = gm
    acc_small[0:1, :] += jnp.sum(gn2 * nn, axis=0, keepdims=True)
    acc_small[1:2, :] += jnp.sum(gn2, axis=0, keepdims=True)
    acc_small[2:3, :] += jnp.sum(gm, axis=0, keepdims=True)
    acc_small[3:4, :] += jnp.sum(gf, axis=0, keepdims=True)
    gmb = gm.astype(BF16)
    gctx_a[...] = dot_nt(gmb, wo_a[...]).astype(BF16)
    gctx_b[...] = dot_nt(gmb, wo_b[...]).astype(BF16)
    width = ctx_a.shape[1]
    acc_o[0:width, :] += dot_tn(ctx_a[...], gmb)
    acc_o[width:, :] += dot_tn(ctx_b[...], gmb)

    @pl.when(i == pl.num_programs(0) - 1)
    def _():
        gwo_a[...] = acc_o[0:width, :].astype(BF16)
        gwo_b[...] = acc_o[width:, :].astype(BF16)
        gwu_a[...] = acc_u[:, :half].astype(BF16)
        gwu_b[...] = acc_u[:, half:].astype(BF16)
        gwd_a[...] = acc_d[:, :half].astype(BF16).T
        gwd_b[...] = acc_d[:, half:].astype(BF16).T
        gbu_a[...] = acc_bu[:, :half]
        gbu_b[...] = acc_bu[:, half:]
        small[...] = acc_small[...]


def middle_block(tspan, fspan, x, cot, ctx_a, ctx_b, wo, wu, wd, bo, gain, shift, bu, bd):
    total, d = x.shape
    width = ctx_a.shape[1]
    half = wu[0].shape[1]
    args = (x, cot, ctx_a, ctx_b, *wo, *wu, *wd, bo, gain, shift, *bu, bd)
    in_specs = [rows_spec(TM, d), rows_spec(TM, d), rows_spec(TM, width), rows_spec(TM, width)]
    in_specs += [const_spec(a.shape) for a in args[4:]]
    outs = [
        ((total, d), BF16, True), ((total, d), F32, True), ((total, width), BF16, True), ((total, width), BF16, True),
        ((width, d), BF16, False), ((width, d), BF16, False),
        ((d, half), BF16, False), ((d, half), BF16, False),
        ((half, d), BF16, False), ((half, d), BF16, False),
        ((1, half), F32, False), ((1, half), F32, False), ((8, d), F32, False),
    ]
    out_specs = [rows_spec(TM, s[1]) if tiled else const_spec(s) for s, _, tiled in outs]
    scratch = [
        pltpu.VMEM((2 * width, d), F32), pltpu.VMEM((d, 2 * half), F32), pltpu.VMEM((d, 2 * half), F32),
        pltpu.VMEM((1, 2 * half), F32), pltpu.VMEM((8, d), F32),
        pltpu.VMEM((TM, d), BF16), pltpu.VMEM((TM, d), F32), pltpu.VMEM((TM, d), F32),
    ]
    flops = 2 * total * d * (2 * half * 6 + 2 * width * 3)
    per_seq = SEQ_LEN // TM

    def body(*refs):
        middle_kernel(per_seq, *refs)

    return pl.pallas_call(
        body,
        grid_spec=pltpu.PrefetchScalarGridSpec(
            num_scalar_prefetch=2, grid=(total // TM,), in_specs=in_specs, out_specs=out_specs, scratch_shapes=scratch
        ),
        out_shape=[jax.ShapeDtypeStruct(s, t) for s, t, _ in outs],
        compiler_params=params(),
        cost_estimate=pl.CostEstimate(flops=flops, bytes_accessed=total * d * 14, transcendentals=0),
        name="feed_forward",
    )(tspan, fspan, *args)


def attend_back_kernel(heads, n1, proj, probs, gctx, gproj, gw, gb, kpad, vpad, dk, dv, acc, acc_b):
    s = pl.program_id(0)

    @pl.when(s == 0)
    def _():
        acc[...] = jnp.zeros_like(acc)
        acc_b[...] = jnp.zeros_like(acc_b)

    width = heads * HEAD_DIM
    edge = jnp.zeros((MARGIN, width), BF16)
    for pad, j in ((kpad, 1), (vpad, 2)):
        pad[0:MARGIN, :] = edge
        pad[MARGIN + SEQ_LEN :, :] = edge
        pad[MARGIN : MARGIN + SEQ_LEN, :] = proj[:, j * width : (j + 1) * width]
    mask = head_mask(1.0, heads)
    dk[0 : 2 * MARGIN, :] = jnp.zeros((2 * MARGIN, width), F32)
    dv[0 : 2 * MARGIN, :] = jnp.zeros((2 * MARGIN, width), F32)
    scale = HEAD_DIM**-0.5

    def block(b, carry):
        first = pl.multiple_of(b * QB, QB)
        k_win = kpad[pl.ds(first, WIN), :]
        v_win = vpad[pl.ds(first, WIN), :]
        q_all = spread(proj[pl.ds(first, QB), 0:width], mask, heads)
        o_all = spread(gctx[pl.ds(first, QB), :], mask, heads)
        pb = probs[pl.ds(pl.multiple_of(b * WIN, WIN), WIN), :]
        p = pb.astype(F32)
        gp = dot_nt(v_win, o_all)
        gs = (p * (gp - jnp.sum(p * gp, axis=0, keepdims=True))).astype(BF16)
        gproj[pl.ds(first, QB), 0:width] = (pair_rows(gs, k_win, heads) * scale).astype(BF16)
        for total, term in ((dk, dot_nn(gs, q_all) * scale), (dv, dot_nn(pb, o_all))):
            total[pl.ds(first, 2 * MARGIN), :] += term[: 2 * MARGIN]
            total[pl.ds(first + 2 * MARGIN, QB), :] = term[2 * MARGIN :]
        return carry

    lax.fori_loop(0, NBLK, block, 0, unroll=4)
    gproj[:, width : 2 * width] = dk[MARGIN : MARGIN + SEQ_LEN, :].astype(BF16)
    gproj[:, 2 * width :] = dv[MARGIN : MARGIN + SEQ_LEN, :].astype(BF16)
    gp_all = gproj[...]
    acc[...] += dot_tn(n1[...], gp_all)
    acc_b[...] += jnp.sum(gp_all.astype(F32), axis=0, keepdims=True)

    @pl.when(s == pl.num_programs(0) - 1)
    def _():
        gw[...] = acc[...].astype(BF16)
        gb[...] = acc_b[...]


def attention_backward(n1, proj, probs, gctx):
    total, d = n1.shape
    seqs = total // SEQ_LEN
    width = gctx.shape[1]
    heads = width // HEAD_DIM

    def body(*refs):
        attend_back_kernel(heads, *refs)

    pad = SEQ_LEN + 2 * MARGIN
    return pl.pallas_call(
        body,
        grid=(seqs,),
        in_specs=[
            rows_spec(SEQ_LEN, d), rows_spec(SEQ_LEN, 3 * width),
            rows_spec(NBLK * WIN, heads * QB), rows_spec(SEQ_LEN, width),
        ],
        out_specs=[rows_spec(SEQ_LEN, 3 * width), const_spec((d, 3 * width)), const_spec((1, 3 * width))],
        out_shape=[
            jax.ShapeDtypeStruct((total, 3 * width), BF16),
            jax.ShapeDtypeStruct((d, 3 * width), BF16),
            jax.ShapeDtypeStruct((1, 3 * width), F32),
        ],
        scratch_shapes=[
            pltpu.VMEM((pad, width), BF16), pltpu.VMEM((pad, width), BF16),
            pltpu.VMEM((pad, width), F32), pltpu.VMEM((pad, width), F32),
            pltpu.VMEM((d, 3 * width), F32), pltpu.VMEM((1, 3 * width), F32),
        ],
        compiler_params=params(),
        cost_estimate=pl.CostEstimate(
            flops=2 * total * d * 3 * width + 16 * total * WIN * width,
            bytes_accessed=total * (d + 9 * width) * 2, transcendentals=0,
        ),
        name="attend_back",
    )(n1, proj, probs, gctx)


def last_kernel(per_seq, tspan, fspan, x, gmid, gp_a, gp_b, w_a, w_b, gain, gin, small, acc):
    i = pl.program_id(0)

    @pl.when(i == 0)
    def _():
        acc[...] = jnp.zeros_like(acc)

    keep = keep_of(x.shape, (i % per_seq) * x.shape[0], i // per_seq, tspan, fspan)
    nn, r = normalize(x[...].astype(F32) * keep)
    gn1 = dot_nt(gp_a[...], w_a[...]) + dot_nt(gp_b[...], w_b[...])
    u = gn1 * gain[...]
    a = r * (u - jnp.mean(u, axis=-1, keepdims=True) - nn * jnp.mean(u * nn, axis=-1, keepdims=True))
    gin[...] = (gmid[...] + a) * keep
    acc[0:1, :] += jnp.sum(gn1 * nn, axis=0, keepdims=True)
    acc[1:2, :] += jnp.sum(gn1, axis=0, keepdims=True)

    @pl.when(i == pl.num_programs(0) - 1)
    def _():
        small[...] = acc[...]


def last_block(tspan, fspan, x, gmid, gp_a, gp_b, w_a, w_b, gain):
    total, d = x.shape
    per_seq = SEQ_LEN // TM

    def body(*refs):
        last_kernel(per_seq, *refs)

    return pl.pallas_call(
        body,
        grid_spec=pltpu.PrefetchScalarGridSpec(
            num_scalar_prefetch=2,
            grid=(total // TM,),
            in_specs=[
                rows_spec(TM, d), rows_spec(TM, d), rows_spec(TM, gp_a.shape[1]), rows_spec(TM, gp_b.shape[1]),
                const_spec(w_a.shape), const_spec(w_b.shape), const_spec(gain.shape),
            ],
            out_specs=[rows_spec(TM, d), const_spec((8, d))],
            scratch_shapes=[pltpu.VMEM((8, d), F32)],
        ),
        out_shape=[jax.ShapeDtypeStruct((total, d), F32), jax.ShapeDtypeStruct((8, d), F32)],
        compiler_params=params(),
        cost_estimate=pl.CostEstimate(
            flops=2 * total * d * (gp_a.shape[1] + gp_b.shape[1]), bytes_accessed=total * d * 16, transcendentals=0
        ),
        name="input_gradient",
    )(tspan, fspan, x, gmid, gp_a, gp_b, w_a, w_b, gain)


def make_body(mesh):
    tp = mesh.shape["tensor"]

    def pick(own, other):
        return own, other

    def halves(local, axis):
        if tp == 2:
            return local, lax.ppermute(local, "tensor", [(0, 1), (1, 0)])
        whole = lax.all_gather(local, "tensor", axis=axis, tiled=True)
        return tuple(jnp.split(whole, 2, axis=axis))

    def reduce_halves(own, other, axis):
        if tp == 2:
            own = own + lax.ppermute(other, "tensor", [(0, 1), (1, 0)])
        else:
            own = lax.psum_scatter(
                jnp.concatenate([own, other], axis=axis), "tensor", scatter_dimension=axis, tiled=True
            )
        return own

    def body(
        inputs, cotangent, lengths, time_span, freq_span, gain_one, shift_one, qkv_weight, qkv_bias,
        out_weight, out_bias, gain_two, shift_two, up_weight, up_bias, down_weight, down_bias,
    ):
        total, d = inputs.shape
        seqs = total // SEQ_LEN
        here = lax.axis_index("tensor") * seqs
        length = lax.dynamic_slice_in_dim(lengths, here, seqs, 0)
        tspan = lax.dynamic_slice_in_dim(time_span, here, seqs, 0)
        fspan = lax.dynamic_slice_in_dim(freq_span, here, seqs, 0)
        row = lambda v: v.reshape(1, -1)

        qkv = halves(qkv_weight, 2)
        qkv = [w.reshape(d, -1) for w in qkv]
        qb = halves(qkv_bias, 1)
        qb = [jnp.concatenate([b[0:1], jnp.zeros_like(b[0:1]), b[1:2]], axis=1) for b in qb]
        wo = halves(out_weight, 0)
        wu = halves(up_weight, 1)
        bu = [row(b) for b in halves(up_bias, 0)]
        wd = halves(down_weight, 0)

        n1, proj_a, ctx_a, probs_a = attention_forward(
            True, length, tspan, fspan, inputs, qkv[0], qb[0], row(gain_one), row(shift_one)
        )
        proj_b, ctx_b, probs_b = attention_forward(
            False, length, tspan, fspan, n1, qkv[1], qb[1], None, None
        )
        (
            layer_out, gmid, gctx_a, gctx_b, gwo_a, gwo_b, gwu_a, gwu_b, gwd_a, gwd_b, gbu_a, gbu_b, small_two
        ) = middle_block(
            tspan, fspan, inputs, cotangent, ctx_a, ctx_b, wo, wu, wd,
            row(out_bias), row(gain_two), row(shift_two), bu, row(down_bias),
        )
        gproj_b, gwq_b, gbq_b = attention_backward(n1, proj_b, probs_b, gctx_b)
        gproj_a, gwq_a, gbq_a = attention_backward(n1, proj_a, probs_a, gctx_a)
        input_grad, small_one = last_block(
            tspan, fspan, inputs, gmid, gproj_a, gproj_b, qkv[0], qkv[1], row(gain_one)
        )

        def finish(own, other, axis):
            return lax.psum(reduce_halves(own, other, axis), "dp").astype(F32)

        def three(v):
            return v.reshape(v.shape[0], 3, -1)

        g_qkv = finish(three(gwq_a), three(gwq_b), 2)
        g_qb = finish(three(gbq_a)[0], three(gbq_b)[0], 1)
        g_qb = jnp.stack([g_qb[0], g_qb[2]], axis=0)
        g_out = finish(gwo_a, gwo_b, 0)
        g_up = finish(gwu_a, gwu_b, 1)
        g_bu = finish(gbu_a[0], gbu_b[0], 0)
        g_down = finish(gwd_a, gwd_b, 0)
        small = lax.psum(jnp.concatenate([small_one[0:2], small_two[0:4]], axis=0), ("dp", "tensor"))
        return (
            layer_out, input_grad, small[0], small[1], g_qkv, g_qb, g_out, small[4], small[2], small[3],
            g_up, g_bu, g_down, small[5],
        )

    return body


def solution(mesh):
    in_specs = (
        P(("dp", "tensor"), None), P(("dp", "tensor"), None), P("dp"), P("dp", None), P("dp", None), P(), P(),
        P(None, None, "tensor"), P(None, "tensor"), P("tensor", None), P(), P(), P(), P(None, "tensor"),
        P("tensor"), P("tensor", None), P(),
    )
    out_specs = (
        P(("dp", "tensor"), None), P(("dp", "tensor"), None), P(), P(), P(None, None, "tensor"), P(None, "tensor"),
        P("tensor", None), P(), P(), P(), P(None, "tensor"), P("tensor"), P("tensor", None), P(),
    )
    return jax.shard_map(make_body(mesh), mesh=mesh, in_specs=in_specs, out_specs=out_specs, check_vma=False)
```

time: 2040 us -> 366 us (0.18)
  waiting for transfers between devices: 778 us -> 18.2 us
  matrix products: 470 us -> 0 us
  local copies, waits for them, and re-layouts: 373 us -> 15.6 us
  Pallas kernels: 0 us -> 214 us
  other arithmetic: 212 us -> 15.9 us
  loops' own time: 107 us -> 0 us
    dot_general x124 -> x0, matrix products: 470 us -> none  [the longest x4 75 us: times_transposed(): lax.dot_general(left_side, right_side, (((1,), (1,)), ((), ())), preferre...]
    reduce_scatter x4 -> x0, waiting for transfers between devices: 362 us -> none  [the longest x1 99.3 us: body(): lax.psum_scatter(jnp.dot(context, out_weight, preferred_element_type=jnp....]
    all_gather x4 -> x0, waiting for transfers between devices: 360 us -> none  [the longest x1 106 us: body(): rows_one = lax.all_gather(normed_one_low, 'tensor', axis=0, tiled=True)]
    pallas_call x0 -> x6, Pallas kernels: none -> 214 us  [the longest x1 86.2 us: middle_block(): pl.pallas_call(body, grid_spec=pltpu.PrefetchScalarGridSpec(num_scalar_pr...]
    reduce_sum x27 -> x0, other arithmetic: 117 us -> none  [the longest x3 33.3 us: layer_norm(): return offset * lax.rsqrt(variance + epsilon) * norm_gain + norm_shift]
    another operation x2 -> x0, loops' own time: 107 us -> none  [the longest x1 63.9 us: attend_backward(): lax.scan(one_block, (empty, empty), jnp.arange(block_total, dtype=jnp.int...]
    dynamic_update_slice x32 -> x0, local copies, waits for them, and re-layouts: 103 us -> none  [the longest x16 51.8 us: one_block(): lax.dynamic_update_slice(key_grads, lax.dynamic_slice(key_grads, corner,...]
    another operation x6 -> x3, local copies, waits for them, and re-layouts: 76.4 us -> 0.02 us  [the longest x2 0.02 us: body(): g_qb = finish(three(gbq_a)[0], three(gbq_b)[0], 1)]
  transfers between devices with their start and end apart: 9 -> 13, of which waited for: 9 -> 3; matrix products, arithmetic and copies ran while one was open for 6% -> 5% of each run, Pallas kernels for 0% -> 35%
where the time goes in v1:
time: 366 us; the launch traced here: 365 us
  Pallas kernels  214 us (58%)
  blocking collectives  73.6 us (20%)
  waiting for transfers between devices  18.2 us (5%)
  other arithmetic  15.9 us (4%)
  local copies, waits for them, and re-layouts  15.6 us (4%)
  between operations  14.2 us (4%)
  starting transfers between devices  13.6 us (4%)
    pallas_call x1, Pallas kernels, middle_block(): pl.pallas_call(body, grid_spec=pltpu.PrefetchScalarGridSpec(num_scalar_pr...  86.2 us
    pallas_call x2, Pallas kernels, attention_forward(): pl.pallas_call(body, grid_spec=pltpu.PrefetchScalarGridSpec(num_scalar_pr...  57 us
    pallas_call x2, Pallas kernels, attention_backward(): pl.pallas_call(body, grid=(seqs,), in_specs=[rows_spec(SEQ_LEN, d), rows_...  52.1 us
    psum x1, blocking collectives, body(): lax.psum(jnp.concatenate([small_one[0:2], small_two[0:4]], axis=0), ('dp'...  40 us
    psum x1, blocking collectives, finish(): return lax.psum(reduce_halves(own, other, axis), 'dp').astype(F32)  33.6 us
    pallas_call x1, Pallas kernels, last_block(): pl.pallas_call(body, grid_spec=pltpu.PrefetchScalarGridSpec(num_scalar_pr...  19 us
    ppermute x6, waiting for transfers between devices, reduce_halves(): own = own + lax.ppermute(other, 'tensor', [(0, 1), (1, 0)])  8.86 us
    add x6, other arithmetic, reduce_halves(): own = own + lax.ppermute(other, 'tensor', [(0, 1), (1, 0)])  8.07 us
  transfers between devices with their start and end apart: 13, of which 3 were waited for; matrix products, arithmetic and copies ran while one was open for 5% of the time, Pallas kernels for 35%

profile of v1, /device:TPU:0, one launch (start us, length us, event | category | flops | bytes accessed | tf_op | source)
XLA Modules:
  0.0 365.2 jit_solution(5029040035787593129)
XLA Ops:
  7.2 3.0 collective-permute-start.1
  11.8 2.0 collective-permute-start.3
  13.8 1.9 collective-permute-start.2
  21.8 30.2 %attend_first.1 = (bf16[4096,512]{1,0:T(8,128)(2,1)}, bf16[4096,768]{1,0:T(8,128)(2,1)}, bf16[4096,256]{1,0:T(8,128)(2,1)}, bf16[6144,256]{1,0:T(8,128)(2,1)}) custom-call(s32[4]{0:T(128)} %dynamic_slice.11.refs_0_, s32[4,2]{1,0:T(4,128)} %copy.48.refs_1_.refs_0_, s32[4,2]{1,0:T(4,128)} %copy.49.refs_2_.refs_1_, bf16[4096,512]{1,0:T(8,128)(2,1)} %refs_2_.3, ...), custom_call_target="tpu_custom_call" | custom-call | flops 4026531840 | bytes 16777216 | tf_op jit(solution)/shard_map/attend_first/pallas_call | solution.py:160
  53.2 26.8 %attend_second.1 = (bf16[4096,768]{1,0:T(8,128)(2,1)}, bf16[4096,256]{1,0:T(8,128)(2,1)}, bf16[6144,256]{1,0:T(8,128)(2,1)}) custom-call(s32[4]{0:T(128)} %dynamic_slice.11.refs_0_, bf16[4096,512]{1,0:T(8,128)(2,1)} %get-tuple-element.43.refs_1_.refs_0_, bf16[512,768]{1,0:T(8,128)(2,1)} %copy.42.refs_2_.refs_7_, f32[1,768]{1,0:T(1,128)} %get-tuple-element.98.refs_3_), custom_call_target="tpu_custom_call" | custom-call | flops 4026531840 | bytes 16777216 | tf_op jit(solution)/shard_map/attend_second/pallas_call | solution.py:160
  82.4 86.2 %feed_forward.1 = (bf16[4096,512]{1,0:T(8,128)(2,1)}, f32[4096,512]{1,0:T(8,128)}, bf16[4096,256]{1,0:T(8,128)(2,1)}, bf16[4096,256]{1,0:T(8,128)(2,1)}, bf16[25...) custom-call(s32[4,2]{1,0:T(4,128)} %copy.48.refs_1_.refs_0_, ...), custom_call_target="tpu_custom_call" | custom-call | flops 57982058496 | bytes 29360128 | tf_op jit(solution)/shard_map/feed_forward/pallas_call | solution.py:287
  169.3 1.4 collective-permute-start.9
  170.7 26.0 %attend_back.3 = (bf16[4096,768]{1,0:T(8,128)(2,1)}, bf16[512,768]{1,0:T(8,128)(2,1)}, f32[1,768]{1,0:T(1,128)}) custom-call(bf16[4096,512]{1,0:T(8,128)(2,1)} %get-tuple-element.43.refs_1_.refs_0_, bf16[4096,768]{1,0:T(8,128)(2,1)} %get-tuple-element.51.refs_1_, bf16[6144,256]{1,0:T(8,128)(2,1)} %get-tuple-element.52.refs_2_, ...), custom_call_target="tpu_custom_call" | custom-call | flops 4831838208 | bytes 23068672 | tf_op jit(solution)/shard_map/attend_back/pallas_call | solution.py:357
  196.8 2.3 copy.46
  199.7 1.4 collective-permute-start.8
  201.1 26.1 %attend_back.2 = (bf16[4096,768]{1,0:T(8,128)(2,1)}, bf16[512,768]{1,0:T(8,128)(2,1)}, f32[1,768]{1,0:T(1,128)}) custom-call(bf16[4096,512]{1,0:T(8,128)(2,1)} %get-tuple-element.43.refs_1_.refs_0_, bf16[4096,768]{1,0:T(8,128)(2,1)} %get-tuple-element.47.refs_1_, bf16[6144,256]{1,0:T(8,128)(2,1)} %get-tuple-element.48.refs_2_, ...), custom_call_target="tpu_custom_call" | custom-call | flops 4831838208 | bytes 23068672 | tf_op jit(solution)/shard_map/attend_back/pallas_call | solution.py:357
  227.2 1.6 copy.45
  228.8 8.8 %collective-permute-done.8 = bf16[256,512]{1,0:T(8,128)(2,1)S(1)} collective-permute-done((bf16[256,512]{1,0:T(8,128)(2,1)}, bf16[256,512]{1,0:T(8,128)(2,1)S(1)}, u32[]{:S(2)}, u32[]{:S(2)}) %collective-permute-start.8) | collective-permute-done | bytes 262176 | tf_op jit(solution)/shard_map/ppermute | solution.py:447
  238.4 2.2 add.38
  240.6 2.5 add.43
  243.1 2.6 add.41
  246.4 1.5 collective-permute-start.7
  247.9 19.0 %input_gradient.1 = (f32[4096,512]{1,0:T(8,128)}, f32[8,512]{1,0:T(8,128)}) custom-call(s32[4,2]{1,0:T(4,128)} %copy.48.refs_1_.refs_0_, s32[4,2]{1,0:T(4,128)} %copy.49.refs_2_.refs_1_, bf16[4096,512]{1,0:T(8,128)(2,1)} %refs_2_.3, f32[4096,512]{1,0:T(8,128)} %get-tuple-element.46.refs_3_, bf16[4096,768]{1,0:T(8,128)(2,1)} %get-tuple-element.50.refs_4_, ...), custom_call_target="tpu_custom_call" | custom-call | flops 6442450944 | bytes 33554432 | tf_op jit(solution)/shard_map/input_gradient/pallas_call | solution.py:412
  267.7 40.0 %psum.49 = f32[6,512]{1,0:T(8,128)S(1)} all-reduce(f32[6,512]{1,0:T(8,128)S(1)} %pad_maximum_fusion), channel_id=1, replica_groups=mesh['dp'=16,'tensor'=2] {'dp','tensor'}, use_global_device_ids=true, to_apply=%region_0.0 | all-reduce | flops 3072 | bytes 24576 | tf_op jit(solution)/shard_map/psum | solution.py:506
  308.3 33.6 %all-reduce = (f32[3,256]{1,0:T(4,128)S(1)}, f32[1024]{0:T(1024)}) all-reduce(f32[3,256]{1,0:T(4,128)S(1)} %add.39, f32[1024]{0:T(1024)S(1)} %add.42), channel_id=1, replica_groups=mesh['dp'=16,'tensor'=2] {'dp'}, use_global_device_ids=true, to_apply=%region_2.0 | all-reduce | flops 1792 | bytes 14336 | tf_op jit(solution)/shard_map/psum | solution.py:494
  342.5 7.9 %all-reduce.4.cloned.1.call-done = (bf16[512,3,256]{0,2,1:T(8,128)(2,1)}, bf16[256,512]{1,0:T(8,128)(2,1)}, bf16[512,1024]{1,0:T(8,128)(2,1)}, bf16[1024,512]{1,0:T(8,128)(2,1)}) async-done(((bf16[512,3,256]{0,2,1:T(8,128)(2,1)}, bf16[256,512]{1,0:T(8,128)(2,1)}, bf16[512,1024]{1,0:T(8,128)(2,1)}, bf16[1024,512]{1,0:T(8,128)(2,1)}), (bf16[512,3,256]{0,2,1:T(8,128)(2,1)}, bf16[256,512]{1,0:T(8,128)(2,1)}, ...) | async-done | bytes 3145744 | tf_op jit(solution)/shard_map/psum | solution.py:494
  350.4 2.9 convert_element_type.14
  353.3 2.8 convert_element_type.15
  356.1 1.4 copy.47
  (71 shorter events, 16.8 us)
Async XLA Ops:
  7.2 343.2 %all-reduce.4.cloned.1.call-start = ((), (), s32[]{:S(2)}) async-start(), calls=%async_computation | async-start | bytes 6291456 | tf_op jit(solution)/shard_map/psum | solution.py:494
  7.2 13.9 %collective-permute-start.1 = (f32[2,256]{1,0:T(2,128)}, f32[2,256]{1,0:T(2,128)S(1)}, u32[]{:S(2)}, u32[]{:S(2)}) collective-permute-start(f32[2,256]{1,0:T(2,128)} %param.25), channel_id=1, source_target_pairs={{0,1},{1,0},{2,3},{3,2},{4,5},{5,4},{6,7},{7,6},{8,9},{9,8},{10,11... | collective-permute-start | bytes 6152 | tf_op jit(solution)/shard_map/ppermute | solution.py:441
  11.7 40.4 %collective-permute-start = (bf16[512,3,256]{0,2,1:T(8,128)(2,1)S(1)}, bf16[512,3,256]{0,2,1:T(8,128)(2,1)S(1)}, u32[]{:S(2)}, u32[]{:S(2)}) collective-permute-start(bf16[512,3,256]{0,2,1:T(8,128)(2,1)S(1)} %copy.39), channel_id=1, source_target_pairs={{0,1},{1,0},{2,3},{3,2},{4,5},{5,4},{6,7},{7,6},{8,9},{9,8},{10,11... | collective-permute-start | bytes 2359304 | tf_op jit(solution)/shard_map/ppermute | solution.py:441
  11.8 69.6 %collective-permute-start.3 = (bf16[512,1024]{1,0:T(8,128)(2,1)}, bf16[512,1024]{1,0:T(8,128)(2,1)S(1)}, u32[]{:S(2)}, u32[]{:S(2)}) collective-permute-start(bf16[512,1024]{1,0:T(8,128)(2,1)} %refs_8_.1), channel_id=1, source_target_pairs={{0,1},{1,0},{2,3},{3,2},{4,5},{5,4},{6,7},{7,6},{8,9},{9,8},{10,11... | collective-permute-start | bytes 3145736 | tf_op jit(solution)/shard_map/ppermute | solution.py:441
  13.8 67.7 %collective-permute-start.4 = (bf16[1024,512]{1,0:T(8,128)(2,1)}, bf16[1024,512]{1,0:T(8,128)(2,1)}, u32[]{:S(2)}, u32[]{:S(2)}) collective-permute-start(bf16[1024,512]{1,0:T(8,128)(2,1)} %refs_10_.1), channel_id=1, source_target_pairs={{0,1},{1,0},{2,3},{3,2},{4,5},{5,4},{6,7},{7,6},{8,9},{9,8},{10,11... | collective-permute-start | bytes 3145736 | tf_op jit(solution)/shard_map/ppermute | solution.py:441
  13.8 67.5 %collective-permute-start.2 = (bf16[256,512]{1,0:T(8,128)(2,1)}, bf16[256,512]{1,0:T(8,128)(2,1)S(1)}, u32[]{:S(2)}, u32[]{:S(2)}) collective-permute-start(bf16[256,512]{1,0:T(8,128)(2,1)} %refs_6_.1), channel_id=1, source_target_pairs={{0,1},{1,0},{2,3},{3,2},{4,5},{5,4},{6,7},{7,6},{8,9},{9,8},{10,11... | collective-permute-start | bytes 786440 | tf_op jit(solution)/shard_map/ppermute | solution.py:441
  21.1 60.3 %collective-permute-start.5 = (f32[1024]{0:T(1024)}, f32[1024]{0:T(1024)S(1)}, u32[]{:S(2)}, u32[]{:S(2)}) collective-permute-start(f32[1024]{0:T(1024)} %param.31), channel_id=1, source_target_pairs={{0,1},{1,0},{2,3},{3,2},{4,5},{5,4},{6,7},{7,6},{8,9},{9,8},{10,11... | collective-permute-start | bytes 12296 | tf_op jit(solution)/shard_map/ppermute | solution.py:441
  81.4 1.0 copy-start.9
  168.7 71.9 %collective-permute-start.11 = (bf16[1024,512]{1,0:T(8,128)(2,1)}, bf16[1024,512]{1,0:T(8,128)(2,1)}, u32[]{:S(2)}, u32[]{:S(2)}) collective-permute-start(bf16[1024,512]{1,0:T(8,128)(2,1)} %get-tuple-element.69), channel_id=1, source_target_pairs={{0,1},{1,0},{2,3},{3,2},{4,5},{5,4},{6,7},{7,6},{8,9},{9,8},{10,11... | collective-permute-start | bytes 3145736 | tf_op jit(solution)/shard_map/ppermute | solution.py:447
  169.3 73.8 %collective-permute-start.9 = (bf16[512,1024]{1,0:T(8,128)(2,1)}, bf16[512,1024]{1,0:T(8,128)(2,1)}, u32[]{:S(2)}, u32[]{:S(2)}) collective-permute-start(bf16[512,1024]{1,0:T(8,128)(2,1)} %get-tuple-element.65), channel_id=1, source_target_pairs={{0,1},{1,0},{2,3},{3,2},{4,5},{5,4},{6,7},{7,6},{8,9},{9,8},{10,11... | collective-permute-start | bytes 3145736 | tf_op jit(solution)/shard_map/ppermute | solution.py:447
  199.1 39.3 %collective-permute-start.6 = (bf16[512,3,256]{0,2,1:T(8,128)(2,1)}, bf16[512,3,256]{0,2,1:T(8,128)(2,1)}, u32[]{:S(2)}, u32[]{:S(2)}) collective-permute-start(bf16[512,3,256]{0,2,1:T(8,128)(2,1)} %bitcast.13), channel_id=1, source_target_pairs={{0,1},{1,0},{2,3},{3,2},{4,5},{5,4},{6,7},{7,6},{8,9},{9,8},{10,11... | collective-permute-start | bytes 2359304 | tf_op jit(solution)/shard_map/ppermute | solution.py:447
  199.7 37.9 %collective-permute-start.8 = (bf16[256,512]{1,0:T(8,128)(2,1)}, bf16[256,512]{1,0:T(8,128)(2,1)S(1)}, u32[]{:S(2)}, u32[]{:S(2)}) collective-permute-start(bf16[256,512]{1,0:T(8,128)(2,1)} %get-tuple-element.63), channel_id=1, source_target_pairs={{0,1},{1,0},{2,3},{3,2},{4,5},{5,4},{6,7},{7,6},{8,9},{9,8},{10,11... | collective-permute-start | bytes 786440 | tf_op jit(solution)/shard_map/ppermute | solution.py:447
  201.1 36.5 %copy-start.4 = (bf16[256,512]{1,0:T(8,128)(2,1)S(1)}, bf16[256,512]{1,0:T(8,128)(2,1)}, u32[]{:S(2)}) copy-start(bf16[256,512]{1,0:T(8,128)(2,1)} %get-tuple-element.62) | copy-start | bytes 786436
  227.2 13.4 %copy-start.1 = (bf16[1024,512]{1,0:T(8,128)(2,1)S(1)}, bf16[1024,512]{1,0:T(8,128)(2,1)}, u32[]{:S(2)}) copy-start(bf16[1024,512]{1,0:T(8,128)(2,1)} %get-tuple-element.68) | copy-start | bytes 3145732
  227.2 15.9 %copy-start = (bf16[512,1024]{1,0:T(8,128)(2,1)S(1)}, bf16[512,1024]{1,0:T(8,128)(2,1)}, u32[]{:S(2)}) copy-start(bf16[512,1024]{1,0:T(8,128)(2,1)} %get-tuple-element.64) | copy-start | bytes 3145732
  240.6 5.1 %copy-start.11 = (f32[1,1024]{1,0:T(1,128)S(1)}, f32[1,1024]{1,0:T(1,128)}, u32[]{:S(2)}) copy-start(f32[1,1024]{1,0:T(1,128)} %get-tuple-element.67) | copy-start | bytes 12292
  240.6 5.8 %copy-start.8 = (f32[1,768]{1,0:T(1,128)S(1)}, f32[1,768]{1,0:T(1,128)}, u32[]{:S(2)}) copy-start(f32[1,768]{1,0:T(1,128)} %get-tuple-element.61) | copy-start | bytes 9220
  245.7 62.5 %collective-permute-start.10 = (f32[1024]{0:T(1024)S(1)}, f32[1024]{0:T(1024)S(1)}, u32[]{:S(2)}, u32[]{:S(2)}) collective-permute-start(f32[1024]{0:T(1024)S(1)} %bitcast.33), channel_id=1, source_target_pairs={{0,1},{1,0},{2,3},{3,2},{4,5},{5,4},{6,7},{7,6},{8,9},{9,8},{10,11... | collective-permute-start | bytes 12296 | tf_op jit(solution)/shard_map/ppermute | solution.py:447
  246.4 61.8 %collective-permute-start.7 = (f32[3,256]{1,0:T(4,128)S(1)}, f32[3,256]{1,0:T(4,128)S(1)}, u32[]{:S(2)}, u32[]{:S(2)}) collective-permute-start(f32[3,256]{1,0:T(4,128)S(1)} %squeeze_reshape.7), channel_id=1, source_target_pairs={{0,1},{1,0},{2,3},{3,2},{4,5},{5,4},{6,7},{7,6},{8,9},{9,8},{10,11... | collective-permute-start | bytes 9224 | tf_op jit(solution)/shard_map/ppermute | solution.py:447
  247.9 19.7 %copy-start.6 = (f32[8,512]{1,0:T(8,128)S(1)}, f32[8,512]{1,0:T(8,128)}, u32[]{:S(2)}) copy-start(f32[8,512]{1,0:T(8,128)} %get-tuple-element.57) | copy-start | bytes 49156
  247.9 60.3 %copy-start.7 = (f32[1,768]{1,0:T(1,128)S(1)}, f32[1,768]{1,0:T(1,128)}, u32[]{:S(2)}) copy-start(f32[1,768]{1,0:T(1,128)} %get-tuple-element.60) | copy-start | bytes 9220
  247.9 60.4 %copy-start.5 = (f32[1,1024]{1,0:T(1,128)S(1)}, f32[1,1024]{1,0:T(1,128)}, u32[]{:S(2)}) copy-start(f32[1,1024]{1,0:T(1,128)} %get-tuple-element.66) | copy-start | bytes 12292
  350.4 5.7 %copy-start.2 = (bf16[512,3,256]{0,2,1:T(8,128)(2,1)S(1)}, bf16[512,3,256]{0,2,1:T(8,128)(2,1)}, u32[]{:S(2)}) copy-start(bf16[512,3,256]{0,2,1:T(8,128)(2,1)} %get-tuple-element.86) | copy-start | bytes 2359300
  350.4 7.1 %copy-start.3 = (bf16[256,512]{1,0:T(8,128)(2,1)S(1)}, bf16[256,512]{1,0:T(8,128)(2,1)}, u32[]{:S(2)}) copy-start(bf16[256,512]{1,0:T(8,128)(2,1)} %get-tuple-element.87) | copy-start | bytes 786436
  (2 other events, 1.3 us)
Sparse Core Ops, SparseCore 0:
  245.8 104.5 all-reduce.3

commit v2 on v1

v2 whole, which is shorter than its diff:
```python
import jax
import jax.numpy as jnp
from jax import lax
from jax.experimental import pallas as pl
from jax.experimental.pallas import tpu as pltpu
from jax.sharding import PartitionSpec as P

HEAD_DIM = 64
SEQ_LEN = 1024
LEFT = 10
RIGHT = 2
QB = 64
MARGIN = 16
WIN = QB + 2 * MARGIN
NBLK = SEQ_LEN // QB
EPS = 1e-05
LN_ROWS = 256
NEG = -1000000000.0
VMEM = 60 * 1024 * 1024
F32 = jnp.float32
BF16 = jnp.bfloat16


def dot_nn(a, b):
    return jnp.dot(a, b, preferred_element_type=F32)


def dot_nt(a, b):
    return lax.dot_general(a, b, (((1,), (1,)), ((), ())), preferred_element_type=F32)


def dot_tn(a, b):
    return lax.dot_general(a, b, (((0,), (0,)), ((), ())), preferred_element_type=F32)


def length_of(scal, seq):
    return scal[1 + seq]


def keep_of(shape, first_pos, seq, scal):
    seqs = (scal.shape[0] - 1) // 5
    ends = [scal[1 + k * seqs + seq] for k in range(1, 5)]
    pos = first_pos + lax.broadcasted_iota(jnp.int32, (shape[0], 1), 0)
    col = lax.broadcasted_iota(jnp.int32, (1, shape[1]), 1)
    rows = jnp.where((pos >= ends[0]) & (pos < ends[1]), 0.0, 1.0)
    cols = jnp.where((col >= ends[2]) & (col < ends[3]), 0.0, 1.0)
    return rows * cols


def normalize(v):
    off = v - jnp.mean(v, axis=-1, keepdims=True)
    r = lax.rsqrt(jnp.mean(off * off, axis=-1, keepdims=True) + EPS)
    return off * r, r


def head_mask(scale, heads):
    row = lax.broadcasted_iota(jnp.int32, (heads * QB, heads * HEAD_DIM), 0)
    col = lax.broadcasted_iota(jnp.int32, (heads * QB, heads * HEAD_DIM), 1)
    return jnp.where(row // QB == col // HEAD_DIM, scale, 0.0).astype(BF16)


def spread(block, mask, heads):
    return jnp.concatenate([block] * heads, axis=0) * mask


def pair_rows(probs, window, heads):
    out = []
    low = lax.broadcasted_iota(jnp.int32, (QB, 2 * HEAD_DIM), 1) < HEAD_DIM
    for p in range(heads // 2):
        both = dot_tn(
            probs[:, p * 2 * QB : (p + 1) * 2 * QB],
            window[:, p * 2 * HEAD_DIM : (p + 1) * 2 * HEAD_DIM],
        )
        out.append(jnp.where(low, both[:QB], both[QB:]))
    return jnp.concatenate(out, axis=1)


def attend(length, proj, kpad, vpad, scores, ctx, probs_out, heads):
    width = heads * HEAD_DIM
    edge = jnp.zeros((MARGIN, width), BF16)
    for pad, j in ((kpad, 1), (vpad, 2)):
        pad[0:MARGIN, :] = edge
        pad[MARGIN + SEQ_LEN :, :] = edge
        pad[MARGIN : MARGIN + SEQ_LEN, :] = proj[:, j * width : (j + 1) * width]
    mask = head_mask(HEAD_DIM**-0.5, heads)
    key = lax.broadcasted_iota(jnp.int32, (WIN, heads * QB), 0)
    query = lax.broadcasted_iota(jnp.int32, (WIN, heads * QB), 1) % QB
    rel = key - MARGIN - query
    band = jnp.where((rel >= -LEFT) & (rel <= RIGHT), 0.0, NEG)
    diagonal = jnp.where(rel == 0, 0.0, NEG)

    for b in range(NBLK):
        q_all = spread(proj[b * QB : (b + 1) * QB, 0:width], mask, heads)
        scores[b * WIN : (b + 1) * WIN, :] = dot_nt(kpad[b * QB : b * QB + WIN, :], q_all)
    for b in range(NBLK):
        at = slice(b * WIN, (b + 1) * WIN)
        pos = key + (b * QB - MARGIN)
        live = (pos < length) if b else (pos >= 0) & (pos < length)
        masked = scores[at, :] + jnp.where(live, band, diagonal)
        weights = jnp.exp(masked - jnp.max(masked, axis=0, keepdims=True))
        probs_out[at, :] = (weights / jnp.sum(weights, axis=0, keepdims=True)).astype(BF16)
    for b in range(NBLK):
        v_win = vpad[b * QB : b * QB + WIN, :]
        ctx[b * QB : (b + 1) * QB, :] = pair_rows(probs_out[b * WIN : (b + 1) * WIN, :], v_win, heads).astype(BF16)


def first_kernel(heads, scal, x, w, bias, gain, shift, n1, proj, ctx, probs, *scratch):
    s = pl.program_id(0)
    for first in range(0, SEQ_LEN, LN_ROWS):
        at = slice(first, first + LN_ROWS)
        for r in range(first, first + LN_ROWS, SUB):
            sub = slice(r, r + SUB)
            keep = keep_of((SUB, x.shape[1]), r, s, scal)
            n1[sub, :] = (normalize(x[sub, :].astype(F32) * keep)[0] * gain[...] + shift[...]).astype(BF16)
        proj[at, :] = (dot_nn(n1[at, :], w[...]) + bias[...]).astype(BF16)
    attend(length_of(scal, s), proj, *scratch, ctx, probs, heads)


def second_kernel(heads, scal, n1, w, bias, proj, ctx, probs, *scratch):
    s = pl.program_id(0)
    for first in range(0, SEQ_LEN, LN_ROWS):
        at = slice(first, first + LN_ROWS)
        proj[at, :] = (dot_nn(n1[at, :], w[...]) + bias[...]).astype(BF16)
    attend(length_of(scal, s), proj, *scratch, ctx, probs, heads)


def const_spec(shape):
    return pl.BlockSpec(shape, lambda *_: (0,) * len(shape), pipeline_mode=pl.Buffered(1))


def rows_spec(rows, cols):
    return pl.BlockSpec((rows, cols), lambda i, *_: (i, 0))


def params():
    return pltpu.CompilerParams(vmem_limit_bytes=VMEM, dimension_semantics=("arbitrary",))


def attention_forward(first, scal, rows, w, bias, gain, shift):
    total, width_in = rows.shape
    seqs = total // SEQ_LEN
    width = w.shape[1] // 3
    heads = width // HEAD_DIM
    outs = [
        jax.ShapeDtypeStruct((total, 3 * width), BF16),
        jax.ShapeDtypeStruct((total, width), BF16),
        jax.ShapeDtypeStruct((seqs * NBLK * WIN, heads * QB), BF16),
    ]
    out_specs = [
        rows_spec(SEQ_LEN, 3 * width),
        rows_spec(SEQ_LEN, width),
        rows_spec(NBLK * WIN, heads * QB),
    ]
    scratch = [pltpu.VMEM((SEQ_LEN + 2 * MARGIN, width), BF16)] * 2
    scratch += [pltpu.VMEM((NBLK * WIN, heads * QB), F32)]
    flops = 2 * total * width_in * 3 * width + 8 * total * WIN * width
    cost = pl.CostEstimate(flops=flops, bytes_accessed=total * (width_in + 6 * width) * 2, transcendentals=0)
    in_specs = [rows_spec(SEQ_LEN, width_in), const_spec(w.shape), const_spec(bias.shape)]
    if first:
        in_specs += [const_spec(gain.shape), const_spec(shift.shape)]
        outs = [jax.ShapeDtypeStruct(rows.shape, BF16)] + outs
        out_specs = [rows_spec(SEQ_LEN, width_in)] + out_specs
        args = (rows, w, bias, gain, shift)
    else:
        args = (rows, w, bias)

    def body(*refs):
        (first_kernel if first else second_kernel)(heads, *refs)

    return pl.pallas_call(
        body,
        grid_spec=pltpu.PrefetchScalarGridSpec(
            num_scalar_prefetch=1,
            grid=(seqs,),
            in_specs=in_specs,
            out_specs=out_specs,
            scratch_shapes=scratch,
        ),
        out_shape=outs,
        compiler_params=params(),
        cost_estimate=cost,
        name="attend_first" if first else "attend_second",
    )(scal, *args)


TM = 512
FC = 512
SUB = 32
GELU_A = 0.7978845608028654
GELU_B = 0.7978845608028654 * 0.044715


def subs(rows):
    return [slice(r, r + SUB) for r in range(0, rows, SUB)]


def fold_rows(v):
    return jnp.sum(v.reshape(-1, 8, v.shape[-1]), axis=0)


def clear(i, *refs):
    @pl.when(i == 0)
    def _():
        for ref in refs:
            ref[...] = jnp.zeros_like(ref)


EXTRA = 128
BLOCKS = 16


def put_blocks(me, packs, acc, columns):
    rows = acc.shape[0] // BLOCKS
    each = BLOCKS // len(packs)
    for j in range(BLOCKS):
        first = pl.multiple_of((j ^ me) * rows, rows)
        packs[j // each][j % each] = acc[pl.ds(first, rows), columns].astype(BF16)


def put_vectors(acc, first, vectors):
    spare = EXTRA - len(vectors)
    acc[:, first:] = jnp.concatenate(vectors + [jnp.zeros((spare, acc.shape[0]), F32)], axis=0).T


def up_kernel(
    per_seq, scal,
    x, cot, ctx_a, ctx_b, wo_a, wo_b, wu_a, wu_b, bo, gain, shift, bu_a, bu_b,
    mid_out, n2_out, hidden_out, slope_out, pack_own, pack_other, small,
    acc_d, acc_small, branch_a, branch_b, n2_half, pre_even, pre_odd,
):
    i = pl.program_id(0)
    clear(i, acc_d, acc_small)
    rows = x.shape[0]
    branch_a[...] = dot_nn(ctx_a[...], wo_a[...])
    branch_b[...] = dot_nn(ctx_b[...], wo_b[...])
    g = cot[...]
    g_t = g.T
    bias_sum = jnp.zeros(acc_small.shape, F32)
    for sub in subs(rows):
        keep = keep_of((SUB, x.shape[1]), (i % per_seq) * rows + sub.start, i // per_seq, scal)
        mid = x[sub, :].astype(F32) * keep + branch_a[sub, :] + branch_b[sub, :] + bo[...]
        mid_out[sub, :] = mid
        n2 = (normalize(mid)[0] * gain[...] + shift[...]).astype(BF16)
        n2_out[sub, :] = n2
        n2_half[sub, :] = n2 * 0.5
        bias_sum += fold_rows(cot[sub, :].astype(F32))
    acc_small[...] += bias_sum
    half = wu_a.shape[1]
    chunks = [(part, c) for part in range(2) for c in range(half // FC)]
    pres = (pre_even, pre_odd)

    def up(n):
        part, c = chunks[n]
        pres[n % 2][...] = dot_nn(n2_half[...], (wu_a, wu_b)[part][:, c * FC : (c + 1) * FC])

    up(0)
    for n, (part, c) in enumerate(chunks):
        if n + 1 < len(chunks):
            up(n + 1)
        bias = (bu_a, bu_b)[part][:, c * FC : (c + 1) * FC] * 0.5
        ts = slice(part * half + c * FC, part * half + (c + 1) * FC)
        for sub in subs(rows):
            v = pres[n % 2][sub, :] + bias
            v2 = v * v
            t = jnp.tanh(v * (2 * GELU_A + (8 * GELU_B) * v2))
            hidden_out[sub, ts] = (v + v * t).astype(BF16)
            w = v * (GELU_A + (12 * GELU_B) * v2)
            slope_out[sub, ts] = ((0.5 + 0.5 * t) + w * (1.0 - t * t)).astype(BF16)
        acc_d[:, ts] += dot_nn(g_t, hidden_out[:, ts])

    @pl.when(i == pl.num_programs(0) - 1)
    def _():
        put_blocks(scal[0], [pack_own], acc_d, slice(0, half))
        put_blocks(scal[0], [pack_other], acc_d, slice(half, 2 * half))
        small[...] = acc_small[...]


def call(kernel, name, grid, scalars, in_specs, outs, out_specs, scratch, flops, nbytes, args, alias=()):
    return pl.pallas_call(
        kernel,
        grid_spec=pltpu.PrefetchScalarGridSpec(
            num_scalar_prefetch=len(scalars), grid=(grid,), in_specs=in_specs, out_specs=out_specs,
            scratch_shapes=scratch,
        ),
        out_shape=[jax.ShapeDtypeStruct(s, t) for s, t in outs],
        compiler_params=params(),
        input_output_aliases=dict(alias),
        cost_estimate=pl.CostEstimate(flops=flops, bytes_accessed=nbytes, transcendentals=0),
        name=name,
    )(*scalars, *args)


def up_block(scal, x, cot, ctx_a, ctx_b, wo, wu, bo, gain, shift, bu):
    total, d = x.shape
    width = ctx_a.shape[1]
    half = wu[0].shape[1]
    args = (x, cot, ctx_a, ctx_b, *wo, *wu, bo, gain, shift, *bu)
    in_specs = [rows_spec(TM, d), rows_spec(TM, d), rows_spec(TM, width), rows_spec(TM, width)]
    in_specs += [const_spec(a.shape) for a in args[4:]]
    pack = (BLOCKS, d // BLOCKS, half)
    outs = [
        ((total, d), F32), ((total, d), BF16), ((total, 2 * half), BF16), ((total, 2 * half), BF16),
        (pack, BF16), (pack, BF16), ((8, d), F32),
    ]
    out_specs = [rows_spec(TM, d), rows_spec(TM, d), rows_spec(TM, 2 * half), rows_spec(TM, 2 * half)]
    out_specs += [const_spec(pack), const_spec(pack), const_spec((8, d))]
    scratch = [pltpu.VMEM((d, 2 * half), F32), pltpu.VMEM((8, d), F32)]
    scratch += [pltpu.VMEM((TM, d), F32)] * 2 + [pltpu.VMEM((TM, d), BF16)] + [pltpu.VMEM((TM, FC), F32)] * 2

    def body(*refs):
        up_kernel(SEQ_LEN // TM, *refs)

    return call(
        body, "feed_up", total // TM, (scal,), in_specs, outs, out_specs, scratch,
        2 * total * d * (4 * half + 2 * width), total * (18 * d + 8 * half), args,
    )


def down_kernel(
    scal,
    cot, mid, n2_in, slope, ctx_a, ctx_b, wo_a, wo_b, wu_a, wu_b, wd_a, wd_b, gain, small_up,
    gmid_out, gctx_a, gctx_b, keep_own, keep_other, send_own, send_other,
    acc_own, acc_other, acc_bu, acc_small, gh_even, gh_odd, gpre, back_a, back_b, gmid_low,
):
    i = pl.program_id(0)
    clear(i, acc_own, acc_other, acc_bu, acc_small)
    rows = cot.shape[0]
    n2_t = n2_in[...].T
    half = wu_a.shape[1]
    chunks = [(part, c) for part in range(2) for c in range(half // FC)]
    ghs = (gh_even, gh_odd)

    def up(n):
        part, c = chunks[n]
        ghs[n % 2][...] = dot_nt(cot[...], (wd_a, wd_b)[part][c * FC : (c + 1) * FC, :])

    up(0)
    for n, (part, c) in enumerate(chunks):
        if n + 1 < len(chunks):
            up(n + 1)
        ts = slice(part * half + c * FC, part * half + (c + 1) * FC)
        bias_sum = jnp.zeros((8, FC), F32)
        for sub in subs(rows):
            value = slope[sub, ts].astype(F32) * ghs[n % 2][sub, :]
            gpre[sub, ts] = value.astype(BF16)
            bias_sum += fold_rows(value)
        acc_bu[:, ts] += bias_sum
        (acc_own, acc_other)[part][:, c * FC : (c + 1) * FC] += dot_nn(n2_t, gpre[:, ts])
    back_a[...] = dot_nt(gpre[:, :half], wu_a[...])
    back_b[...] = dot_nt(gpre[:, half:], wu_b[...])
    sums = [jnp.zeros((8, cot.shape[1]), F32) for _ in range(3)]
    for sub in subs(rows):
        gn2 = back_a[sub, :] + back_b[sub, :]
        nn, r = normalize(mid[sub, :])
        gnn = gn2 * nn
        u = gn2 * gain[...]
        mean_un = jnp.mean(gnn * gain[...], axis=-1, keepdims=True)
        gm = cot[sub, :].astype(F32) + r * (u - jnp.mean(u, axis=-1, keepdims=True) - nn * mean_un)
        gmid_out[sub, :] = gm
        gmid_low[sub, :] = gm.astype(BF16)
        for k, term in enumerate((gnn, gn2, gm)):
            sums[k] += fold_rows(term)
    for k in range(3):
        acc_small[8 * k : 8 * k + 8, :] += sums[k]
    gctx_a[...] = dot_nt(gmid_low[...], wo_a[...]).astype(BF16)
    gctx_b[...] = dot_nt(gmid_low[...], wo_b[...]).astype(BF16)
    width = ctx_a.shape[1]
    side = gmid_low.shape[1] // 2
    for acc, ctx in ((acc_own, ctx_a), (acc_other, ctx_b)):
        both = dot_tn(ctx[...], gmid_low[...])
        acc[:width, half : half + side] += both[:, :side]
        acc[width:, half : half + side] += both[:, side:]

    @pl.when(i == pl.num_programs(0) - 1)
    def _():
        vectors = [jnp.sum(acc_small[8 * k : 8 * k + 8, :], axis=0, keepdims=True) for k in range(3)]
        vectors += [jnp.sum(small_up[...], axis=0, keepdims=True)]
        biases = jnp.sum(acc_bu[...], axis=0, keepdims=True)
        d = cot.shape[1]
        for part, (acc, keep, send) in enumerate(((acc_own, keep_own, send_own), (acc_other, keep_other, send_other))):
            mine = biases[:, part * half : (part + 1) * half]
            put_vectors(acc, half + side, vectors + [mine[:, :d], mine[:, d:]])
            put_blocks(scal[0], [keep, send], acc, slice(None))


def down_block(scal, cot, mid, n2, slope, ctx_a, ctx_b, wo, wu, wd, gain, small_up):
    total, d = cot.shape
    width = ctx_a.shape[1]
    half = wu[0].shape[1]
    args = (cot, mid, n2, slope, ctx_a, ctx_b, *wo, *wu, *wd, gain, small_up)
    in_specs = [rows_spec(TM, d), rows_spec(TM, d), rows_spec(TM, d), rows_spec(TM, 2 * half)]
    in_specs += [rows_spec(TM, width), rows_spec(TM, width)]
    in_specs += [const_spec(a.shape) for a in args[6:]]
    columns = half + d // 2 + EXTRA
    pack = (BLOCKS // 2, d // BLOCKS, columns)
    outs = [
        ((total, d), F32), ((total, width), BF16), ((total, width), BF16),
        *[(pack, BF16)] * 4,
    ]
    out_specs = [rows_spec(TM, d), rows_spec(TM, width), rows_spec(TM, width)]
    out_specs += [const_spec(s) for s, _ in outs[3:]]
    scratch = [
        pltpu.VMEM((d, columns), F32), pltpu.VMEM((d, columns), F32), pltpu.VMEM((8, 2 * half), F32),
        pltpu.VMEM((24, d), F32), pltpu.VMEM((TM, FC), F32), pltpu.VMEM((TM, FC), F32),
        pltpu.VMEM((TM, 2 * half), BF16), pltpu.VMEM((TM, d), F32), pltpu.VMEM((TM, d), F32), pltpu.VMEM((TM, d), BF16),
    ]
    return call(
        down_kernel, "feed_back", total // TM, (scal,), in_specs, outs, out_specs, scratch,
        2 * total * d * (6 * half + 4 * width), total * (16 * d + 4 * half), args,
    )


def out_kernel(mid, hidden, wd_a, wd_b, bd, *refs):
    half = wd_a.shape[0]
    refs[-1][...] = (
        mid[...] + dot_nn(hidden[:, :half], wd_a[...]) + dot_nn(hidden[:, half:], wd_b[...]) + bd[...]
    ).astype(BF16)


def part_spec(tiles, part, cols):
    return pl.BlockSpec((TM, cols), lambda i, *_: (i + part * tiles, 0))


def out_block(part, parts, mid, hidden, wd, bd, before):
    total, d = mid.shape
    tiles = total // TM // parts
    args = (mid, hidden, *wd, bd)
    specs = [part_spec(tiles, part, d), part_spec(tiles, part, hidden.shape[1])]
    specs += [const_spec(a.shape) for a in (*wd, bd)]
    alias = {}
    if before is not None:
        alias = {len(args): 0}
        args += (before,)
        specs += [pl.BlockSpec(memory_space=pl.ANY)]
    return call(
        out_kernel, "layer_out", tiles, (), specs, [((total, d), BF16)], [part_spec(tiles, part, d)], [],
        2 * tiles * TM * d * hidden.shape[1], tiles * TM * (6 * d + 2 * hidden.shape[1]), args, alias,
    )[0]


def attend_back_kernel(
    heads, scal, n1, proj, probs, gctx, gproj, pack_keep, pack_send, kpad, vpad, dk, dv, acc, acc_b, gprob, gscore
):
    s = pl.program_id(0)
    clear(s, acc, acc_b)
    width = heads * HEAD_DIM
    edge = jnp.zeros((MARGIN, width), BF16)
    for pad, j in ((kpad, 1), (vpad, 2)):
        pad[0:MARGIN, :] = edge
        pad[MARGIN + SEQ_LEN :, :] = edge
        pad[MARGIN : MARGIN + SEQ_LEN, :] = proj[:, j * width : (j + 1) * width]
    mask = head_mask(1.0, heads)
    dk[0 : 2 * MARGIN, :] = jnp.zeros((2 * MARGIN, width), F32)
    dv[0 : 2 * MARGIN, :] = jnp.zeros((2 * MARGIN, width), F32)
    scale = HEAD_DIM**-0.5

    def rows(b):
        return slice(b * QB, (b + 1) * QB)

    def keys(b):
        return slice(b * QB, b * QB + WIN)

    def own(b):
        return slice(b * WIN, (b + 1) * WIN)

    for b in range(NBLK):
        gprob[own(b), :] = dot_nt(vpad[keys(b), :], spread(gctx[rows(b), :], mask, heads))
    for b in range(NBLK):
        p = probs[own(b), :].astype(F32)
        gp = gprob[own(b), :]
        gscore[own(b), :] = (p * (gp - jnp.sum(p * gp, axis=0, keepdims=True))).astype(BF16)
    for b in range(NBLK):
        gproj[rows(b), 0:width] = (pair_rows(gscore[own(b), :], kpad[keys(b), :], heads) * scale).astype(BF16)
    for b in range(NBLK):
        key_term = dot_nn(gscore[own(b), :], spread(proj[rows(b), 0:width], mask, heads)) * scale
        value_term = dot_nn(probs[own(b), :], spread(gctx[rows(b), :], mask, heads))
        for total, term in ((dk, key_term), (dv, value_term)):
            total[b * QB : b * QB + 2 * MARGIN, :] += term[: 2 * MARGIN]
            total[b * QB + 2 * MARGIN : b * QB + WIN, :] = term[2 * MARGIN :]
    gproj[:, width : 2 * width] = dk[MARGIN : MARGIN + SEQ_LEN, :].astype(BF16)
    gproj[:, 2 * width :] = dv[MARGIN : MARGIN + SEQ_LEN, :].astype(BF16)
    gp_all = gproj[...]
    acc[:, : 3 * width] += dot_tn(n1[...], gp_all)
    acc_b[...] += jnp.sum(gp_all.astype(F32), axis=0, keepdims=True)

    @pl.when(s == pl.num_programs(0) - 1)
    def _():
        put_vectors(acc, 3 * width, [jnp.concatenate([acc_b[:, :width], acc_b[:, 2 * width :]], axis=1)])
        put_blocks(scal[0], [pack_keep, pack_send], acc, slice(None))


def attention_backward(scal, n1, proj, probs, gctx):
    total, d = n1.shape
    seqs = total // SEQ_LEN
    width = gctx.shape[1]
    heads = width // HEAD_DIM

    def body(*refs):
        attend_back_kernel(heads, *refs)

    pad = SEQ_LEN + 2 * MARGIN
    columns = 3 * width + EXTRA
    pack = (BLOCKS // 2, d // BLOCKS, columns)
    return call(
        body, "attend_back", seqs, (scal,),
        [
            rows_spec(SEQ_LEN, d), rows_spec(SEQ_LEN, 3 * width),
            rows_spec(NBLK * WIN, heads * QB), rows_spec(SEQ_LEN, width),
        ],
        [((total, 3 * width), BF16), (pack, BF16), (pack, BF16)],
        [rows_spec(SEQ_LEN, 3 * width), const_spec(pack), const_spec(pack)],
        [
            pltpu.VMEM((pad, width), BF16), pltpu.VMEM((pad, width), BF16),
            pltpu.VMEM((pad, width), F32), pltpu.VMEM((pad, width), F32),
            pltpu.VMEM((d, columns), F32), pltpu.VMEM((1, 3 * width), F32),
            pltpu.VMEM((NBLK * WIN, heads * QB), F32), pltpu.VMEM((NBLK * WIN, heads * QB), BF16),
        ],
        2 * total * d * 3 * width + 16 * total * WIN * width, total * (d + 9 * width) * 2,
        (n1, proj, probs, gctx),
    )


def last_kernel(per_seq, first, scal, x, gmid, gp_a, gp_b, w_a, w_b, gain, *refs):
    gin, small, acc, back_a, back_b = refs[-5:]
    i = pl.program_id(0)
    clear(i, acc)
    rows = x.shape[0]
    tile = i + first
    back_a[...] = dot_nt(gp_a[...], w_a[...])
    back_b[...] = dot_nt(gp_b[...], w_b[...])
    sums = [jnp.zeros((8, x.shape[1]), F32) for _ in range(2)]
    for sub in subs(rows):
        keep = keep_of((SUB, x.shape[1]), (tile % per_seq) * rows + sub.start, tile // per_seq, scal)
        nn, r = normalize(x[sub, :].astype(F32) * keep)
        gn1 = back_a[sub, :] + back_b[sub, :]
        gnn = gn1 * nn
        u = gn1 * gain[...]
        mean_un = jnp.mean(gnn * gain[...], axis=-1, keepdims=True)
        a = r * (u - jnp.mean(u, axis=-1, keepdims=True) - nn * mean_un)
        gin[sub, :] = (gmid[sub, :] + a) * keep
        sums[0] += fold_rows(gnn)
        sums[1] += fold_rows(gn1)
    acc[0:8, :] += sums[0]
    acc[8:16, :] += sums[1]

    @pl.when(i == pl.num_programs(0) - 1)
    def _():
        small[...] = acc[...]


def last_block(part, parts, scal, x, gmid, gp_a, gp_b, w_a, w_b, gain, before):
    total, d = x.shape
    tiles = total // TM // parts

    def body(*refs):
        last_kernel(SEQ_LEN // TM, part * tiles, *refs)

    width = gp_a.shape[1]
    args = (x, gmid, gp_a, gp_b, w_a, w_b, gain)
    specs = [part_spec(tiles, part, c) for c in (d, d, width, width)]
    specs += [const_spec(a.shape) for a in args[4:]]
    alias = {}
    if before is not None:
        alias = {len(args) + 1: 0}
        args += (before,)
        specs += [pl.BlockSpec(memory_space=pl.ANY)]
    return call(
        body, "input_gradient", tiles, (scal,), specs,
        [((total, d), F32), ((16, d), F32)], [part_spec(tiles, part, d), const_spec((16, d))],
        [pltpu.VMEM((16, d), F32), pltpu.VMEM((TM, d), F32), pltpu.VMEM((TM, d), F32)],
        4 * tiles * TM * d * width, tiles * TM * (10 * d + 4 * width), args, alias,
    )


def place(me, pieces, out, kind):
    each = pieces[0].shape[0]
    rows = pieces[0].shape[1]
    for j in range(BLOCKS):
        at = pl.ds(pl.multiple_of((j ^ me) * rows, rows), rows)
        out[at, :] = pieces[j // each][j % each].astype(kind)


def unpack_turned(scal, p0, p1, out, natural):
    place(scal[0], (p0, p1), natural, BF16)
    out[...] = natural[...].T.astype(F32)


def unpack_pair(scal, p0, p1, out, beside, small, natural):
    place(scal[0], (p0, p1), natural, F32)
    half = out.shape[1]
    rows, cols = beside.shape
    side = cols // 2
    out[...] = natural[:, :half]
    beside[:, :side] = natural[:rows, half : half + side]
    beside[:, side:] = natural[rows:, half : half + side]
    small[...] = natural[:, half + side :].T[0:8, :]


def unpack_plain(scal, p0, p1, out, small, natural):
    place(scal[0], (p0, p1), natural, F32)
    width = out.shape[1]
    out[...] = natural[:, :width]
    small[...] = natural[:, width:].T[0:8, :]


def unpack(kernel, name, scal, pieces, shapes, natural):
    size = sum(p.size for p in pieces)
    return call(
        kernel, name, 1, (scal,), [const_spec(p.shape) for p in pieces], [(s, F32) for s in shapes],
        [const_spec(s) for s in shapes], natural, 0, 6 * size, tuple(pieces),
    )


def make_body(mesh):
    tp = mesh.shape["tensor"]
    dp = mesh.shape["dp"]
    paired = tp == 2 and dp == BLOCKS

    def across(v):
        return lax.ppermute(v, "tensor", [(0, 1), (1, 0)])

    def swap(v, distance):
        return lax.ppermute(v, "dp", [(i, i ^ distance) for i in range(dp)])

    def core(v):
        return swap(v, 1)

    def plus(first, *rest):
        total = first.astype(F32)
        for v in rest:
            total = total + v.astype(F32)
        return total.astype(first.dtype)

    def lower(v):
        return v[: v.shape[0] // 2]

    def upper(v):
        return v[v.shape[0] // 2 :]

    def join(a, b):
        return jnp.concatenate([a, b], axis=0)

    def window(kernel, args, moves):
        args, sent = lax.optimization_barrier((args, [v for v, _ in moves]))
        arrived = [move(v) for v, (_, move) in zip(sent, moves)]
        return lax.optimization_barrier((kernel(*args), arrived, sent))

    def body(
        inputs, cotangent, lengths, time_span, freq_span, gain_one, shift_one, qkv_weight, qkv_bias,
        out_weight, out_bias, gain_two, shift_two, up_weight, up_bias, down_weight, down_bias,
    ):
        total, d = inputs.shape
        width = out_weight.shape[0]
        seqs = total // SEQ_LEN
        here = lax.axis_index("tensor") * seqs
        index = lax.axis_index("dp")
        label = jnp.int32(0)
        if paired:
            label = ((index & 1) << 3) | ((index & 2) << 1) | ((index & 4) >> 1)
        table = jnp.concatenate([lengths[:, None], time_span, freq_span], axis=1)
        table = lax.dynamic_slice_in_dim(table, here, seqs, 0)
        scal = jnp.concatenate([label.astype(jnp.int32).reshape(1), table.T.reshape(-1)])
        row = lambda v: v.reshape(1, -1)
        rows_of = lambda v: jnp.sum(v.reshape(-1, 8, d), axis=1)
        three_biases = lambda b: jnp.concatenate([b[0:1], jnp.zeros_like(b[0:1]), b[1:2]], axis=1)

        def attend_a(rows, w, bias):
            return attention_forward(True, scal, rows, w, bias, row(gain_one), row(shift_one))

        def attend_b(rows, w, bias):
            return attention_forward(False, scal, rows, w, bias, None, None)

        def up(ctx_a, ctx_b, wo, wu, bu):
            return up_block(
                scal, inputs, cotangent, ctx_a, ctx_b, wo, wu, row(out_bias), row(gain_two), row(shift_two), bu
            )

        def down(mid, n2, slope, ctx_a, ctx_b, wo, wu, wd, small_up):
            return down_block(scal, cotangent, mid, n2, slope, ctx_a, ctx_b, wo, wu, wd, row(gain_two), small_up)

        def back(n1, proj, probs, gctx):
            return attention_backward(scal, n1, proj, probs, gctx)

        def last(part, parts):
            return lambda gmid, gp_a, gp_b, w_a, w_b, before: last_block(
                part, parts, scal, inputs, gmid, gp_a, gp_b, w_a, w_b, row(gain_one), before
            )

        def out(part, parts):
            return lambda mid, hidden, wd, before: out_block(part, parts, mid, hidden, wd, row(down_bias), before)

        flat = lambda w: w.reshape(d, -1)
        if paired:
            odd = index & 1

            def part_of(v):
                rows = v.shape[0] // 2
                return lax.dynamic_slice_in_dim(v, odd * rows, rows, 0)

            def whole(mine, theirs):
                return jnp.concatenate([jnp.where(odd == 0, mine, theirs), jnp.where(odd == 0, theirs, mine)], axis=0)

            biases = jnp.concatenate([qkv_bias, up_bias.reshape(-1, qkv_bias.shape[1])], axis=0)
            qkv_a = flat(qkv_weight)
            qkv_half = part_of(qkv_a)
            up_half = part_of(jnp.concatenate([out_weight.reshape(-1, up_weight.shape[1]), up_weight], axis=0))
            (n1, proj_a, ctx_a, probs_a), (qkv_half, up_half, biases_b), (qkv_mine, up_mine, _) = window(
                attend_a, (inputs, qkv_a, three_biases(qkv_bias)),
                [(qkv_half, across), (up_half, across), (biases, across)],
            )
            qkv_b = whole(qkv_half, core(qkv_half))
            (proj_b, ctx_b, probs_b), (up_theirs, down_half), (up_half, _) = window(
                attend_b, (n1, qkv_b, three_biases(biases_b[:2])), [(up_half, core), (part_of(down_weight), across)]
            )
            both = whole(up_half, up_theirs)
            split = width * d // up_weight.shape[1]
            wo = (out_weight, both[:split].reshape(out_weight.shape))
            wu = (up_weight, both[split:])
            bu = (row(up_bias), row(biases_b[2:]))
            (mid, n2, hidden, slope, d_own, d_other, small_up), (down_theirs,), (down_half,) = window(
                up, (ctx_a, ctx_b, wo, wu, bu), [(down_half, core)]
            )
            wd = (down_weight, whole(down_half, down_theirs))
            (gmid, gctx_a, gctx_b, u_own, u_other, u_send_own, u_send_other), (d_cross,), _ = window(
                down, (mid, n2, slope, ctx_a, ctx_b, wo, wu, wd, small_up), [(d_other, across)]
            )
            u_other, u_own = plus(u_other, core(u_send_other)), plus(u_own, core(u_send_own))
            d_sum = plus(d_own, d_cross)
            d_sum = plus(lower(d_sum), core(upper(d_sum)))
            (gproj_b, q_other, q_send), (u_cross, d_in), _ = window(
                back, (n1, proj_b, probs_b, gctx_b), [(u_other, across), (upper(d_sum), lambda v: swap(v, 2))]
            )
            u_sum = plus(u_own, u_cross)
            d_sum = plus(lower(d_sum), d_in)
            q_other = plus(q_other, core(q_send))
            (gproj_a, q_own, q_send), (u_in, d_in, q_cross), _ = window(
                back, (n1, proj_a, probs_a, gctx_a),
                [(upper(u_sum), lambda v: swap(v, 2)), (upper(d_sum), lambda v: swap(v, 4)), (q_other, across)],
            )
            u_sum = plus(lower(u_sum), u_in)
            d_sum = plus(lower(d_sum), d_in)
            q_sum = plus(q_own, core(q_send), q_cross)
            (input_grad, small_a), (u_in, d_in, q_in), _ = window(
                last(0, 2), (gmid, gproj_a, gproj_b, qkv_a, qkv_b, None),
                [
                    (upper(u_sum), lambda v: swap(v, 4)), (d_sum, lambda v: swap(v, 8)),
                    (upper(q_sum), lambda v: swap(v, 2)),
                ],
            )
            u_sum = plus(lower(u_sum), u_in)
            d_sum = plus(d_sum, d_in)
            q_sum = plus(lower(q_sum), q_in)
            (input_grad, small_b), (u_in, d_in, q_in), _ = window(
                last(1, 2), (gmid, gproj_a, gproj_b, qkv_a, qkv_b, input_grad),
                [(u_sum, lambda v: swap(v, 8)), (d_sum, lambda v: swap(v, 4)), (upper(q_sum), lambda v: swap(v, 4))],
            )
            u_sum = plus(u_sum, u_in)
            d_sum = join(d_sum, d_in)
            q_sum = plus(lower(q_sum), q_in)
            s_sum = rows_of(small_a + small_b)
            (layer_out,), (u_in, d_in, q_in, s_in), _ = window(
                lambda *a: [out(0, 4)(*a)], (mid, hidden, wd, None),
                [
                    (u_sum, lambda v: swap(v, 4)), (d_sum, lambda v: swap(v, 2)), (q_sum, lambda v: swap(v, 8)),
                    (s_sum, across),
                ],
            )
            u_sum = join(u_sum, u_in)
            d_sum = join(d_sum, d_in)
            q_sum = plus(q_sum, q_in)
            s_sum = plus(s_sum, s_in)
            (layer_out,), (u_in, d_in, q_in, s_in), _ = window(
                lambda *a: [out(1, 4)(*a)], (mid, hidden, wd, layer_out),
                [(u_sum, lambda v: swap(v, 2)), (d_sum, core), (q_sum, lambda v: swap(v, 4)), (s_sum, core)],
            )
            u_sum = join(u_sum, u_in)
            q_sum = join(q_sum, q_in)
            s_sum = plus(s_sum, s_in)
            (layer_out,), (u_in, q_in, s_in), _ = window(
                lambda *a: [out(2, 4)(*a)], (mid, hidden, wd, layer_out),
                [(u_sum, core), (q_sum, lambda v: swap(v, 2)), (s_sum, lambda v: swap(v, 2))],
            )
            q_sum = join(q_sum, q_in)
            s_sum = plus(s_sum, s_in)
            (layer_out,), (q_in, s_in), _ = window(
                lambda *a: [out(3, 4)(*a)], (mid, hidden, wd, layer_out),
                [(q_sum, core), (s_sum, lambda v: swap(v, 4))],
            )
            s_sum = plus(s_sum, s_in)
            s_sum = plus(s_sum, swap(s_sum, 8))
            half = up_weight.shape[1]
            (g_down,) = unpack(
                unpack_turned, "unpack_down", scal, (d_sum, d_in), [down_weight.shape], [pltpu.VMEM((d, half), BF16)]
            )
            g_up, g_out, small_two = unpack(
                unpack_pair, "unpack_up", scal, (u_sum, u_in), [up_weight.shape, out_weight.shape, (8, d)],
                [pltpu.VMEM((d, u_sum.shape[2]), F32)],
            )
            g_qkv, small_q = unpack(
                unpack_plain, "unpack_qkv", scal, (q_sum, q_in), [(d, 3 * width), (8, d)],
                [pltpu.VMEM((d, q_sum.shape[2]), F32)],
            )
            g_qkv = g_qkv.reshape(d, 3, -1)
            g_qb = small_q[0].reshape(2, -1)
            g_bu = small_two[4:6].reshape(-1)
            shared_one, shared_two = s_sum, small_two
        else:
            def halves(local, axis):
                return tuple(jnp.split(lax.all_gather(local, "tensor", axis=axis, tiled=True), 2, axis=axis))

            def sums(own, other, axis):
                whole = jnp.concatenate([own, other], axis=axis)
                part = lax.psum_scatter(whole, "tensor", scatter_dimension=axis, tiled=True)
                return lax.psum(part, "dp").astype(F32)

            natural = lambda *packs: jnp.concatenate(packs, axis=0).reshape(d, -1)
            qkv = [flat(w) for w in halves(qkv_weight, 2)]
            qb = [three_biases(b) for b in halves(qkv_bias, 1)]
            bu = [row(b) for b in halves(up_bias, 0)]
            wo, wu, wd = halves(out_weight, 0), halves(up_weight, 1), halves(down_weight, 0)
            n1, proj_a, ctx_a, probs_a = attend_a(inputs, qkv[0], qb[0])
            proj_b, ctx_b, probs_b = attend_b(n1, qkv[1], qb[1])
            mid, n2, hidden, slope, d_own, d_other, small_up = up(ctx_a, ctx_b, wo, wu, bu)
            gmid, gctx_a, gctx_b, *u_packs = down(mid, n2, slope, ctx_a, ctx_b, wo, wu, wd, small_up)
            gproj_b, *q_other = back(n1, proj_b, probs_b, gctx_b)
            gproj_a, *q_own = back(n1, proj_a, probs_a, gctx_a)
            input_grad, small_one = last(0, 1)(gmid, gproj_a, gproj_b, *qkv, None)
            layer_out = out(0, 1)(mid, hidden, wd, None)
            g_down = sums(natural(d_own), natural(d_other), 1).T
            u = natural(u_packs[0], u_packs[2]), natural(u_packs[1], u_packs[3])
            half, side = wu[0].shape[1], d // 2
            g_up = sums(u[0][:, :half], u[1][:, :half], 1)
            beside = [jnp.concatenate(jnp.split(v[:, half : half + side], 2, axis=0), axis=1) for v in u]
            g_out = sums(*beside, 0)
            q = natural(*q_own), natural(*q_other)
            wide = 3 * qkv[0].shape[1] // 3
            g_qkv = sums(*[v[:, :wide].reshape(d, 3, -1) for v in q], 2)
            g_qb = sums(*[v[:, wide].reshape(2, -1) for v in q], 1)
            small_two = [v[:, half + side :].T for v in u]
            g_bu = sums(*[v[4:6].reshape(-1) for v in small_two], 0)
            shared_two = lax.psum(small_two[0][:4], ("dp", "tensor")).astype(F32)
            shared_one = lax.psum(rows_of(small_one), ("dp", "tensor"))
        return (
            layer_out, input_grad, shared_one[0], shared_one[1], g_qkv, g_qb, g_out, shared_two[2],
            shared_two[0], shared_two[1], g_up, g_bu, g_down, shared_two[3],
        )

    return body


def solution(mesh):
    in_specs = (
        P(("dp", "tensor"), None), P(("dp", "tensor"), None), P("dp"), P("dp", None), P("dp", None), P(), P(),
        P(None, None, "tensor"), P(None, "tensor"), P("tensor", None), P(), P(), P(), P(None, "tensor"),
        P("tensor"), P("tensor", None), P(),
    )
    out_specs = (
        P(("dp", "tensor"), None), P(("dp", "tensor"), None), P(), P(), P(None, None, "tensor"), P(None, "tensor"),
        P("tensor", None), P(), P(), P(), P(None, "tensor"), P("tensor"), P("tensor", None), P(),
    )
    return jax.shard_map(make_body(mesh), mesh=mesh, in_specs=in_specs, out_specs=out_specs, check_vma=False)
```

time: 366 us -> 285 us (0.78)
  blocking collectives: 73.6 us -> 0 us
  starting transfers between devices: 13.6 us -> 31.8 us
  between operations: 14.2 us -> 1.32 us
  Pallas kernels: 214 us -> 203 us
  other arithmetic: 15.9 us -> 11 us
    psum x2 -> x0, blocking collectives: 73.6 us -> none  [the longest x1 40 us: body(): lax.psum(jnp.concatenate([small_one[0:2], small_two[0:4]], axis=0), ('dp'...]
    pallas_call x2, Pallas kernels: 57 us -> 24.6 us  [attention_forward(): pl.pallas_call(body, grid_spec=pltpu.PrefetchScalarGridSpec(num_scalar_pr...]
    pallas_call x4 -> x13, Pallas kernels: 157 us -> 178 us  [call(): pl.pallas_call(kernel, grid_spec=pltpu.PrefetchScalarGridSpec(num_scalar_...]
    ppermute x12 -> x38, starting transfers between devices: 13.6 us -> 31.8 us  [the longest x30 22.8 us: swap(): return lax.ppermute(v, 'dp', [(i, i ^ distance) for i in range(dp)])]
    add x6 -> x5, other arithmetic: 8.07 us -> 0.03 us  [plus(): total = total + v.astype(F32)]
    ppermute x12 -> x38, waiting for transfers between devices: 10.3 us -> 18.2 us  [the longest x8 9.44 us: across(): return lax.ppermute(v, 'tensor', [(0, 1), (1, 0)])]
    psum x1 -> x0, waiting for transfers between devices: 7.88 us -> none  [finish(): return lax.psum(reduce_halves(own, other, axis), 'dp').astype(F32)]
    concatenate x1 -> x13, other arithmetic: 0.01 us -> 4.87 us  [the longest x3 3.1 us: whole(): jnp.concatenate([jnp.where(odd == 0, mine, theirs), jnp.where(odd == 0, t...]
  transfers between devices with their start and end apart: 13 -> 38, of which waited for: 3 -> 8; matrix products, arithmetic and copies ran while one was open for 5% -> 5% of each run, Pallas kernels for 35% -> 71%
where the time goes in v2:
time: 285 us; the launch traced here: 284 us
  Pallas kernels  203 us (71%)
  starting transfers between devices  31.8 us (11%)
  local copies, waits for them, and re-layouts  19.1 us (7%)
  waiting for transfers between devices  18.2 us (6%)
  other arithmetic  11 us (4%)
    pallas_call x13, Pallas kernels, call(): pl.pallas_call(kernel, grid_spec=pltpu.PrefetchScalarGridSpec(num_scalar_...  178 us
    pallas_call x2, Pallas kernels, attention_forward(): pl.pallas_call(body, grid_spec=pltpu.PrefetchScalarGridSpec(num_scalar_pr...  24.6 us
    ppermute x30, starting transfers between devices, swap(): return lax.ppermute(v, 'dp', [(i, i ^ distance) for i in range(dp)])  22.8 us
    ppermute x8, waiting for transfers between devices, across(): return lax.ppermute(v, 'tensor', [(0, 1), (1, 0)])  9.44 us
    ppermute x8, starting transfers between devices, across(): return lax.ppermute(v, 'tensor', [(0, 1), (1, 0)])  9.04 us
    ppermute x30, waiting for transfers between devices, swap(): return lax.ppermute(v, 'dp', [(i, i ^ distance) for i in range(dp)])  8.76 us
    unnamed x42, local copies, waits for them, and re-layouts  5.75 us
  transfers between devices with their start and end apart: 38, of which 8 were waited for; matrix products, arithmetic and copies ran while one was open for 5% of the time, Pallas kernels for 71%

profile of v2, /device:TPU:0, one launch (start us, length us, event | category | flops | bytes accessed | tf_op | source)
XLA Modules:
  0.0 284.0 jit_solution(6626159965717966207)
XLA Ops:
  7.1 3.0 %collective-permute-start.2 = (f32[6,256]{1,0:T(8,128)S(1)}, f32[6,256]{1,0:T(8,128)S(1)}, u32[]{:S(2)}, u32[]{:S(2)}) collective-permute-start(f32[6,256]{1,0:T(8,128)S(1)} %pad_maximum_fusion.9), channel_id=1, source_target_pairs={{0,1},{1,0},{2,3},{3,2},{4,5},{5,4},{6,7},{7,6},{8,9},{9,8},{10,11... | collective-permute-start | bytes 18440 | tf_op jit(solution)/shard_map/ppermute | solution.py:620
  10.2 1.9 collective-permute-start.1
  14.1 13.3 %attend_first.1 = (bf16[4096,512]{1,0:T(8,128)(2,1)}, bf16[4096,768]{1,0:T(8,128)(2,1)}, bf16[4096,256]{1,0:T(8,128)(2,1)}, bf16[6144,256]{1,0:T(8,128)(2,1)}) custom-call(s32[21]{0:T(128)} %pad_add_fusion.1.refs_0_.scal, bf16[4096,512]{1,0:T(8,128)(2,1)} %refs_1_.6, bf16[512,768]{1,0:T(8,128)(2,1)} %copy.39.refs_2_, f32[1,768]{1,0:T(1,128)} %pad_maximum_fusion.10.refs_3_, ...), custom_call_target="tpu_custom_call" | custom-call | flops 4026531840 | bytes 16777216 | tf_op jit(solution)/shard_map/attend_first/pallas_call | solution.py:170
  27.4 7.6 %collective-permute-done.1 = bf16[320,1024]{1,0:T(8,128)(2,1)S(1)} collective-permute-done((bf16[320,1024]{1,0:T(8,128)(2,1)S(1)}, bf16[320,1024]{1,0:T(8,128)(2,1)S(1)}, u32[]{:S(2)}, u32[]{:S(2)}) %collective-permute-start.1) | collective-permute-done | bytes 655392 | tf_op jit(solution)/shard_map/ppermute | solution.py:620
  40.4 11.3 %attend_second.1 = (bf16[4096,768]{1,0:T(8,128)(2,1)}, bf16[4096,256]{1,0:T(8,128)(2,1)}, bf16[6144,256]{1,0:T(8,128)(2,1)}) custom-call(s32[21]{0:T(128)} %pad_add_fusion.1.refs_0_.scal, bf16[4096,512]{1,0:T(8,128)(2,1)} %get-tuple-element.309.refs_1_, bf16[512,768]{1,0:T(8,128)(2,1)} %pad_maximum_fusion.2.refs_2_.refs_6_, f32[1,768]{1,0:T(1,128)} %pad_maximum_fusion.11.refs_3_), custom_call_target="tpu_custom_call" | custom-call | flops 4026531840 | bytes 16777216 | tf_op jit(solution)/shard_map/attend_second/pallas_call | solution.py:170
  51.6 1.9 collective-permute-done.5
  55.5 45.6 %feed_up.1 = (f32[4096,512]{1,0:T(8,128)}, bf16[4096,512]{1,0:T(8,128)(2,1)}, bf16[4096,2048]{1,0:T(8,128)(2,1)}, bf16[4096,2048]{1,0:T(8,128)(2,1)}, bf16[16,32...) custom-call(s32[21]{0:T(128)} %pad_add_fusion.1.refs_0_.scal, bf16[4096,512]{1,0:T(8,128)(2,1)} %refs_1_.6, ...), custom_call_target="tpu_custom_call" | custom-call | flops 19327352832 | bytes 71303168 | tf_op jit(solution)/shard_map/feed_up/pallas_call | solution.py:279
  102.7 44.1 %feed_back.1 = (f32[4096,512]{1,0:T(8,128)}, bf16[4096,256]{1,0:T(8,128)(2,1)}, bf16[4096,256]{1,0:T(8,128)(2,1)}, bf16[8,32,1408]{2,1,0:T(8,128)(2,1)}, bf16[8,...) custom-call(s32[21]{0:T(128)} %pad_add_fusion.1.refs_0_.scal, ...), custom_call_target="tpu_custom_call" | custom-call | flops 30064771072 | bytes 50331648 | tf_op jit(solution)/shard_map/feed_back/pallas_call | solution.py:279
  153.7 16.0 %attend_back.2 = (bf16[4096,768]{1,0:T(8,128)(2,1)}, bf16[8,32,896]{2,1,0:T(8,128)(2,1)}, bf16[8,32,896]{2,1,0:T(8,128)(2,1)}) custom-call(s32[21]{0:T(128)} %pad_add_fusion.1.refs_0_.scal, bf16[4096,512]{1,0:T(8,128)(2,1)} %get-tuple-element.309.refs_1_, bf16[4096,768]{1,0:T(8,128)(2,1)} %get-tuple-element.294.refs_2_, ...), custom_call_target="tpu_custom_call" | custom-call | flops 4831838208 | bytes 23068672 | tf_op jit(solution)/shard_map/attend_back/pallas_call | solution.py:279
  176.0 16.0 %attend_back.3 = (bf16[4096,768]{1,0:T(8,128)(2,1)}, bf16[8,32,896]{2,1,0:T(8,128)(2,1)}, bf16[8,32,896]{2,1,0:T(8,128)(2,1)}) custom-call(s32[21]{0:T(128)} %pad_add_fusion.1.refs_0_.scal, bf16[4096,512]{1,0:T(8,128)(2,1)} %get-tuple-element.309.refs_1_, bf16[4096,768]{1,0:T(8,128)(2,1)} %get-tuple-element.310.refs_2_, ...), custom_call_target="tpu_custom_call" | custom-call | flops 4831838208 | bytes 23068672 | tf_op jit(solution)/shard_map/attend_back/pallas_call | solution.py:279
  192.2 1.9 collective-permute-done.17
  194.3 2.7 collective-permute-start.19
  199.1 11.1 %input_gradient.2 = (f32[4096,512]{1,0:T(8,128)}, f32[16,512]{1,0:T(8,128)}) custom-call(s32[21]{0:T(128)} %pad_add_fusion.1.refs_0_.scal, bf16[4096,512]{1,0:T(8,128)(2,1)} %refs_1_.6, f32[4096,512]{1,0:T(8,128)} %get-tuple-element.341.refs_2_, bf16[4096,768]{1,0:T(8,128)(2,1)} %get-tuple-element.342.refs_3_, bf16[4096,768]{1,0:T(8,128)(2,1)} %get-tuple-element.343.refs_4_, ...), custom_call_target="tpu_custom_call" | custom-call | flops 3221225472 | bytes 16777216 | tf_op jit(solution)/shard_map/input_gradient/pallas_call | solution.py:279
  214.0 11.3 %input_gradient.3 = (f32[4096,512]{1,0:T(8,128)}, f32[16,512]{1,0:T(8,128)}) custom-call(s32[21]{0:T(128)} %pad_add_fusion.1.refs_0_.scal, bf16[4096,512]{1,0:T(8,128)(2,1)} %refs_1_.6, f32[4096,512]{1,0:T(8,128)} %get-tuple-element.341.refs_2_, bf16[4096,768]{1,0:T(8,128)(2,1)} %get-tuple-element.342.refs_3_, ...), custom_call_target="tpu_custom_call", output_to_operand_aliasing={{0}: (8, {})} | custom-call | flops 3221225472 | bytes 16777216 | tf_op jit(solution)/shard_map/input_gradient/pallas_call | solution.py:279
  228.4 2.7 collective-permute-start.26
  232.7 5.8 %layer_out.4.refs_0_ = bf16[4096,512]{1,0:T(8,128)(2,1)} custom-call(f32[4096,512]{1,0:T(8,128)} %get-tuple-element.394.mid, bf16[4096,2048]{1,0:T(8,128)(2,1)} %get-tuple-element.395.hidden, bf16[1024,512]{1,0:T(8,128)(2,1)} %wd_a.4, bf16[1024,512]{1,0:T(8,128)(2,1)} %pad_maximum_fusion.1.wd_b, f32[1,512]{1,0:T(1,128)} %bitcast.33), custom_call_target="tpu_custom_call" | custom-call | flops 2147483648 | bytes 7340032 | tf_op jit(solution)/shard_map/layer_out/pallas_call | solution.py:279
  240.5 5.8 %layer_out.5.refs_0_ = bf16[4096,512]{1,0:T(8,128)(2,1)} custom-call(f32[4096,512]{1,0:T(8,128)} %get-tuple-element.394.mid, bf16[4096,2048]{1,0:T(8,128)(2,1)} %get-tuple-element.395.hidden, bf16[1024,512]{1,0:T(8,128)(2,1)} %wd_a.4, bf16[1024,512]{1,0:T(8,128)(2,1)} %pad_maximum_fusion.1.wd_b, f32[1,512]{1,0:T(1,128)} %bitcast.34, ...), custom_call_target="tpu_custom_call", output_to_operand_aliasing={{}: (5, {})} | custom-call | flops 2147483648 | bytes 7340032 | tf_op jit(solution)/shard_map/layer_out/pallas_call | solution.py:279
  246.3 3.2 %collective-permute-done.28 = bf16[4,32,1408]{2,1,0:T(8,128)(2,1)S(1)} collective-permute-done((bf16[4,32,1408]{2,1,0:T(8,128)(2,1)S(1)}, bf16[4,32,1408]{2,1,0:T(8,128)(2,1)S(1)}, u32[]{:S(2)}, u32[]{:S(2)}) %collective-permute-start.28) | collective-permute-done | bytes 360480 | tf_op jit(solution)/shard_map/ppermute | solution.py:623
  251.9 5.8 %layer_out.6.refs_0_ = bf16[4096,512]{1,0:T(8,128)(2,1)} custom-call(f32[4096,512]{1,0:T(8,128)} %get-tuple-element.394.mid, bf16[4096,2048]{1,0:T(8,128)(2,1)} %get-tuple-element.395.hidden, bf16[1024,512]{1,0:T(8,128)(2,1)} %wd_a.4, bf16[1024,512]{1,0:T(8,128)(2,1)} %pad_maximum_fusion.1.wd_b, f32[1,512]{1,0:T(1,128)} %bitcast.35, ...), custom_call_target="tpu_custom_call", output_to_operand_aliasing={{}: (5, {})} | custom-call | flops 2147483648 | bytes 7340032 | tf_op jit(solution)/shard_map/layer_out/pallas_call | solution.py:279
  257.7 3.6 %unpack_down.1 = f32[1024,512]{1,0:T(8,128)} custom-call(s32[21]{0:T(128)} %pad_add_fusion.1.refs_0_.scal, bf16[8,32,1024]{2,1,0:T(8,128)(2,1)} %copy-done.2, bf16[8,32,1024]{2,1,0:T(8,128)(2,1)} %copy-done.9), custom_call_target="tpu_custom_call" | custom-call | bytes 3145728 | tf_op jit(solution)/shard_map/unpack_down/pallas_call | solution.py:279
  262.3 3.7 %unpack_up.1 = (f32[512,1024]{1,0:T(8,128)}, f32[256,512]{1,0:T(8,128)}, f32[8,512]{1,0:T(8,128)}) custom-call(s32[21]{0:T(128)} %pad_add_fusion.1.refs_0_.scal, bf16[8,32,1408]{2,1,0:T(8,128)(2,1)} %copy-done.1, bf16[8,32,1408]{2,1,0:T(8,128)(2,1)} %copy-done.8), custom_call_target="tpu_custom_call" | custom-call | bytes 4325376 | tf_op jit(solution)/shard_map/unpack_up/pallas_call | solution.py:279
  268.2 5.8 %layer_out.7 = bf16[4096,512]{1,0:T(8,128)(2,1)} custom-call(f32[4096,512]{1,0:T(8,128)} %get-tuple-element.394.mid, bf16[4096,2048]{1,0:T(8,128)(2,1)} %get-tuple-element.395.hidden, bf16[1024,512]{1,0:T(8,128)(2,1)} %wd_a.4, bf16[1024,512]{1,0:T(8,128)(2,1)} %pad_maximum_fusion.1.wd_b, f32[1,512]{1,0:T(1,128)} %bitcast.36, ...), custom_call_target="tpu_custom_call", output_to_operand_aliasing={{}: (5, {})} | custom-call | flops 2147483648 | bytes 7340032 | tf_op jit(solution)/shard_map/layer_out/pallas_call | solution.py:279
  275.4 3.2 %unpack_qkv.1 = (f32[512,768]{1,0:T(8,128)}, f32[8,512]{1,0:T(8,128)}) custom-call(s32[21]{0:T(128)} %pad_add_fusion.1.refs_0_.scal, bf16[8,32,896]{2,1,0:T(8,128)(2,1)} %copy-done.3, bf16[8,32,896]{2,1,0:T(8,128)(2,1)} %copy-done.11), custom_call_target="tpu_custom_call" | custom-call | bytes 2752512 | tf_op jit(solution)/shard_map/unpack_qkv/pallas_call | solution.py:279
  279.4 1.9 copy.42
  (176 shorter events, 53.4 us)
Async XLA Ops:
  7.1 20.3 %collective-permute-start.2 = (f32[6,256]{1,0:T(8,128)S(1)}, f32[6,256]{1,0:T(8,128)S(1)}, u32[]{:S(2)}, u32[]{:S(2)}) collective-permute-start(f32[6,256]{1,0:T(8,128)S(1)} %pad_maximum_fusion.9), channel_id=1, source_target_pairs={{0,1},{1,0},{2,3},{3,2},{4,5},{5,4},{6,7},{7,6},{8,9},{9,8},{10,11... | collective-permute-start | bytes 18440 | tf_op jit(solution)/shard_map/ppermute | solution.py:620
  10.1 17.3 %collective-permute-start = (bf16[256,768]{1,0:T(8,128)(2,1)}, bf16[256,768]{1,0:T(8,128)(2,1)}, u32[]{:S(2)}, u32[]{:S(2)}) collective-permute-start(bf16[256,768]{1,0:T(8,128)(2,1)} %copy.44), channel_id=1, source_target_pairs={{0,1},{1,0},{2,3},{3,2},{4,5},{5,4},{6,7},{7,6},{8,9},{9,8},{10,11... | collective-permute-start | bytes 1179656 | tf_op jit(solution)/shard_map/ppermute | solution.py:620
  10.2 24.8 %collective-permute-start.1 = (bf16[320,1024]{1,0:T(8,128)(2,1)S(1)}, bf16[320,1024]{1,0:T(8,128)(2,1)S(1)}, u32[]{:S(2)}, u32[]{:S(2)}) collective-permute-start(bf16[320,1024]{1,0:T(8,128)(2,1)S(1)} %fusion), channel_id=1, source_target_pairs={{0,1},{1,0},{2,3},{3,2},{4,5},{5,4},{6,7},{7,6},{8,9},{9,8},{10,11... | collective-permute-start | bytes 1966088 | tf_op jit(solution)/shard_map/ppermute | solution.py:620
  39.2 14.3 %collective-permute-start.4 = (bf16[320,1024]{1,0:T(8,128)(2,1)S(1)}, bf16[320,1024]{1,0:T(8,128)(2,1)S(1)}, u32[]{:S(2)}, u32[]{:S(2)}) collective-permute-start(bf16[320,1024]{1,0:T(8,128)(2,1)S(1)} %collective-permute-done.1), channel_id=1, source_target_pairs={{0,2},{2,0},{4,6},{6,4},{8,10},{10,8},{12,14},{14,12},{16,18},{18,... | collective-permute-start | bytes 1966088 | tf_op jit(solution)/shard_map/ppermute | solution.py:623
  39.3 14.2 %collective-permute-start.5 = (bf16[512,512]{1,0:T(8,128)(2,1)S(1)}, bf16[512,512]{1,0:T(8,128)(2,1)S(1)}, u32[]{:S(2)}, u32[]{:S(2)}) collective-permute-start(bf16[512,512]{1,0:T(8,128)(2,1)S(1)} %constant_dynamic-slice_fusion), channel_id=1, source_target_pairs={{0,1},{1,0},{2,3},{3,2},{4,5},{5,4},{6,7},{7,6},{8,9},{9,8},{10,11... | collective-permute-start | bytes 1572872 | tf_op jit(solution)/shard_map/ppermute | solution.py:620
  55.5 45.7 %collective-permute-start.6 = (bf16[512,512]{1,0:T(8,128)(2,1)S(1)}, bf16[512,512]{1,0:T(8,128)(2,1)S(1)}, u32[]{:S(2)}, u32[]{:S(2)}) collective-permute-start(bf16[512,512]{1,0:T(8,128)(2,1)S(1)} %collective-permute-done.5), channel_id=1, source_target_pairs={{0,2},{2,0},{4,6},{6,4},{8,10},{10,8},{12,14},{14,12},{16,18},{18,... | collective-permute-start | bytes 1572872 | tf_op jit(solution)/shard_map/ppermute | solution.py:623
  102.3 44.6 %collective-permute-start.7 = (bf16[16,32,1024]{2,1,0:T(8,128)(2,1)}, bf16[16,32,1024]{2,1,0:T(8,128)(2,1)S(1)}, u32[]{:S(2)}, u32[]{:S(2)}) collective-permute-start(bf16[16,32,1024]{2,1,0:T(8,128)(2,1)} %get-tuple-element.283), channel_id=1, source_target_pairs={{0,1},{1,0},{2,3},{3,2},{4,5},{5,4},{6,7},{7,6},{8,9},{9,8},{10,11... | collective-permute-start | bytes 3145736 | tf_op jit(solution)/shard_map/ppermute | solution.py:620
  150.6 19.1 %collective-permute-start.11 = (bf16[8,32,1408]{2,1,0:T(8,128)(2,1)S(1)}, bf16[8,32,1408]{2,1,0:T(8,128)(2,1)S(1)}, u32[]{:S(2)}, u32[]{:S(2)}) collective-permute-start(bf16[8,32,1408]{2,1,0:T(8,128)(2,1)S(1)} %add_convert_fusion.2), channel_id=1, source_target_pairs={{0,1},{1,0},{2,3},{3,2},{4,5},{5,4},{6,7},{7,6},{8,9},{9,8},{10,11... | collective-permute-start | bytes 2162696 | tf_op jit(solution)/shard_map/ppermute | solution.py:620
  152.2 17.9 %collective-permute-start.8 = (bf16[8,32,1408]{2,1,0:T(8,128)(2,1)}, bf16[8,32,1408]{2,1,0:T(8,128)(2,1)}, u32[]{:S(2)}, u32[]{:S(2)}) collective-permute-start(bf16[8,32,1408]{2,1,0:T(8,128)(2,1)} %get-tuple-element.285), channel_id=1, source_target_pairs={{0,2},{2,0},{4,6},{6,4},{8,10},{10,8},{12,14},{14,12},{16,18},{18,... | collective-permute-start | bytes 2162696 | tf_op jit(solution)/shard_map/ppermute | solution.py:623
  152.2 17.5 %collective-permute-start.12 = (bf16[4,32,1024]{2,1,0:T(8,128)(2,1)S(1)}, bf16[4,32,1024]{2,1,0:T(8,128)(2,1)S(1)}, u32[]{:S(2)}, u32[]{:S(2)}) collective-permute-start(bf16[4,32,1024]{2,1,0:T(8,128)(2,1)S(1)} %slice.122), channel_id=1, source_target_pairs={{0,4},{2,6},{4,0},{6,2},{8,12},{10,14},{12,8},{14,10},{16,20},{18,... | collective-permute-start | bytes 786440 | tf_op jit(solution)/shard_map/ppermute | solution.py:623
  172.1 19.9 %collective-permute-start.16 = (bf16[8,32,896]{2,1,0:T(8,128)(2,1)S(1)}, bf16[8,32,896]{2,1,0:T(8,128)(2,1)S(1)}, u32[]{:S(2)}, u32[]{:S(2)}) collective-permute-start(bf16[8,32,896]{2,1,0:T(8,128)(2,1)S(1)} %add_convert_fusion.6), channel_id=1, source_target_pairs={{0,1},{1,0},{2,3},{3,2},{4,5},{5,4},{6,7},{7,6},{8,9},{9,8},{10,11... | collective-permute-start | bytes 1376264 | tf_op jit(solution)/shard_map/ppermute | solution.py:620
  172.9 19.1 %collective-permute-start.15 = (bf16[2,32,1024]{2,1,0:T(8,128)(2,1)S(1)}, bf16[2,32,1024]{2,1,0:T(8,128)(2,1)S(1)}, u32[]{:S(2)}, u32[]{:S(2)}) collective-permute-start(bf16[2,32,1024]{2,1,0:T(8,128)(2,1)S(1)} %slice.126), channel_id=1, source_target_pairs={{0,8},{2,10},{4,12},{6,14},{8,0},{10,2},{12,4},{14,6},{16,24},{18,... | collective-permute-start | bytes 393224 | tf_op jit(solution)/shard_map/ppermute | solution.py:623
  174.5 17.5 %collective-permute-start.14 = (bf16[4,32,1408]{2,1,0:T(8,128)(2,1)S(1)}, bf16[4,32,1408]{2,1,0:T(8,128)(2,1)S(1)}, u32[]{:S(2)}, u32[]{:S(2)}) collective-permute-start(bf16[4,32,1408]{2,1,0:T(8,128)(2,1)S(1)} %slice.124), channel_id=1, source_target_pairs={{0,4},{2,6},{4,0},{6,2},{8,12},{10,14},{12,8},{14,10},{16,20},{18,... | collective-permute-start | bytes 1081352 | tf_op jit(solution)/shard_map/ppermute | solution.py:623
  194.3 15.9 %collective-permute-start.19 = (bf16[2,32,1024]{2,1,0:T(8,128)(2,1)S(1)}, bf16[2,32,1024]{2,1,0:T(8,128)(2,1)S(1)}, u32[]{:S(2)}, u32[]{:S(2)}) collective-permute-start(bf16[2,32,1024]{2,1,0:T(8,128)(2,1)S(1)} %add_convert_fusion.13), channel_id=1, source_target_pairs={{0,16},{2,18},{4,20},{6,22},{8,24},{10,26},{12,28},{14,30},{16,0},... | collective-permute-start | bytes 393224 | tf_op jit(solution)/shard_map/ppermute | solution.py:623
  196.9 13.3 %collective-permute-start.18 = (bf16[2,32,1408]{2,1,0:T(8,128)(2,1)S(1)}, bf16[2,32,1408]{2,1,0:T(8,128)(2,1)S(1)}, u32[]{:S(2)}, u32[]{:S(2)}) collective-permute-start(bf16[2,32,1408]{2,1,0:T(8,128)(2,1)S(1)} %slice.128), channel_id=1, source_target_pairs={{0,8},{2,10},{4,12},{6,14},{8,0},{10,2},{12,4},{14,6},{16,24},{18,... | collective-permute-start | bytes 540680 | tf_op jit(solution)/shard_map/ppermute | solution.py:623
  197.4 12.8 %collective-permute-start.20 = (bf16[4,32,896]{2,1,0:T(8,128)(2,1)S(1)}, bf16[4,32,896]{2,1,0:T(8,128)(2,1)S(1)}, u32[]{:S(2)}, u32[]{:S(2)}) collective-permute-start(bf16[4,32,896]{2,1,0:T(8,128)(2,1)S(1)} %slice.130), channel_id=1, source_target_pairs={{0,4},{2,6},{4,0},{6,2},{8,12},{10,14},{12,8},{14,10},{16,20},{18,... | collective-permute-start | bytes 688136 | tf_op jit(solution)/shard_map/ppermute | solution.py:623
  210.4 14.9 %collective-permute-start.23 = (bf16[2,32,896]{2,1,0:T(8,128)(2,1)S(1)}, bf16[2,32,896]{2,1,0:T(8,128)(2,1)S(1)}, u32[]{:S(2)}, u32[]{:S(2)}) collective-permute-start(bf16[2,32,896]{2,1,0:T(8,128)(2,1)S(1)} %slice.132), channel_id=1, source_target_pairs={{0,8},{2,10},{4,12},{6,14},{8,0},{10,2},{12,4},{14,6},{16,24},{18,... | collective-permute-start | bytes 344072 | tf_op jit(solution)/shard_map/ppermute | solution.py:623
  212.1 13.2 %collective-permute-start.22 = (bf16[2,32,1024]{2,1,0:T(8,128)(2,1)S(1)}, bf16[2,32,1024]{2,1,0:T(8,128)(2,1)S(1)}, u32[]{:S(2)}, u32[]{:S(2)}) collective-permute-start(bf16[2,32,1024]{2,1,0:T(8,128)(2,1)S(1)} %add_convert_fusion.12), channel_id=1, source_target_pairs={{0,8},{2,10},{4,12},{6,14},{8,0},{10,2},{12,4},{14,6},{16,24},{18,... | collective-permute-start | bytes 393224 | tf_op jit(solution)/shard_map/ppermute | solution.py:623
  212.5 12.8 %collective-permute-start.21 = (bf16[2,32,1408]{2,1,0:T(8,128)(2,1)S(1)}, bf16[2,32,1408]{2,1,0:T(8,128)(2,1)S(1)}, u32[]{:S(2)}, u32[]{:S(2)}) collective-permute-start(bf16[2,32,1408]{2,1,0:T(8,128)(2,1)S(1)} %add_convert_fusion.11), channel_id=1, source_target_pairs={{0,16},{2,18},{4,20},{6,22},{8,24},{10,26},{12,28},{14,30},{16,0},... | collective-permute-start | bytes 540680 | tf_op jit(solution)/shard_map/ppermute | solution.py:623
  226.2 12.3 %collective-permute-start.25 = (bf16[4,32,1024]{2,1,0:T(8,128)(2,1)S(1)}, bf16[4,32,1024]{2,1,0:T(8,128)(2,1)S(1)}, u32[]{:S(2)}, u32[]{:S(2)}) collective-permute-start(bf16[4,32,1024]{2,1,0:T(8,128)(2,1)S(1)} %pad_maximum_fusion.7), channel_id=1, source_target_pairs={{0,4},{2,6},{4,0},{6,2},{8,12},{10,14},{12,8},{14,10},{16,20},{18,... | collective-permute-start | bytes 786440 | tf_op jit(solution)/shard_map/ppermute | solution.py:623
  249.7 11.6 %collective-permute-start.32 = (bf16[8,32,1408]{2,1,0:T(8,128)(2,1)S(1)}, bf16[8,32,1408]{2,1,0:T(8,128)(2,1)S(1)}, u32[]{:S(2)}, u32[]{:S(2)}) collective-permute-start(bf16[8,32,1408]{2,1,0:T(8,128)(2,1)S(1)} %pad_maximum_fusion.3.p0), channel_id=1, source_target_pairs={{0,2},{2,0},{4,6},{6,4},{8,10},{10,8},{12,14},{14,12},{16,18},{18,... | collective-permute-start | bytes 2162696 | tf_op jit(solution)/shard_map/ppermute | solution.py:623
  249.8 11.5 %collective-permute-start.33 = (bf16[4,32,896]{2,1,0:T(8,128)(2,1)S(1)}, bf16[4,32,896]{2,1,0:T(8,128)(2,1)S(1)}, u32[]{:S(2)}, u32[]{:S(2)}) collective-permute-start(bf16[4,32,896]{2,1,0:T(8,128)(2,1)S(1)} %pad_maximum_fusion.8), channel_id=1, source_target_pairs={{0,4},{2,6},{4,0},{6,2},{8,12},{10,14},{12,8},{14,10},{16,20},{18,... | collective-permute-start | bytes 688136 | tf_op jit(solution)/shard_map/ppermute | solution.py:623
  261.5 13.1 %collective-permute-start.36 = (f32[2,512]{1,0:T(2,128)S(1)}, f32[2,512]{1,0:T(2,128)S(1)}, u32[]{:S(2)}, u32[]{:S(2)}) collective-permute-start(f32[2,512]{1,0:T(2,128)S(1)} %add.105), channel_id=1, source_target_pairs={{0,8},{2,10},{4,12},{6,14},{8,0},{10,2},{12,4},{14,6},{16,24},{18,... | collective-permute-start | bytes 12296 | tf_op jit(solution)/shard_map/ppermute | solution.py:623
  262.0 12.6 %collective-permute-start.35 = (bf16[8,32,896]{2,1,0:T(8,128)(2,1)S(1)}, bf16[8,32,896]{2,1,0:T(8,128)(2,1)S(1)}, u32[]{:S(2)}, u32[]{:S(2)}) collective-permute-start(bf16[8,32,896]{2,1,0:T(8,128)(2,1)S(1)} %pad_maximum_fusion.5.p0), channel_id=1, source_target_pairs={{0,2},{2,0},{4,6},{6,4},{8,10},{10,8},{12,14},{14,12},{16,18},{18,... | collective-permute-start | bytes 1376264 | tf_op jit(solution)/shard_map/ppermute | solution.py:623
  (32 other events, 262.3 us)

commit v3 on v2

v3 whole, which is shorter than its diff:
```python
import jax
import jax.numpy as jnp
from jax import lax
from jax.experimental import pallas as pl
from jax.experimental.pallas import tpu as pltpu
from jax.sharding import PartitionSpec as P

HEAD_DIM = 64
SEQ_LEN = 1024
LEFT = 10
RIGHT = 2
QB = 64
MARGIN = 16
WIN = QB + 2 * MARGIN
NBLK = SEQ_LEN // QB
EPS = 1e-05
LN_ROWS = 256
NEG = -1000000000.0
VMEM = 60 * 1024 * 1024
F32 = jnp.float32
BF16 = jnp.bfloat16


def dot_nn(a, b):
    return jnp.dot(a, b, preferred_element_type=F32)


def dot_nt(a, b):
    return lax.dot_general(a, b, (((1,), (1,)), ((), ())), preferred_element_type=F32)


def dot_tn(a, b):
    return lax.dot_general(a, b, (((0,), (0,)), ((), ())), preferred_element_type=F32)


def length_of(scal, seq):
    return scal[3 + scal[2] + seq]


def keep_of(shape, first_pos, seq, scal):
    seqs = (scal.shape[0] - 3) // 5
    ends = [scal[3 + k * seqs + scal[2] + seq] for k in range(1, 5)]
    pos = first_pos + lax.broadcasted_iota(jnp.int32, (shape[0], 1), 0)
    col = lax.broadcasted_iota(jnp.int32, (1, shape[1]), 1)
    rows = jnp.where((pos >= ends[0]) & (pos < ends[1]), 0.0, 1.0)
    cols = jnp.where((col >= ends[2]) & (col < ends[3]), 0.0, 1.0)
    return rows * cols


def normalize(v):
    off = v - jnp.mean(v, axis=-1, keepdims=True)
    r = lax.rsqrt(jnp.mean(off * off, axis=-1, keepdims=True) + EPS)
    return off * r, r


def head_mask(scale, heads):
    row = lax.broadcasted_iota(jnp.int32, (heads * QB, heads * HEAD_DIM), 0)
    col = lax.broadcasted_iota(jnp.int32, (heads * QB, heads * HEAD_DIM), 1)
    return jnp.where(row // QB == col // HEAD_DIM, scale, 0.0).astype(BF16)


def spread(block, mask, heads):
    return jnp.concatenate([block] * heads, axis=0) * mask


def pair_rows(probs, window, heads):
    out = []
    low = lax.broadcasted_iota(jnp.int32, (QB, 2 * HEAD_DIM), 1) < HEAD_DIM
    for p in range(heads // 2):
        both = dot_tn(
            probs[:, p * 2 * QB : (p + 1) * 2 * QB],
            window[:, p * 2 * HEAD_DIM : (p + 1) * 2 * HEAD_DIM],
        )
        out.append(jnp.where(low, both[:QB], both[QB:]))
    return jnp.concatenate(out, axis=1)


def attend(length, proj, kpad, vpad, scores, ctx, probs_out, heads):
    width = heads * HEAD_DIM
    edge = jnp.zeros((MARGIN, width), BF16)
    for pad, j in ((kpad, 1), (vpad, 2)):
        pad[0:MARGIN, :] = edge
        pad[MARGIN + SEQ_LEN :, :] = edge
        pad[MARGIN : MARGIN + SEQ_LEN, :] = proj[:, j * width : (j + 1) * width]
    mask = head_mask(HEAD_DIM**-0.5, heads)
    key = lax.broadcasted_iota(jnp.int32, (WIN, heads * QB), 0)
    query = lax.broadcasted_iota(jnp.int32, (WIN, heads * QB), 1) % QB
    rel = key - MARGIN - query
    band = jnp.where((rel >= -LEFT) & (rel <= RIGHT), 0.0, NEG)
    diagonal = jnp.where(rel == 0, 0.0, NEG)

    for b in range(NBLK):
        q_all = spread(proj[b * QB : (b + 1) * QB, 0:width], mask, heads)
        scores[b * WIN : (b + 1) * WIN, :] = dot_nt(kpad[b * QB : b * QB + WIN, :], q_all)
    for b in range(NBLK):
        at = slice(b * WIN, (b + 1) * WIN)
        pos = key + (b * QB - MARGIN)
        live = (pos < length) if b else (pos >= 0) & (pos < length)
        masked = scores[at, :] + jnp.where(live, band, diagonal)
        weights = jnp.exp(masked - jnp.max(masked, axis=0, keepdims=True))
        probs_out[at, :] = (weights / jnp.sum(weights, axis=0, keepdims=True)).astype(BF16)
    for b in range(NBLK):
        v_win = vpad[b * QB : b * QB + WIN, :]
        ctx[b * QB : (b + 1) * QB, :] = pair_rows(probs_out[b * WIN : (b + 1) * WIN, :], v_win, heads).astype(BF16)


def project(at, n1, w_side, bias, proj):
    width = bias.shape[1]
    value = dot_nn(n1[at, :], w_side[...])
    proj[at, :width] = (value[:, :width] + bias[0:1, :]).astype(BF16)
    proj[at, width : 2 * width] = value[:, width : 2 * width].astype(BF16)
    proj[at, 2 * width :] = (value[:, 2 * width :] + bias[1:2, :]).astype(BF16)


def side_by_side(i, w, w_side):
    @pl.when(i == 0)
    def _():
        width = w.shape[2]
        for j in range(3):
            w_side[:, j * width : (j + 1) * width] = w[j]


def first_kernel(heads, scal, x, w, bias, gain, shift, nn, n1, proj, ctx, probs, w_side, *scratch):
    s = pl.program_id(0)
    side_by_side(s, w, w_side)
    for first in range(0, SEQ_LEN, LN_ROWS):
        at = slice(first, first + LN_ROWS)
        for r in range(first, first + LN_ROWS, SUB):
            sub = slice(r, r + SUB)
            keep = keep_of((SUB, x.shape[1]), r, s, scal)
            value = normalize(x[sub, :].astype(F32) * keep)[0]
            nn[sub, :] = value.astype(BF16)
            n1[sub, :] = (value * gain[...] + shift[...]).astype(BF16)
        project(at, n1, w_side, bias, proj)
    attend(length_of(scal, s), proj, *scratch, ctx, probs, heads)


def second_kernel(heads, scal, n1, w, bias, proj, ctx, probs, w_side, *scratch):
    s = pl.program_id(0)
    side_by_side(s, w, w_side)
    for first in range(0, SEQ_LEN, LN_ROWS):
        project(slice(first, first + LN_ROWS), n1, w_side, bias, proj)
    attend(length_of(scal, s), proj, *scratch, ctx, probs, heads)


def const_spec(shape):
    return pl.BlockSpec(shape, lambda *_: (0,) * len(shape), pipeline_mode=pl.Buffered(1))


def rows_spec(rows, cols):
    return pl.BlockSpec((rows, cols), lambda i, *_: (i, 0))


def params():
    return pltpu.CompilerParams(vmem_limit_bytes=VMEM, dimension_semantics=("arbitrary",))


def attention_forward(first, scal, rows, w, bias, gain, shift):
    total, width_in = rows.shape
    seqs = total // SEQ_LEN
    width = w.shape[2]
    heads = width // HEAD_DIM
    outs = [
        jax.ShapeDtypeStruct((total, 3 * width), BF16),
        jax.ShapeDtypeStruct((total, width), BF16),
        jax.ShapeDtypeStruct((seqs * NBLK * WIN, heads * QB), BF16),
    ]
    out_specs = [
        rows_spec(SEQ_LEN, 3 * width),
        rows_spec(SEQ_LEN, width),
        rows_spec(NBLK * WIN, heads * QB),
    ]
    scratch = [pltpu.VMEM((width_in, 3 * width), BF16)]
    scratch += [pltpu.VMEM((SEQ_LEN + 2 * MARGIN, width), BF16)] * 2
    scratch += [pltpu.VMEM((NBLK * WIN, heads * QB), F32)]
    flops = 2 * total * width_in * 3 * width + 8 * total * WIN * width
    cost = pl.CostEstimate(flops=flops, bytes_accessed=total * (width_in + 6 * width) * 2, transcendentals=0)
    in_specs = [rows_spec(SEQ_LEN, width_in), const_spec(w.shape), const_spec(bias.shape)]
    if first:
        in_specs += [const_spec(gain.shape), const_spec(shift.shape)]
        outs = [jax.ShapeDtypeStruct(rows.shape, BF16)] * 2 + outs
        out_specs = [rows_spec(SEQ_LEN, width_in)] * 2 + out_specs
        args = (rows, w, bias, gain, shift)
    else:
        args = (rows, w, bias)

    def body(*refs):
        (first_kernel if first else second_kernel)(heads, *refs)

    return pl.pallas_call(
        body,
        grid_spec=pltpu.PrefetchScalarGridSpec(
            num_scalar_prefetch=1,
            grid=(seqs,),
            in_specs=in_specs,
            out_specs=out_specs,
            scratch_shapes=scratch,
        ),
        out_shape=outs,
        compiler_params=params(),
        cost_estimate=cost,
        name="attend_first" if first else "attend_second",
    )(scal, *args)


TM = 512
TU = 1024
TB = 512
FC = 512
FB = 512
SUB = 32
GELU_A = 0.7978845608028654
GELU_K = 0.044715 / 0.7978845608028654**2


def subs(rows):
    return [slice(r, r + SUB) for r in range(0, rows, SUB)]


def fold_rows(v):
    return jnp.sum(v.reshape(-1, 8, v.shape[-1]), axis=0)


def clear(i, *refs):
    @pl.when(i == 0)
    def _():
        for ref in refs:
            ref[...] = jnp.zeros_like(ref)


TAIL = 2
ONES = 16
EXTRA = 128
BLOCKS = 16


def put_blocks(me, packs, acc, columns):
    rows = packs[0].shape[1]
    each = BLOCKS // len(packs)
    for j in range(BLOCKS):
        first = pl.multiple_of((j ^ me) * rows, rows)
        packs[j // each][j % each] = acc[pl.ds(first, rows), columns].astype(BF16)


def put_vectors(acc, first, vectors):
    spare = EXTRA - len(vectors)
    rows = vectors[0].shape[1]
    acc[:rows, first:] = jnp.concatenate(vectors + [jnp.zeros((spare, rows), F32)], axis=0).T


def bias_chunk(biases, first, count):
    width = biases.shape[1]
    rows = range(2 + first // width, 2 + (first + count) // width)
    return jnp.concatenate([biases[r : r + 1, :] for r in rows], axis=1)


def up_kernel(
    per_seq, scal,
    x, cot, ctx_a, ctx_b, wo_a, wo_b, wu_a, wu_b, bo, gain, shift, bias_a, bias_b,
    mid_out, n2_out, hidden_out, pre_out, pack_own, pack_other,
    acc_d, wo_s, ctx_s, branch, n2_half, pre_even, pre_odd,
):
    i = pl.program_id(0)
    clear(i, acc_d)
    width = ctx_a.shape[1]

    @pl.when(i == 0)
    def _():
        wo_s[:width, :] = wo_a[...]
        wo_s[width:, :] = wo_b[...]

    rows = x.shape[0]
    ctx_s[:, :width] = ctx_a[...]
    ctx_s[:, width:] = ctx_b[...]
    branch[...] = dot_nn(ctx_s[...], wo_s[...])
    g_t = cot[...].T
    for sub in subs(rows):
        keep = keep_of((SUB, x.shape[1]), (i % per_seq) * rows + sub.start, i // per_seq, scal)
        mid = x[sub, :].astype(F32) * keep + branch[sub, :] + bo[...]
        mid_out[sub, :] = mid
        n2 = (normalize(mid)[0] * gain[...] + shift[...]).astype(BF16)
        n2_out[sub, :] = n2
        n2_half[sub, :] = n2 * 0.5
    half = wu_a.shape[1]
    chunks = [(part, c) for part in range(2) for c in range(half // FC)]
    pres = (pre_even, pre_odd)

    def up(n):
        part, c = chunks[n]
        pres[n % 2][...] = dot_nn(n2_half[...], (wu_a, wu_b)[part][:, c * FC : (c + 1) * FC])

    up(0)
    for n, (part, c) in enumerate(chunks):
        if n + 1 < len(chunks):
            up(n + 1)
        bias = bias_chunk((bias_a, bias_b)[part], c * FC, FC) * 0.5
        ts = slice(part * half + c * FC, part * half + (c + 1) * FC)
        for sub in subs(rows):
            v = pres[n % 2][sub, :] + bias
            z = v * (2 * GELU_A)
            pre_out[sub, ts] = z.astype(BF16)
            t = jnp.tanh(z * (1.0 + GELU_K * (z * z)))
            hidden_out[sub, ts] = (v + v * t).astype(BF16)
        acc_d[:, ts] += dot_nn(g_t, hidden_out[:, ts])

    @pl.when(i == pl.num_programs(0) - 1)
    def _():
        put_blocks(scal[0], [pack_own], acc_d, slice(0, half))
        put_blocks(scal[0], [pack_other], acc_d, slice(half, 2 * half))


def call(kernel, name, grid, scalars, in_specs, outs, out_specs, scratch, flops, nbytes, args, alias=()):
    return pl.pallas_call(
        kernel,
        grid_spec=pltpu.PrefetchScalarGridSpec(
            num_scalar_prefetch=len(scalars), grid=(grid,), in_specs=in_specs, out_specs=out_specs,
            scratch_shapes=scratch,
        ),
        out_shape=[jax.ShapeDtypeStruct(s, t) for s, t in outs],
        compiler_params=params(),
        input_output_aliases=dict(alias),
        cost_estimate=pl.CostEstimate(flops=flops, bytes_accessed=nbytes, transcendentals=0),
        name=name,
    )(*scalars, *args)


def up_block(scal, x, cot, ctx_a, ctx_b, wo, wu, bo, gain, shift, biases):
    total, d = x.shape
    width = ctx_a.shape[1]
    half = wu[0].shape[1]
    args = (x, cot, ctx_a, ctx_b, *wo, *wu, bo, gain, shift, *biases)
    in_specs = [rows_spec(TU, d), rows_spec(TU, d), rows_spec(TU, width), rows_spec(TU, width)]
    in_specs += [const_spec(a.shape) for a in args[4:]]
    pack = (BLOCKS, d // BLOCKS, half)
    outs = [
        ((total, d), F32), ((total, d), BF16), ((total, 2 * half), BF16), ((total, 2 * half), BF16),
        (pack, BF16), (pack, BF16),
    ]
    out_specs = [rows_spec(TU, d), rows_spec(TU, d), rows_spec(TU, 2 * half), rows_spec(TU, 2 * half)]
    out_specs += [const_spec(pack), const_spec(pack)]
    scratch = [
        pltpu.VMEM((d, 2 * half), F32), pltpu.VMEM((2 * width, d), BF16), pltpu.VMEM((TU, 2 * width), BF16),
        pltpu.VMEM((TU, d), F32), pltpu.VMEM((TU, d), BF16), pltpu.VMEM((TU, FC), F32), pltpu.VMEM((TU, FC), F32),
    ]

    def body(*refs):
        up_kernel(SEQ_LEN // TU, *refs)

    return call(
        body, "feed_up", total // TU, (scal,), in_specs, outs, out_specs, scratch,
        2 * total * d * (4 * half + 2 * width), total * (18 * d + 8 * half), args,
    )


def down_kernel(
    scal,
    cot, mid, n2_in, pre, ctx_a, ctx_b, wo_a, wo_b, wu_a, wu_b, wd_a, wd_b, gain,
    gmid_out, gctx_a, gctx_b, keep_own, keep_other, send_own, send_other,
    acc_own, acc_other, acc_small, wo_s, ctx_s, n2_t, gh_even, gh_odd, gpre, back_a, back_b,
):
    i = pl.program_id(0)
    clear(i, acc_own, acc_other, acc_small)
    width = ctx_a.shape[1]

    @pl.when(i == 0)
    def _():
        wo_s[:width, :] = wo_a[...]
        wo_s[width:, :] = wo_b[...]

    rows = cot.shape[0]
    ctx_s[:, :width] = ctx_a[...]
    ctx_s[:, width:] = ctx_b[...]
    n2_t[:-ONES, :] = n2_in[...].T
    n2_t[-ONES:, :] = jnp.ones((ONES, rows), BF16)
    half = wu_a.shape[1]
    chunks = [(part, c) for part in range(2) for c in range(half // FB)]
    ghs = (gh_even, gh_odd)

    def up(n):
        part, c = chunks[n]
        ghs[n % 2][...] = dot_nt(cot[...], (wd_a, wd_b)[part][c * FB : (c + 1) * FB, :]).astype(BF16)

    def vector(n):
        part, c = chunks[n]
        ts = slice(part * half + c * FB, part * half + (c + 1) * FB)
        for sub in subs(rows):
            z = pre[sub, ts]
            k = z * z * GELU_K
            t = jnp.tanh(z * (k + 1.0))
            slope = (t + 1.0) * ((z * (k * 1.5 + 0.5)) * (1.0 - t) + 0.5)
            gpre[sub, ts] = slope * ghs[n % 2][sub, :]

    def use(n):
        part, c = chunks[n]
        ts = slice(part * half + c * FB, part * half + (c + 1) * FB)
        (acc_own, acc_other)[part][:, c * FB : (c + 1) * FB] += dot_nn(n2_t[...], gpre[:, ts])

    up(0)
    for n in range(len(chunks)):
        if n + 1 < len(chunks):
            up(n + 1)
        if n:
            use(n - 1)
        vector(n)
    use(len(chunks) - 1)
    sums = [jnp.zeros((8, cot.shape[1]), F32) for _ in range(4)]
    side = cot.shape[1] // 2
    parts = [slice(k * rows // TAIL, (k + 1) * rows // TAIL) for k in range(TAIL)]

    def back(at):
        back_a[at, :] = dot_nt(gpre[at, :half], wu_a[...])
        back_b[at, :] = dot_nt(gpre[at, half:], wu_b[...])

    back(parts[0])
    for k, at in enumerate(parts):
        if k + 1 < TAIL:
            back(parts[k + 1])
        for r in range(at.start, at.stop, SUB):
            sub = slice(r, r + SUB)
            gn2 = back_a[sub, :] + back_b[sub, :]
            nn, r_std = normalize(mid[sub, :])
            gnn = gn2 * nn
            u = gn2 * gain[...]
            mean_un = jnp.mean(gnn * gain[...], axis=-1, keepdims=True)
            g = cot[sub, :].astype(F32)
            gm = g + r_std * (u - jnp.mean(u, axis=-1, keepdims=True) - nn * mean_un)
            gmid_out[sub, :] = gm.astype(BF16)
            for q, term in enumerate((gnn, gn2, gm, g)):
                sums[q] += fold_rows(term)
        gctx = dot_nt(gmid_out[at, :], wo_s[...])
        gctx_a[at, :] = gctx[:, :width].astype(BF16)
        gctx_b[at, :] = gctx[:, width:].astype(BF16)
    both = dot_tn(ctx_s[...], gmid_out[...])
    for acc, part in ((acc_own, both[:width]), (acc_other, both[width:])):
        acc[:width, half : half + side] += part[:, :side]
        acc[width : 2 * width, half : half + side] += part[:, side:]
    for k in range(4):
        acc_small[8 * k : 8 * k + 8, :] += sums[k]

    @pl.when(i == pl.num_programs(0) - 1)
    def _():
        vectors = [jnp.sum(acc_small[8 * k : 8 * k + 8, :], axis=0, keepdims=True) for k in range(4)]
        d = cot.shape[1]
        for acc, keep, send in ((acc_own, keep_own, send_own), (acc_other, keep_other, send_other)):
            mine = acc[d : d + 1, :half]
            put_vectors(acc, half + side, vectors + [mine[:, :d], mine[:, d:]])
            put_blocks(scal[0], [keep, send], acc, slice(None))


def down_block(scal, cot, mid, n2, pre, ctx_a, ctx_b, wo, wu, wd, gain):
    total, d = cot.shape
    width = ctx_a.shape[1]
    half = wu[0].shape[1]
    args = (cot, mid, n2, pre, ctx_a, ctx_b, *wo, *wu, *wd, gain)
    in_specs = [rows_spec(TB, d), rows_spec(TB, d), rows_spec(TB, d), rows_spec(TB, 2 * half)]
    in_specs += [rows_spec(TB, width), rows_spec(TB, width)]
    in_specs += [const_spec(a.shape) for a in args[6:]]
    columns = half + d // 2 + EXTRA
    pack = (BLOCKS // 2, d // BLOCKS, columns)
    outs = [((total, d), BF16), ((total, width), BF16), ((total, width), BF16), *[(pack, BF16)] * 4]
    out_specs = [rows_spec(TB, d), rows_spec(TB, width), rows_spec(TB, width)]
    out_specs += [const_spec(s) for s, _ in outs[3:]]
    scratch = [
        pltpu.VMEM((d + ONES, columns), F32), pltpu.VMEM((d + ONES, columns), F32),
        pltpu.VMEM((32, d), F32), pltpu.VMEM((2 * width, d), BF16), pltpu.VMEM((TB, 2 * width), BF16),
        pltpu.VMEM((d + ONES, TB), BF16),
        pltpu.VMEM((TB, FB), BF16), pltpu.VMEM((TB, FB), BF16), pltpu.VMEM((TB, 2 * half), BF16),
        pltpu.VMEM((TB, d), F32), pltpu.VMEM((TB, d), F32),
    ]
    return call(
        down_kernel, "feed_back", total // TB, (scal,), in_specs, outs, out_specs, scratch,
        2 * total * d * (6 * half + 4 * width), total * (16 * d + 4 * half), args,
    )


def out_rows(mid, hidden, wd_a, wd_b, bd, out):
    half = wd_a.shape[0]
    out[...] = (
        mid[...] + dot_nn(hidden[:, :half], wd_a[...]) + dot_nn(hidden[:, half:], wd_b[...]) + bd[...]
    ).astype(BF16)


def out_kernel(scal, mid, hidden, wd_a, wd_b, bd, *refs):
    out_rows(mid, hidden, wd_a, wd_b, bd, refs[-1])


def out_down_kernel(scal, mid, hidden, wd_a, wd_b, bd, before, d0, d1, out, down, d_all):
    out_rows(mid, hidden, wd_a, wd_b, bd, out)

    @pl.when(pl.program_id(0) == 0)
    def _():
        place(scal[0], (d0, d1), d_all, BF16)
        down[...] = d_all[...].T.astype(F32)


def part_spec(first, cols):
    return pl.BlockSpec((TM, cols), lambda i, *_: (i + first, 0))


def out_block(first, tiles, scal, mid, hidden, wd, bd, before, pieces=()):
    total, d = mid.shape
    args = (mid, hidden, *wd, bd)
    specs = [part_spec(first, d), part_spec(first, hidden.shape[1])]
    specs += [const_spec(a.shape) for a in (*wd, bd)]
    alias = {}
    if before is not None:
        alias = {len(args) + 1: 0}
        args += (before,)
        specs += [pl.BlockSpec(memory_space=pl.ANY)]
    outs, out_specs, scratch = [((total, d), BF16)], [part_spec(first, d)], []
    if pieces:
        args += tuple(pieces)
        specs += [const_spec(p.shape) for p in pieces]
        shape = (pieces[0].shape[2], d)
        outs += [(shape, F32)]
        out_specs += [const_spec(shape)]
        scratch = [pltpu.VMEM(shape[::-1], BF16)]
    return call(
        out_down_kernel if pieces else out_kernel, "layer_out", tiles, (scal,), specs, outs, out_specs, scratch,
        2 * tiles * TM * d * hidden.shape[1], tiles * TM * (6 * d + 2 * hidden.shape[1]), args, alias,
    )


def attend_back_kernel(
    heads, scal, nn, proj, probs, gctx, w, gain, shift, gproj, pack_keep, pack_send, kpad, vpad, dk, dv, acc, acc_b, gprob, gscore
):
    s = pl.program_id(0)
    clear(s, acc, acc_b)
    width = heads * HEAD_DIM
    edge = jnp.zeros((MARGIN, width), BF16)
    for pad, j in ((kpad, 1), (vpad, 2)):
        pad[0:MARGIN, :] = edge
        pad[MARGIN + SEQ_LEN :, :] = edge
        pad[MARGIN : MARGIN + SEQ_LEN, :] = proj[:, j * width : (j + 1) * width]
    mask = head_mask(1.0, heads)
    dk[0 : 2 * MARGIN, :] = jnp.zeros((2 * MARGIN, width), F32)
    dv[0 : 2 * MARGIN, :] = jnp.zeros((2 * MARGIN, width), F32)
    scale = HEAD_DIM**-0.5

    def rows(b):
        return slice(b * QB, (b + 1) * QB)

    def keys(b):
        return slice(b * QB, b * QB + WIN)

    def own(b):
        return slice(b * WIN, (b + 1) * WIN)

    for b in range(NBLK):
        gprob[own(b), :] = dot_nt(vpad[keys(b), :], spread(gctx[rows(b), :], mask, heads))
    for b in range(NBLK):
        p = probs[own(b), :].astype(F32)
        gp = gprob[own(b), :]
        gscore[own(b), :] = (p * (gp - jnp.sum(p * gp, axis=0, keepdims=True))).astype(BF16)
    for b in range(NBLK):
        gproj[rows(b), 0:width] = (pair_rows(gscore[own(b), :], kpad[keys(b), :], heads) * scale).astype(BF16)
    for b in range(NBLK):
        key_term = dot_nn(gscore[own(b), :], spread(proj[rows(b), 0:width], mask, heads)) * scale
        value_term = dot_nn(probs[own(b), :], spread(gctx[rows(b), :], mask, heads))
        for total, term in ((dk, key_term), (dv, value_term)):
            total[b * QB : b * QB + 2 * MARGIN, :] += term[: 2 * MARGIN]
            total[b * QB + 2 * MARGIN : b * QB + WIN, :] = term[2 * MARGIN :]
    gproj[:, width : 2 * width] = dk[MARGIN : MARGIN + SEQ_LEN, :].astype(BF16)
    gproj[:, 2 * width :] = dv[MARGIN : MARGIN + SEQ_LEN, :].astype(BF16)
    gp_all = gproj[...]
    acc[:, : 3 * width] += dot_tn(nn[...], gp_all)
    acc_b[...] += jnp.sum(gp_all.astype(F32), axis=0, keepdims=True)

    @pl.when(s == pl.num_programs(0) - 1)
    def _():
        d = acc.shape[0]
        column = lambda v: jnp.broadcast_to(v[...], (EXTRA, d)).T[:, 0:1]
        gain_col, shift_col = column(gain), column(shift)
        gain_grad, shift_grad = jnp.zeros((d, 1), F32), jnp.zeros((d, 1), F32)
        for j in range(3):
            at = slice(j * width, (j + 1) * width)
            weight = w[j].astype(F32)
            gain_grad += jnp.sum(weight * acc[:, at], axis=1, keepdims=True)
            shift_grad += jnp.sum(weight * acc_b[:, at], axis=1, keepdims=True)
            acc[:, at] = gain_col * acc[:, at] + shift_col * acc_b[:, at]
        put_vectors(acc, 3 * width, [jnp.concatenate([acc_b[:, :width], acc_b[:, 2 * width :]], axis=1)])
        lane = lax.broadcasted_iota(jnp.int32, (d, EXTRA), 1)
        extra = jnp.where(lane == 1, gain_grad, acc[:, 3 * width :])
        acc[:, 3 * width :] = jnp.where(lane == 2, shift_grad, extra)
        put_blocks(scal[1], [pack_keep, pack_send], acc, slice(None))


def attention_backward(scal, nn, proj, probs, gctx, w, gain, shift):
    total, d = nn.shape
    seqs = total // SEQ_LEN
    width = gctx.shape[1]
    heads = width // HEAD_DIM

    def body(*refs):
        attend_back_kernel(heads, *refs)

    pad = SEQ_LEN + 2 * MARGIN
    columns = 3 * width + EXTRA
    pack = (BLOCKS // 2, d // BLOCKS, columns)
    return call(
        body, "attend_back", seqs, (scal,),
        [
            rows_spec(SEQ_LEN, d), rows_spec(SEQ_LEN, 3 * width),
            rows_spec(NBLK * WIN, heads * QB), rows_spec(SEQ_LEN, width),
            const_spec(w.shape), const_spec(gain.shape), const_spec(shift.shape),
        ],
        [((total, 3 * width), BF16), (pack, BF16), (pack, BF16)],
        [rows_spec(SEQ_LEN, 3 * width), const_spec(pack), const_spec(pack)],
        [
            pltpu.VMEM((pad, width), BF16), pltpu.VMEM((pad, width), BF16),
            pltpu.VMEM((pad, width), F32), pltpu.VMEM((pad, width), F32),
            pltpu.VMEM((d, columns), F32), pltpu.VMEM((1, 3 * width), F32),
            pltpu.VMEM((NBLK * WIN, heads * QB), F32), pltpu.VMEM((NBLK * WIN, heads * QB), BF16),
        ],
        2 * total * d * 3 * width + 16 * total * WIN * width, total * (d + 9 * width) * 2,
        (nn, proj, probs, gctx, w, gain, shift),
    )


def last_kernel(per_seq, first, scal, x, gmid, gp_a, gp_b, w_a, w_b, gain, *refs):
    gin, back_a, back_b, side_a, side_b = refs[-5:]
    i = pl.program_id(0)
    side_by_side(i, w_a, side_a)
    side_by_side(i, w_b, side_b)
    rows = x.shape[0]
    tile = i + first
    back_a[...] = dot_nt(gp_a[...], side_a[...])
    back_b[...] = dot_nt(gp_b[...], side_b[...])
    for sub in subs(rows):
        keep = keep_of((SUB, x.shape[1]), (tile % per_seq) * rows + sub.start, tile // per_seq, scal)
        nn, r = normalize(x[sub, :].astype(F32) * keep)
        u = (back_a[sub, :] + back_b[sub, :]) * gain[...]
        mean_un = jnp.mean(u * nn, axis=-1, keepdims=True)
        a = r * (u - jnp.mean(u, axis=-1, keepdims=True) - nn * mean_un)
        gin[sub, :] = (gmid[sub, :].astype(F32) + a) * keep


def last_block(part, parts, scal, x, gmid, gp_a, gp_b, w_a, w_b, gain, before):
    total, d = x.shape
    tiles = total // TM // parts

    def body(*refs):
        last_kernel(SEQ_LEN // TM, part * tiles, *refs)

    width = gp_a.shape[1]
    args = (x, gmid, gp_a, gp_b, w_a, w_b, gain)
    specs = [part_spec(part * tiles, c) for c in (d, d, width, width)]
    specs += [const_spec(a.shape) for a in args[4:]]
    alias = {}
    if before is not None:
        alias = {len(args) + 1: 0}
        args += (before,)
        specs += [pl.BlockSpec(memory_space=pl.ANY)]
    return call(
        body, "input_gradient", tiles, (scal,), specs, [((total, d), F32)], [part_spec(part * tiles, d)],
        [pltpu.VMEM((TM, d), F32)] * 2 + [pltpu.VMEM((d, width), BF16)] * 2,
        4 * tiles * TM * d * width, tiles * TM * (10 * d + 4 * width), args, alias,
    )[0]


def place(me, pieces, out, kind, columns=slice(None)):
    each = pieces[0].shape[0]
    rows = pieces[0].shape[1]
    for j in range(BLOCKS):
        at = pl.ds(pl.multiple_of((j ^ me) * rows, rows), rows)
        out[at, :] = pieces[j // each][j % each, :, columns].astype(kind)


def unpack_kernel(scal, u0, u1, q0, q1, up, out, *refs):
    vectors, (bias_up, qkv, bias_q, gain, shift, u_side, q_all) = refs[:4], refs[4:]
    me = scal[0]
    half, side = up.shape[1], out.shape[1] // 2
    rows = out.shape[0]
    place(me, (u0, u1), up, F32, slice(0, half))
    place(me, (u0, u1), u_side, F32, slice(half, u0.shape[2]))
    out[:, :side] = u_side[:rows, :side]
    out[:, side:] = u_side[rows:, :side]
    sums = u_side[:, side:].T
    for k in range(4):
        vectors[k][...] = sums[k : k + 1, :]
    bias_up[...] = jnp.concatenate([sums[4:5, :], sums[5:6, :]], axis=1)
    place(scal[1], (q0, q1), q_all, F32)
    width = qkv.shape[2]
    for j in range(3):
        qkv[j] = q_all[:, j * width : (j + 1) * width]
    sums = q_all[:, 3 * width :].T
    bias_q[...] = jnp.concatenate([sums[0:1, :width], sums[0:1, width:]], axis=0)
    gain[...] = sums[1:2, :]
    shift[...] = sums[2:3, :]


def unpack(scal, pieces, up, out, qkv):
    d = up[0]
    shapes = [up, out, *[(1, d)] * 4, (1, up[1]), qkv, (2, qkv[2]), (1, d), (1, d)]
    natural = [(d, pieces[0].shape[2] - up[1]), (d, pieces[2].shape[2])]
    return call(
        unpack_kernel, "unpack", 1, (scal,), [const_spec(p.shape) for p in pieces], [(s, F32) for s in shapes],
        [const_spec(s) for s in shapes], [pltpu.VMEM(s, F32) for s in natural], 0,
        6 * sum(p.size for p in pieces), tuple(pieces),
    )


def make_body(mesh):
    tp = mesh.shape["tensor"]
    dp = mesh.shape["dp"]
    paired = tp == 2 and dp == BLOCKS

    def across(v):
        return lax.ppermute(v, "tensor", [(0, 1), (1, 0)])

    def swap(v, distance):
        return lax.ppermute(v, "dp", [(i, i ^ distance) for i in range(dp)])

    def core(v):
        return swap(v, 1)

    def diagonal(v):
        pairs = [(2 * i + j, 2 * (i ^ 8) + 1 - j) for i in range(dp) for j in range(2)]
        return lax.ppermute(v, ("dp", "tensor"), pairs)

    def plus(first, *rest):
        total = first.astype(F32)
        for v in rest:
            total = total + v.astype(F32)
        return total.astype(first.dtype)

    def lower(v):
        return v[: v.shape[0] // 2]

    def upper(v):
        return v[v.shape[0] // 2 :]

    def join(a, b):
        return jnp.concatenate([a, b], axis=0)

    def window(kernel, args, moves):
        args, sent = lax.optimization_barrier((args, [v for v, _ in moves]))
        arrived = [move(v) for v, (_, move) in zip(sent, moves)]
        return lax.optimization_barrier((kernel(*args), arrived, sent))

    def body(
        inputs, cotangent, lengths, time_span, freq_span, gain_one, shift_one, qkv_weight, qkv_bias,
        out_weight, out_bias, gain_two, shift_two, up_weight, up_bias, down_weight, down_bias,
    ):
        total, d = inputs.shape
        seqs = total // SEQ_LEN
        here = lax.axis_index("tensor") * seqs
        index = lax.axis_index("dp")
        label = label_q = jnp.int32(0)
        if paired:
            label = ((index & 1) << 3) | ((index & 2) << 1) | ((index & 4) >> 1)
            label_q = ((index & 1) << 3) | (index & 4)
        place_here = jnp.stack([label, label_q, here]).astype(jnp.int32)
        ends = [span[:, k] for span in (time_span, freq_span) for k in range(2)]
        scal = jnp.concatenate([place_here, lengths, *ends])
        row = lambda v: v.reshape(1, -1)
        stack_biases = lambda b, u: jnp.concatenate([b, u.reshape(-1, b.shape[1])], axis=0)

        def attend_a(rows, w, bias):
            return attention_forward(True, scal, rows, w, bias, row(gain_one), row(shift_one))

        def attend_b(rows, w, bias):
            return attention_forward(False, scal, rows, w, bias, None, None)

        def up(ctx_a, ctx_b, wo, wu, biases):
            return up_block(
                scal, inputs, cotangent, ctx_a, ctx_b, wo, wu, row(out_bias), row(gain_two), row(shift_two), biases
            )

        def down(mid, n2, pre, ctx_a, ctx_b, wo, wu, wd):
            return down_block(scal, cotangent, mid, n2, pre, ctx_a, ctx_b, wo, wu, wd, row(gain_two))

        def back(nn, proj, probs, gctx, w):
            return attention_backward(scal, nn, proj, probs, gctx, w, row(gain_one), row(shift_one))

        def last(part, parts):
            return lambda gmid, gp_a, gp_b, w_a, w_b, before: last_block(
                part, parts, scal, inputs, gmid, gp_a, gp_b, w_a, w_b, row(gain_one), before
            )

        def out(first, tiles):
            return lambda mid, hidden, wd, before, *pieces: out_block(
                first, tiles, scal, mid, hidden, wd, row(down_bias), before, pieces
            )

        turned = lambda w: jnp.transpose(w, (1, 0, 2))
        if paired:
            odd = index & 1

            def part_of(v):
                rows = v.shape[0] // 2
                return lax.dynamic_slice_in_dim(v, odd * rows, rows, 0)

            def whole(mine, theirs):
                return jnp.concatenate([jnp.where(odd == 0, mine, theirs), jnp.where(odd == 0, theirs, mine)], axis=0)

            biases = stack_biases(qkv_bias, up_bias)
            qkv_a = turned(qkv_weight)
            qkv_rows = qkv_a.reshape(-1, qkv_a.shape[2])
            (nn, n1, proj_a, ctx_a, probs_a), (qkv_half, out_half, biases_b), _ = window(
                attend_a, (inputs, qkv_a, biases),
                [(part_of(qkv_rows), across), (part_of(out_weight), across), (biases, across)],
            )
            qkv_b = whole(qkv_half, core(qkv_half)).reshape(qkv_a.shape)
            (proj_b, ctx_b, probs_b), (up_half, out_theirs), (_, out_half) = window(
                attend_b, (n1, qkv_b, biases_b), [(part_of(up_weight), across), (out_half, core)]
            )
            wo = (out_weight, whole(out_half, out_theirs))
            wu = (up_weight, whole(up_half, core(up_half)))
            (mid, n2, hidden, pre, d_own, d_other), (down_b,), _ = window(
                up, (ctx_a, ctx_b, wo, wu, (biases, biases_b)), [(down_weight, across)]
            )
            wd = (down_weight, down_b)
            (gmid, gctx_a, gctx_b, u_own, u_other, u_send_own, u_send_other), (d_cross,), _ = window(
                down, (mid, n2, pre, ctx_a, ctx_b, wo, wu, wd), [(d_other, across)]
            )
            u_other, u_own = plus(u_other, core(u_send_other)), plus(u_own, core(u_send_own))
            d_sum = plus(d_own, d_cross)
            d_sum = plus(lower(d_sum), core(upper(d_sum)))
            step = lambda distance: lambda v: swap(v, distance)
            (gproj_b, q_other, q_send), (u_cross, d_in), _ = window(
                back, (nn, proj_b, probs_b, gctx_b, qkv_b), [(u_other, across), (upper(d_sum), step(2))]
            )
            u_sum = plus(u_own, u_cross)
            d_sum = plus(lower(d_sum), d_in)
            q_other = plus(q_other, core(q_send))
            (gproj_a, q_own, q_send), (u_in, d_in, q_cross), _ = window(
                back, (nn, proj_a, probs_a, gctx_a, qkv_a),
                [(upper(u_sum), step(2)), (upper(d_sum), step(4)), (q_other, across)],
            )
            u_sum = plus(lower(u_sum), u_in)
            d_sum = plus(lower(d_sum), d_in)
            q_sum = plus(q_own, core(q_send), q_cross)
            input_grad, (u_in, d_in, q_in), _ = window(
                last(0, 2), (gmid, gproj_a, gproj_b, qkv_a, qkv_b, None),
                [(upper(u_sum), step(4)), (d_sum, step(8)), (q_sum, step(2))],
            )
            u_sum = plus(lower(u_sum), u_in)
            d_sum = plus(d_sum, d_in)
            q_sum = plus(q_sum, q_in)
            input_grad, (u_in, d_in, q_in), _ = window(
                last(1, 2), (gmid, gproj_a, gproj_b, qkv_a, qkv_b, input_grad),
                [(u_sum, step(8)), (d_sum, step(4)), (upper(q_sum), step(4))],
            )
            u_sum = plus(u_sum, u_in)
            d_sum = join(d_sum, d_in)
            q_sum = plus(lower(q_sum), q_in)
            third = q_sum.shape[2] - EXTRA
            q_sides = q_sum[:, :, third:]
            tiles = total // TM
            cuts = (0, tiles // 2, tiles * 3 // 4, tiles)
            (layer_out,), (u_in, d_in, q_in, q_side_y, q_side_d), _ = window(
                out(cuts[0], cuts[1] - cuts[0]), (mid, hidden, wd, None),
                [(u_sum, step(4)), (d_sum, step(2)), (q_sum, step(8)), (q_sides, across), (q_sides, diagonal)],
            )
            u_sum = join(u_sum, u_in)
            d_sum = join(d_sum, d_in)
            lane = lax.broadcasted_iota(jnp.int32, q_sides.shape, 2)
            f32 = lambda v: v.astype(F32)
            q_in_side = f32(q_in[:, :, third:])
            own = f32(q_sides) + q_in_side
            both = own + (f32(q_side_y) + f32(q_side_d))
            q_side = jnp.where((lane == 1) | (lane == 2), both, own).astype(BF16)
            q_sum = jnp.concatenate([plus(q_sum[:, :, :third], q_in[:, :, :third]), q_side], axis=2)
            (layer_out,), (u_in, d_in, q_in), _ = window(
                out(cuts[1], cuts[2] - cuts[1]), (mid, hidden, wd, layer_out),
                [(u_sum, step(2)), (d_sum, core), (q_sum, step(4))],
            )
            u_sum = join(u_sum, u_in)
            q_sum = join(q_sum, q_in)
            (layer_out, g_down), (u_in, q_in), _ = window(
                out(cuts[2], cuts[3] - cuts[2]), (mid, hidden, wd, layer_out, d_sum, d_in),
                [(u_sum, core), (q_sum, core)],
            )
            g_up, g_out, *shared_two, g_bu, g_qkv, g_qb, gain_grad, shift_grad = unpack(
                scal, (u_sum, u_in, q_sum, q_in), up_weight.shape, out_weight.shape, qkv_a.shape
            )
            g_qkv = turned(g_qkv)
            g_bu = g_bu.reshape(-1)
            shared_two = [v.reshape(-1) for v in shared_two]
            shared_one = [v.reshape(-1) for v in (gain_grad, shift_grad)]
        else:
            def halves(local, axis):
                return tuple(jnp.split(lax.all_gather(local, "tensor", axis=axis, tiled=True), 2, axis=axis))

            def sums(own, other, axis):
                whole = jnp.concatenate([own, other], axis=axis)
                part = lax.psum_scatter(whole, "tensor", scatter_dimension=axis, tiled=True)
                return lax.psum(part, "dp").astype(F32)

            natural = lambda *packs: jnp.concatenate(packs, axis=0).reshape(d, -1)
            qkv = [turned(w) for w in halves(qkv_weight, 2)]
            biases = [stack_biases(q, u) for q, u in zip(halves(qkv_bias, 1), halves(up_bias, 0))]
            wo, wu, wd = halves(out_weight, 0), halves(up_weight, 1), halves(down_weight, 0)
            nn, n1, proj_a, ctx_a, probs_a = attend_a(inputs, qkv[0], biases[0])
            proj_b, ctx_b, probs_b = attend_b(n1, qkv[1], biases[1])
            mid, n2, hidden, pre, d_own, d_other = up(ctx_a, ctx_b, wo, wu, biases)
            gmid, gctx_a, gctx_b, *u_packs = down(mid, n2, pre, ctx_a, ctx_b, wo, wu, wd)
            gproj_b, *q_other = back(nn, proj_b, probs_b, gctx_b, qkv[1])
            gproj_a, *q_own = back(nn, proj_a, probs_a, gctx_a, qkv[0])
            input_grad = last(0, 1)(gmid, gproj_a, gproj_b, *qkv, None)
            layer_out = out(0, total // TM)(mid, hidden, wd, None)[0]
            g_down = sums(natural(d_own), natural(d_other), 1).T
            u = natural(u_packs[0], u_packs[2]), natural(u_packs[1], u_packs[3])
            half, side = wu[0].shape[1], d // 2
            g_up = sums(u[0][:, :half], u[1][:, :half], 1)
            beside = [jnp.concatenate(jnp.split(v[:, half : half + side], 2, axis=0), axis=1) for v in u]
            g_out = sums(*beside, 0)
            q = natural(*q_own), natural(*q_other)
            wide = 3 * qkv[0].shape[2]
            g_qkv = sums(*[v[:, :wide].reshape(d, 3, -1) for v in q], 2)
            g_qb = sums(*[v[:, wide].reshape(2, -1) for v in q], 1)
            small_two = [v[:, half + side :].T for v in u]
            g_bu = sums(*[v[4:6].reshape(-1) for v in small_two], 0)
            shared_two = lax.psum(small_two[0][:4], ("dp", "tensor")).astype(F32)
            vectors = (q[0] + q[1])[:, wide + 1 : wide + 3].T
            shared_one = lax.psum(vectors, ("dp", "tensor")).astype(F32)
        return (
            layer_out, input_grad, shared_one[0], shared_one[1], g_qkv, g_qb, g_out, shared_two[2],
            shared_two[0], shared_two[1], g_up, g_bu, g_down, shared_two[3],
        )

    return body


def solution(mesh):
    in_specs = (
        P(("dp", "tensor"), None), P(("dp", "tensor"), None), P("dp"), P("dp", None), P("dp", None), P(), P(),
        P(None, None, "tensor"), P(None, "tensor"), P("tensor", None), P(), P(), P(), P(None, "tensor"),
        P("tensor"), P("tensor", None), P(),
    )
    out_specs = (
        P(("dp", "tensor"), None), P(("dp", "tensor"), None), P(), P(), P(None, None, "tensor"), P(None, "tensor"),
        P("tensor", None), P(), P(), P(), P(None, "tensor"), P("tensor"), P("tensor", None), P(),
    )
    return jax.shard_map(make_body(mesh), mesh=mesh, in_specs=in_specs, out_specs=out_specs, check_vma=False)
```

time: 285 us -> 249 us (0.87)
  local copies, waits for them, and re-layouts: 19.1 us -> 6.55 us
  Pallas kernels: 203 us -> 191 us
  other arithmetic: 11 us -> 5.69 us
  waiting for transfers between devices: 18.2 us -> 13.7 us
    pallas_call x13 -> x10, Pallas kernels: 178 us -> 166 us  [call(): pl.pallas_call(kernel, grid_spec=pltpu.PrefetchScalarGridSpec(num_scalar_...]
    ppermute x8 -> x9, waiting for transfers between devices: 9.44 us -> 2.53 us  [across(): return lax.ppermute(v, 'tensor', [(0, 1), (1, 0)])]
    ppermute x30 -> x25, starting transfers between devices: 22.8 us -> 18 us  [swap(): return lax.ppermute(v, 'dp', [(i, i ^ distance) for i in range(dp)])]
    optimization_barrier x4 -> x0, local copies, waits for them, and re-layouts: 4.38 us -> none  [window(): args, sent = lax.optimization_barrier((args, [v for v, _ in moves]))]
    unnamed x42 -> x34, local copies, waits for them, and re-layouts: 5.75 us -> 1.68 us
    slice x6 -> x1, local copies, waits for them, and re-layouts: 3.6 us -> 0.01 us  [body(): q_sides = q_sum[:, :, third:]]
    ppermute x30 -> x25, waiting for transfers between devices: 8.76 us -> 11.2 us  [swap(): return lax.ppermute(v, 'dp', [(i, i ^ distance) for i in range(dp)])]
    ppermute x8 -> x9, starting transfers between devices: 9.04 us -> 10.2 us  [across(): return lax.ppermute(v, 'tensor', [(0, 1), (1, 0)])]
  transfers between devices with their start and end apart: 38 -> 35, of which waited for: 8 -> 10; matrix products, arithmetic and copies ran while one was open for 5% -> 1% of each run, Pallas kernels for 71% -> 75%
where the time goes in v3:
time: 249 us; the launch traced here: 248 us
  Pallas kernels  191 us (77%)
  starting transfers between devices  29.7 us (12%)
  waiting for transfers between devices  13.7 us (6%)
  local copies, waits for them, and re-layouts  6.55 us (3%)
  other arithmetic  5.69 us (2%)
    pallas_call x10, Pallas kernels, call(): pl.pallas_call(kernel, grid_spec=pltpu.PrefetchScalarGridSpec(num_scalar_...  166 us
    pallas_call x2, Pallas kernels, attention_forward(): pl.pallas_call(body, grid_spec=pltpu.PrefetchScalarGridSpec(num_scalar_pr...  24.9 us
    ppermute x25, starting transfers between devices, swap(): return lax.ppermute(v, 'dp', [(i, i ^ distance) for i in range(dp)])  18 us
    ppermute x25, waiting for transfers between devices, swap(): return lax.ppermute(v, 'dp', [(i, i ^ distance) for i in range(dp)])  11.2 us
    ppermute x9, starting transfers between devices, across(): return lax.ppermute(v, 'tensor', [(0, 1), (1, 0)])  10.2 us
  transfers between devices with their start and end apart: 35, of which 10 were waited for; matrix products, arithmetic and copies ran while one was open for 1% of the time, Pallas kernels for 75%

profile of v3, /device:TPU:0, one launch (start us, length us, event | category | flops | bytes accessed | tf_op | source)
XLA Modules:
  0.0 248.2 jit_solution(12993669460082680887)
XLA Ops:
  4.0 3.0 %collective-permute-start = (bf16[768,256]{1,0:T(8,128)(2,1)S(1)}, bf16[768,256]{1,0:T(8,128)(2,1)S(1)}, u32[]{:S(2)}, u32[]{:S(2)}) collective-permute-start(bf16[768,256]{1,0:T(8,128)(2,1)S(1)} %constant_dynamic-slice_fusion.2), channel_id=1, source_target_pairs={{0,1},{1,0},{2,3},{3,2},{4,5},{5,4},{6,7},{7,6},{8,9},{9,8},{10,11... | collective-permute-start | bytes 1179656 | tf_op jit(solution)/shard_map/ppermute | solution.py:709
  7.0 2.0 collective-permute-start.2
  11.0 13.6 %attend_first.1 = (bf16[4096,512]{1,0:T(8,128)(2,1)}, bf16[4096,512]{1,0:T(8,128)(2,1)}, bf16[4096,768]{1,0:T(8,128)(2,1)}, bf16[4096,256]{1,0:T(8,128)(2,1)}, bf16[6144,256]{1,0:T(8,128)(2,1)}) custom-call(s32[43]{0:T(128)} %concatenate.35.refs_0_.scal, bf16[4096,512]{1,0:T(8,128)(2,1)} %refs_1_.6, bf16[3,512,256]{2,1,0:T(8,128)(2,1)} %bitcast.34, ...), custom_call_target="tpu_custom_call" | custom-call | flops 4026531840 | bytes 16777216 | tf_op jit(solution)/shard_map/attend_first/pallas_call | solution.py:190
  24.8 1.6 collective-permute-done.3
  27.6 11.3 %attend_second.1 = (bf16[4096,768]{1,0:T(8,128)(2,1)}, bf16[4096,256]{1,0:T(8,128)(2,1)}, bf16[6144,256]{1,0:T(8,128)(2,1)}) custom-call(s32[43]{0:T(128)} %concatenate.35.refs_0_.scal, bf16[4096,512]{1,0:T(8,128)(2,1)} %get-tuple-element.222.refs_1_, bf16[3,512,256]{2,1,0:T(8,128)(2,1)} %bitcast.29, f32[6,256]{1,0:T(8,128)} %copy-done.16), custom_call_target="tpu_custom_call" | custom-call | flops 4026531840 | bytes 16777216 | tf_op jit(solution)/shard_map/attend_second/pallas_call | solution.py:190
  38.9 2.5 %collective-permute-done.4 = bf16[256,1024]{1,0:T(8,128)(2,1)S(1)} collective-permute-done((bf16[256,1024]{1,0:T(8,128)(2,1)S(1)}, bf16[256,1024]{1,0:T(8,128)(2,1)S(1)}, u32[]{:S(2)}, u32[]{:S(2)}) %collective-permute-start.4) | collective-permute-done | bytes 524320 | tf_op jit(solution)/shard_map/ppermute | solution.py:709
  44.7 35.5 %feed_up.1 = (f32[4096,512]{1,0:T(8,128)}, bf16[4096,512]{1,0:T(8,128)(2,1)}, bf16[4096,2048]{1,0:T(8,128)(2,1)}, bf16[4096,2048]{1,0:T(8,128)(2,1)}, bf16[16,32...) custom-call(s32[43]{0:T(128)} %concatenate.35.refs_0_.scal, bf16[4096,512]{1,0:T(8,128)(2,1)} %refs_1_.6, ...), custom_call_target="tpu_custom_call" | custom-call | flops 19327352832 | bytes 71303168 | tf_op jit(solution)/shard_map/feed_up/pallas_call | solution.py:313
  80.2 1.8 collective-permute-start.8
  82.0 45.2 %feed_back.1 = (bf16[4096,512]{1,0:T(8,128)(2,1)}, bf16[4096,256]{1,0:T(8,128)(2,1)}, bf16[4096,256]{1,0:T(8,128)(2,1)}, bf16[8,32,1408]{2,1,0:T(8,128)(2,1)}, b...) custom-call(s32[43]{0:T(128)} %concatenate.35.refs_0_.scal, ...), custom_call_target="tpu_custom_call" | custom-call | flops 30064771072 | bytes 50331648 | tf_op jit(solution)/shard_map/feed_back/pallas_call | solution.py:313
  133.5 17.7 %attend_back.2 = (bf16[4096,768]{1,0:T(8,128)(2,1)}, bf16[8,32,896]{2,1,0:T(8,128)(2,1)}, bf16[8,32,896]{2,1,0:T(8,128)(2,1)}) custom-call(s32[43]{0:T(128)} %concatenate.35.refs_0_.scal, bf16[4096,512]{1,0:T(8,128)(2,1)} %get-tuple-element.301.refs_1_, bf16[4096,768]{1,0:T(8,128)(2,1)} %get-tuple-element.285.refs_2_, ...), custom_call_target="tpu_custom_call" | custom-call | flops 4831838208 | bytes 23068672 | tf_op jit(solution)/shard_map/attend_back/pallas_call | solution.py:313
  155.1 1.6 collective-permute-start.16
  156.6 17.9 %attend_back.3 = (bf16[4096,768]{1,0:T(8,128)(2,1)}, bf16[8,32,896]{2,1,0:T(8,128)(2,1)}, bf16[8,32,896]{2,1,0:T(8,128)(2,1)}) custom-call(s32[43]{0:T(128)} %concatenate.35.refs_0_.scal, bf16[4096,512]{1,0:T(8,128)(2,1)} %get-tuple-element.301.refs_1_, bf16[4096,768]{1,0:T(8,128)(2,1)} %get-tuple-element.302.refs_2_, ...), custom_call_target="tpu_custom_call" | custom-call | flops 4831838208 | bytes 23068672 | tf_op jit(solution)/shard_map/attend_back/pallas_call | solution.py:313
  174.8 1.9 collective-permute-done.18
  178.8 2.6 %collective-permute-start.20 = (bf16[2,32,1024]{2,1,0:T(8,128)(2,1)S(1)}, bf16[2,32,1024]{2,1,0:T(8,128)(2,1)S(1)}, u32[]{:S(2)}, u32[]{:S(2)}) collective-permute-start(bf16[2,32,1024]{2,1,0:T(8,128)(2,1)S(1)} %add_convert_fusion.15), channel_id=1, source_target_pairs={{0,16},{2,18},{4,20},{6,22},{8,24},{10,26},{12,28},{14,30},{16,0},... | collective-permute-start | bytes 393224 | tf_op jit(solution)/shard_map/ppermute | solution.py:712
  181.4 10.5 %input_gradient.2.refs_8_ = f32[4096,512]{1,0:T(8,128)} custom-call(s32[43]{0:T(128)} %concatenate.35.refs_0_.scal, bf16[4096,512]{1,0:T(8,128)(2,1)} %refs_1_.6, bf16[4096,512]{1,0:T(8,128)(2,1)} %get-tuple-element.332.refs_2_, bf16[4096,768]{1,0:T(8,128)(2,1)} %get-tuple-element.333.refs_3_, bf16[4096,768]{1,0:T(8,128)(2,1)} %get-tuple-element.334.refs_4_, ...), custom_call_target="tpu_custom_call" | custom-call | flops 3221225472 | bytes 16777216 | tf_op jit(solution)/shard_map/input_gradient/pallas_call | solution.py:313
  192.2 1.6 collective-permute-start.24
  194.6 10.5 %input_gradient.3 = f32[4096,512]{1,0:T(8,128)} custom-call(s32[43]{0:T(128)} %concatenate.35.refs_0_.scal, bf16[4096,512]{1,0:T(8,128)(2,1)} %refs_1_.6, bf16[4096,512]{1,0:T(8,128)(2,1)} %get-tuple-element.332.refs_2_, bf16[4096,768]{1,0:T(8,128)(2,1)} %get-tuple-element.333.refs_3_, ...), custom_call_target="tpu_custom_call", output_to_operand_aliasing={{}: (8, {})} | custom-call | flops 3221225472 | bytes 16777216 | tf_op jit(solution)/shard_map/input_gradient/pallas_call | solution.py:313
  206.6 1.9 collective-permute-start.27
  208.5 1.6 collective-permute-start.25
  212.5 10.1 %layer_out.3.refs_0_ = bf16[4096,512]{1,0:T(8,128)(2,1)} custom-call(s32[43]{0:T(128)} %concatenate.35.refs_0_.scal, f32[4096,512]{1,0:T(8,128)} %get-tuple-element.371.mid, bf16[4096,2048]{1,0:T(8,128)(2,1)} %get-tuple-element.372.hidden, bf16[1024,512]{1,0:T(8,128)(2,1)} %wd_a.3, bf16[1024,512]{1,0:T(8,128)(2,1)} %copy-done.1, f32[1,512]{1,0:T(1,128)} %bitcast.38), custom_call_target="tpu_custom_call" | custom-call | flops 4294967296 | bytes 14680064 | tf_op jit(solution)/shard_map/layer_out/pallas_call | solution.py:313
  224.9 6.5 %layer_out.4.before = bf16[4096,512]{1,0:T(8,128)(2,1)} custom-call(s32[43]{0:T(128)} %concatenate.35.refs_0_.scal, f32[4096,512]{1,0:T(8,128)} %get-tuple-element.371.mid, bf16[4096,2048]{1,0:T(8,128)(2,1)} %get-tuple-element.372.hidden, bf16[1024,512]{1,0:T(8,128)(2,1)} %wd_a.3, bf16[1024,512]{1,0:T(8,128)(2,1)} %copy-done.1, ...), custom_call_target="tpu_custom_call", output_to_operand_aliasing={{}: (6, {})} | custom-call | flops 2147483648 | bytes 7340032 | tf_op jit(solution)/shard_map/layer_out/pallas_call | solution.py:313
  232.1 1.6 collective-permute-done.30
  234.5 7.9 %layer_out.5 = (bf16[4096,512]{1,0:T(8,128)(2,1)}, f32[1024,512]{1,0:T(8,128)}) custom-call(s32[43]{0:T(128)} %concatenate.35.refs_0_.scal, f32[4096,512]{1,0:T(8,128)} %get-tuple-element.371.mid, bf16[4096,2048]{1,0:T(8,128)(2,1)} %get-tuple-element.372.hidden, bf16[1024,512]{1,0:T(8,128)(2,1)} %wd_a.3, ...), custom_call_target="tpu_custom_call", output_to_operand_aliasing={{0}: (6, {})} | custom-call | flops 2147483648 | bytes 7340032 | tf_op jit(solution)/shard_map/layer_out/pallas_call | solution.py:313
  243.5 4.5 %unpack.1 = (f32[512,1024]{1,0:T(8,128)}, f32[256,512]{1,0:T(8,128)}, f32[1,512]{1,0:T(1,128)}, f32[1,512]{1,0:T(1,128)}, f32[1,512]{1,0:T(1,128)}, /*index=5*/f...) custom-call(s32[43]{0:T(128)} %concatenate.35.refs_0_.scal, ...), custom_call_target="tpu_custom_call" | custom-call | bytes 7077888 | tf_op jit(solution)/shard_map/unpack/pallas_call | solution.py:313
  (135 shorter events, 32.0 us)
Async XLA Ops:
  4.0 20.7 %collective-permute-start = (bf16[768,256]{1,0:T(8,128)(2,1)S(1)}, bf16[768,256]{1,0:T(8,128)(2,1)S(1)}, u32[]{:S(2)}, u32[]{:S(2)}) collective-permute-start(bf16[768,256]{1,0:T(8,128)(2,1)S(1)} %constant_dynamic-slice_fusion.2), channel_id=1, source_target_pairs={{0,1},{1,0},{2,3},{3,2},{4,5},{5,4},{6,7},{7,6},{8,9},{9,8},{10,11... | collective-permute-start | bytes 1179656 | tf_op jit(solution)/shard_map/ppermute | solution.py:709
  7.0 17.7 %collective-permute-start.1 = (bf16[128,512]{1,0:T(8,128)(2,1)S(1)}, bf16[128,512]{1,0:T(8,128)(2,1)S(1)}, u32[]{:S(2)}, u32[]{:S(2)}) collective-permute-start(bf16[128,512]{1,0:T(8,128)(2,1)S(1)} %constant_dynamic-slice_fusion.1), channel_id=1, source_target_pairs={{0,1},{1,0},{2,3},{3,2},{4,5},{5,4},{6,7},{7,6},{8,9},{9,8},{10,11... | collective-permute-start | bytes 393224 | tf_op jit(solution)/shard_map/ppermute | solution.py:709
  7.0 17.6 %collective-permute-start.2 = (f32[6,256]{1,0:T(8,128)S(1)}, f32[6,256]{1,0:T(8,128)S(1)}, u32[]{:S(2)}, u32[]{:S(2)}) collective-permute-start(f32[6,256]{1,0:T(8,128)S(1)} %pad_maximum_fusion.9.refs_3_.refs_12_), channel_id=1, source_target_pairs={{0,1},{1,0},{2,3},{3,2},{4,5},{5,4},{6,7},{7,6},{8,9},{9,8},{10,11... | collective-permute-start | bytes 18440 | tf_op jit(solution)/shard_map/ppermute | solution.py:709
  27.4 14.0 %collective-permute-start.4 = (bf16[256,1024]{1,0:T(8,128)(2,1)S(1)}, bf16[256,1024]{1,0:T(8,128)(2,1)S(1)}, u32[]{:S(2)}, u32[]{:S(2)}) collective-permute-start(bf16[256,1024]{1,0:T(8,128)(2,1)S(1)} %constant_dynamic-slice_fusion), channel_id=1, source_target_pairs={{0,1},{1,0},{2,3},{3,2},{4,5},{5,4},{6,7},{7,6},{8,9},{9,8},{10,11... | collective-permute-start | bytes 1572872 | tf_op jit(solution)/shard_map/ppermute | solution.py:709
  27.5 11.4 %collective-permute-start.5 = (bf16[128,512]{1,0:T(8,128)(2,1)S(1)}, bf16[128,512]{1,0:T(8,128)(2,1)S(1)}, u32[]{:S(2)}, u32[]{:S(2)}) collective-permute-start(bf16[128,512]{1,0:T(8,128)(2,1)S(1)} %collective-permute-done.1), channel_id=1, source_target_pairs={{0,2},{2,0},{4,6},{6,4},{8,10},{10,8},{12,14},{14,12},{16,18},{18,... | collective-permute-start | bytes 393224 | tf_op jit(solution)/shard_map/ppermute | solution.py:712
  44.4 35.8 %collective-permute-start.7 = (bf16[1024,512]{1,0:T(8,128)(2,1)S(1)}, bf16[1024,512]{1,0:T(8,128)(2,1)S(1)}, u32[]{:S(2)}, u32[]{:S(2)}) collective-permute-start(bf16[1024,512]{1,0:T(8,128)(2,1)S(1)} %copy-done), channel_id=1, source_target_pairs={{0,1},{1,0},{2,3},{3,2},{4,5},{5,4},{6,7},{7,6},{8,9},{9,8},{10,11... | collective-permute-start | bytes 3145736 | tf_op jit(solution)/shard_map/ppermute | solution.py:709
  80.2 47.1 %collective-permute-start.8 = (bf16[16,32,1024]{2,1,0:T(8,128)(2,1)}, bf16[16,32,1024]{2,1,0:T(8,128)(2,1)S(1)}, u32[]{:S(2)}, u32[]{:S(2)}) collective-permute-start(bf16[16,32,1024]{2,1,0:T(8,128)(2,1)} %get-tuple-element.273), channel_id=1, source_target_pairs={{0,1},{1,0},{2,3},{3,2},{4,5},{5,4},{6,7},{7,6},{8,9},{9,8},{10,11... | collective-permute-start | bytes 3145736 | tf_op jit(solution)/shard_map/ppermute | solution.py:709
  131.0 20.2 %collective-permute-start.12 = (bf16[8,32,1408]{2,1,0:T(8,128)(2,1)S(1)}, bf16[8,32,1408]{2,1,0:T(8,128)(2,1)S(1)}, u32[]{:S(2)}, u32[]{:S(2)}) collective-permute-start(bf16[8,32,1408]{2,1,0:T(8,128)(2,1)S(1)} %add_convert_fusion.2), channel_id=1, source_target_pairs={{0,1},{1,0},{2,3},{3,2},{4,5},{5,4},{6,7},{7,6},{8,9},{9,8},{10,11... | collective-permute-start | bytes 2162696 | tf_op jit(solution)/shard_map/ppermute | solution.py:709
  132.0 19.6 %collective-permute-start.9 = (bf16[8,32,1408]{2,1,0:T(8,128)(2,1)}, bf16[8,32,1408]{2,1,0:T(8,128)(2,1)S(1)}, u32[]{:S(2)}, u32[]{:S(2)}) collective-permute-start(bf16[8,32,1408]{2,1,0:T(8,128)(2,1)} %get-tuple-element.275), channel_id=1, source_target_pairs={{0,2},{2,0},{4,6},{6,4},{8,10},{10,8},{12,14},{14,12},{16,18},{18,... | collective-permute-start | bytes 2162696 | tf_op jit(solution)/shard_map/ppermute | solution.py:712
  132.0 19.2 %collective-permute-start.13 = (bf16[4,32,1024]{2,1,0:T(8,128)(2,1)S(1)}, bf16[4,32,1024]{2,1,0:T(8,128)(2,1)S(1)}, u32[]{:S(2)}, u32[]{:S(2)}) collective-permute-start(bf16[4,32,1024]{2,1,0:T(8,128)(2,1)S(1)} %slice.82), channel_id=1, source_target_pairs={{0,4},{2,6},{4,0},{6,2},{8,12},{10,14},{12,8},{14,10},{16,20},{18,... | collective-permute-start | bytes 786440 | tf_op jit(solution)/shard_map/ppermute | solution.py:712
  153.4 21.2 %collective-permute-start.17 = (bf16[8,32,896]{2,1,0:T(8,128)(2,1)S(1)}, bf16[8,32,896]{2,1,0:T(8,128)(2,1)S(1)}, u32[]{:S(2)}, u32[]{:S(2)}) collective-permute-start(bf16[8,32,896]{2,1,0:T(8,128)(2,1)S(1)} %add_convert_fusion.7), channel_id=1, source_target_pairs={{0,1},{1,0},{2,3},{3,2},{4,5},{5,4},{6,7},{7,6},{8,9},{9,8},{10,11... | collective-permute-start | bytes 1376264 | tf_op jit(solution)/shard_map/ppermute | solution.py:709
  154.5 20.0 %collective-permute-start.15 = (bf16[4,32,1408]{2,1,0:T(8,128)(2,1)S(1)}, bf16[4,32,1408]{2,1,0:T(8,128)(2,1)S(1)}, u32[]{:S(2)}, u32[]{:S(2)}) collective-permute-start(bf16[4,32,1408]{2,1,0:T(8,128)(2,1)S(1)} %slice.84), channel_id=1, source_target_pairs={{0,4},{2,6},{4,0},{6,2},{8,12},{10,14},{12,8},{14,10},{16,20},{18,... | collective-permute-start | bytes 1081352 | tf_op jit(solution)/shard_map/ppermute | solution.py:712
  155.1 19.5 %collective-permute-start.16 = (bf16[2,32,1024]{2,1,0:T(8,128)(2,1)S(1)}, bf16[2,32,1024]{2,1,0:T(8,128)(2,1)S(1)}, u32[]{:S(2)}, u32[]{:S(2)}) collective-permute-start(bf16[2,32,1024]{2,1,0:T(8,128)(2,1)S(1)} %slice.86), channel_id=1, source_target_pairs={{0,8},{2,10},{4,12},{6,14},{8,0},{10,2},{12,4},{14,6},{16,24},{18,... | collective-permute-start | bytes 393224 | tf_op jit(solution)/shard_map/ppermute | solution.py:712
  176.8 15.1 %collective-permute-start.21 = (bf16[8,32,896]{2,1,0:T(8,128)(2,1)S(1)}, bf16[8,32,896]{2,1,0:T(8,128)(2,1)S(1)}, u32[]{:S(2)}, u32[]{:S(2)}) collective-permute-start(bf16[8,32,896]{2,1,0:T(8,128)(2,1)S(1)} %add_convert_fusion.6), channel_id=1, source_target_pairs={{0,4},{2,6},{4,0},{6,2},{8,12},{10,14},{12,8},{14,10},{16,20},{18,... | collective-permute-start | bytes 1376264 | tf_op jit(solution)/shard_map/ppermute | solution.py:712
  178.4 13.5 %collective-permute-start.19 = (bf16[2,32,1408]{2,1,0:T(8,128)(2,1)S(1)}, bf16[2,32,1408]{2,1,0:T(8,128)(2,1)S(1)}, u32[]{:S(2)}, u32[]{:S(2)}) collective-permute-start(bf16[2,32,1408]{2,1,0:T(8,128)(2,1)S(1)} %slice.88), channel_id=1, source_target_pairs={{0,8},{2,10},{4,12},{6,14},{8,0},{10,2},{12,4},{14,6},{16,24},{18,... | collective-permute-start | bytes 540680 | tf_op jit(solution)/shard_map/ppermute | solution.py:712
  178.8 13.1 %collective-permute-start.20 = (bf16[2,32,1024]{2,1,0:T(8,128)(2,1)S(1)}, bf16[2,32,1024]{2,1,0:T(8,128)(2,1)S(1)}, u32[]{:S(2)}, u32[]{:S(2)}) collective-permute-start(bf16[2,32,1024]{2,1,0:T(8,128)(2,1)S(1)} %add_convert_fusion.15), channel_id=1, source_target_pairs={{0,16},{2,18},{4,20},{6,22},{8,24},{10,26},{12,28},{14,30},{16,0},... | collective-permute-start | bytes 393224 | tf_op jit(solution)/shard_map/ppermute | solution.py:712
  192.2 13.5 %collective-permute-start.24 = (bf16[4,32,896]{2,1,0:T(8,128)(2,1)S(1)}, bf16[4,32,896]{2,1,0:T(8,128)(2,1)S(1)}, u32[]{:S(2)}, u32[]{:S(2)}) collective-permute-start(bf16[4,32,896]{2,1,0:T(8,128)(2,1)S(1)} %slice.90), channel_id=1, source_target_pairs={{0,8},{2,10},{4,12},{6,14},{8,0},{10,2},{12,4},{14,6},{16,24},{18,... | collective-permute-start | bytes 688136 | tf_op jit(solution)/shard_map/ppermute | solution.py:712
  193.8 11.9 %collective-permute-start.22 = (bf16[2,32,1408]{2,1,0:T(8,128)(2,1)S(1)}, bf16[2,32,1408]{2,1,0:T(8,128)(2,1)S(1)}, u32[]{:S(2)}, u32[]{:S(2)}) collective-permute-start(bf16[2,32,1408]{2,1,0:T(8,128)(2,1)S(1)} %add_convert_fusion.13), channel_id=1, source_target_pairs={{0,16},{2,18},{4,20},{6,22},{8,24},{10,26},{12,28},{14,30},{16,0},... | collective-permute-start | bytes 540680 | tf_op jit(solution)/shard_map/ppermute | solution.py:712
  194.1 11.6 %collective-permute-start.23 = (bf16[2,32,1024]{2,1,0:T(8,128)(2,1)S(1)}, bf16[2,32,1024]{2,1,0:T(8,128)(2,1)S(1)}, u32[]{:S(2)}, u32[]{:S(2)}) collective-permute-start(bf16[2,32,1024]{2,1,0:T(8,128)(2,1)S(1)} %add_convert_fusion.14), channel_id=1, source_target_pairs={{0,8},{2,10},{4,12},{6,14},{8,0},{10,2},{12,4},{14,6},{16,24},{18,... | collective-permute-start | bytes 393224 | tf_op jit(solution)/shard_map/ppermute | solution.py:712
  205.9 16.7 %collective-permute-start.26 = (bf16[4,32,1024]{2,1,0:T(8,128)(2,1)S(1)}, bf16[4,32,1024]{2,1,0:T(8,128)(2,1)S(1)}, u32[]{:S(2)}, u32[]{:S(2)}) collective-permute-start(bf16[4,32,1024]{2,1,0:T(8,128)(2,1)S(1)} %pad_maximum_fusion.7), channel_id=1, source_target_pairs={{0,4},{2,6},{4,0},{6,2},{8,12},{10,14},{12,8},{14,10},{16,20},{18,... | collective-permute-start | bytes 786440 | tf_op jit(solution)/shard_map/ppermute | solution.py:712
  206.6 15.9 %collective-permute-start.27 = (bf16[4,32,896]{2,1,0:T(8,128)(2,1)S(1)}, bf16[4,32,896]{2,1,0:T(8,128)(2,1)S(1)}, u32[]{:S(2)}, u32[]{:S(2)}) collective-permute-start(bf16[4,32,896]{2,1,0:T(8,128)(2,1)S(1)} %add_convert_fusion.10), channel_id=1, source_target_pairs={{0,16},{2,18},{4,20},{6,22},{8,24},{10,26},{12,28},{14,30},{16,0},... | collective-permute-start | bytes 688136 | tf_op jit(solution)/shard_map/ppermute | solution.py:712
  208.5 14.0 %collective-permute-start.25 = (bf16[2,32,1408]{2,1,0:T(8,128)(2,1)S(1)}, bf16[2,32,1408]{2,1,0:T(8,128)(2,1)S(1)}, u32[]{:S(2)}, u32[]{:S(2)}) collective-permute-start(bf16[2,32,1408]{2,1,0:T(8,128)(2,1)S(1)} %add_convert_fusion.12), channel_id=1, source_target_pairs={{0,8},{2,10},{4,12},{6,14},{8,0},{10,2},{12,4},{14,6},{16,24},{18,... | collective-permute-start | bytes 540680 | tf_op jit(solution)/shard_map/ppermute | solution.py:712
  210.1 12.4 %collective-permute-start.28 = (bf16[4,32,128]{2,1,0:T(8,128)(2,1)S(1)}, bf16[4,32,128]{2,1,0:T(8,128)(2,1)S(1)}, u32[]{:S(2)}, u32[]{:S(2)}) collective-permute-start(bf16[4,32,128]{2,1,0:T(8,128)(2,1)S(1)} %slice.92), channel_id=1, source_target_pairs={{0,1},{1,0},{2,3},{3,2},{4,5},{5,4},{6,7},{7,6},{8,9},{9,8},{10,11... | collective-permute-start | bytes 98312 | tf_op jit(solution)/shard_map/ppermute | solution.py:709
  211.0 11.5 %collective-permute-start.29 = (bf16[4,32,128]{2,1,0:T(8,128)(2,1)S(1)}, bf16[4,32,128]{2,1,0:T(8,128)(2,1)S(1)}, u32[]{:S(2)}, u32[]{:S(2)}) collective-permute-start(bf16[4,32,128]{2,1,0:T(8,128)(2,1)S(1)} %slice.92), channel_id=1, source_target_pairs={{0,17},{1,16},{2,19},{3,18},{4,21},{5,20},{6,23},{7,22},{8,25},{9,... | collective-permute-start | bytes 98312 | tf_op jit(solution)/shard_map/ppermute | solution.py:719
  (28 other events, 190.7 us)

commit v4 on v3

--- a/solution.py
+++ b/solution.py
@@ -16,7 +16,6 @@
 EPS = 1e-05
 LN_ROWS = 256
 NEG = -1000000000.0
-VMEM = 60 * 1024 * 1024
 F32 = jnp.float32
 BF16 = jnp.bfloat16
 
@@ -34,12 +33,12 @@
 
 
 def length_of(scal, seq):
-    return scal[3 + scal[2] + seq]
+    return scal[4 + scal[2] + seq]
 
 
 def keep_of(shape, first_pos, seq, scal):
-    seqs = (scal.shape[0] - 3) // 5
-    ends = [scal[3 + k * seqs + scal[2] + seq] for k in range(1, 5)]
+    seqs = (scal.shape[0] - 4) // 5
+    ends = [scal[4 + k * seqs + scal[2] + seq] for k in range(1, 5)]
     pos = first_pos + lax.broadcasted_iota(jnp.int32, (shape[0], 1), 0)
     col = lax.broadcasted_iota(jnp.int32, (1, shape[1]), 1)
     rows = jnp.where((pos >= ends[0]) & (pos < ends[1]), 0.0, 1.0)
@@ -112,17 +111,20 @@
     proj[at, 2 * width :] = (value[:, 2 * width :] + bias[1:2, :]).astype(BF16)
 
 
-def side_by_side(i, w, w_side):
-    @pl.when(i == 0)
+def parts_in_order(scal, mine, theirs):
+    odd = jnp.where(scal[3] == 0, 0, 1)
+    return ((mine, odd), (theirs, 1 - odd))
+
+
+def first_kernel(heads, scal, x, w, bias, gain, shift, nn, n1, proj, ctx, probs, w_side, *scratch):
+    s = pl.program_id(0)
+
+    @pl.when(s == 0)
     def _():
         width = w.shape[2]
         for j in range(3):
             w_side[:, j * width : (j + 1) * width] = w[j]
 
-
-def first_kernel(heads, scal, x, w, bias, gain, shift, nn, n1, proj, ctx, probs, w_side, *scratch):
-    s = pl.program_id(0)
-    side_by_side(s, w, w_side)
     for first in range(0, SEQ_LEN, LN_ROWS):
         at = slice(first, first + LN_ROWS)
         for r in range(first, first + LN_ROWS, SUB):
@@ -135,9 +137,20 @@
     attend(length_of(scal, s), proj, *scratch, ctx, probs, heads)
 
 
-def second_kernel(heads, scal, n1, w, bias, proj, ctx, probs, w_side, *scratch):
+def second_kernel(heads, scal, n1, mine, theirs, bias, proj, ctx, probs, w_side, *scratch):
     s = pl.program_id(0)
-    side_by_side(s, w, w_side)
+
+    @pl.when(s == 0)
+    def _():
+        width = bias.shape[1]
+        half = n1.shape[1] // 2
+        for part, place_of in parts_in_order(scal, mine, theirs):
+            for k in range(3):
+                stretch = 3 * place_of + k
+                row = pl.multiple_of((stretch % 2) * half, half)
+                column = pl.multiple_of((stretch // 2) * width, width)
+                w_side[pl.ds(row, half), pl.ds(column, width)] = part[k * half : (k + 1) * half, :]
+
     for first in range(0, SEQ_LEN, LN_ROWS):
         project(slice(first, first + LN_ROWS), n1, w_side, bias, proj)
     attend(length_of(scal, s), proj, *scratch, ctx, probs, heads)
@@ -151,38 +164,46 @@
     return pl.BlockSpec((rows, cols), lambda i, *_: (i, 0))
 
 
-def params():
-    return pltpu.CompilerParams(vmem_limit_bytes=VMEM, dimension_semantics=("arbitrary",))
+NEEDS = {
+    "attend_first": 60, "attend_second": 60, "feed_up": 60, "feed_back": 44, "attend_back": 60,
+    "input_gradient": 60, "layer_out": 57, "unpack": 20,
+}
+
+
+def params(name):
+    return pltpu.CompilerParams(vmem_limit_bytes=NEEDS[name] * 1024 * 1024, dimension_semantics=("arbitrary",))
 
 
 def attention_forward(first, scal, rows, w, bias, gain, shift):
     total, width_in = rows.shape
     seqs = total // SEQ_LEN
-    width = w.shape[2]
+    width = bias.shape[1]
     heads = width // HEAD_DIM
     outs = [
         jax.ShapeDtypeStruct((total, 3 * width), BF16),
         jax.ShapeDtypeStruct((total, width), BF16),
         jax.ShapeDtypeStruct((seqs * NBLK * WIN, heads * QB), BF16),
+        jax.ShapeDtypeStruct((width_in, 3 * width), BF16),
     ]
     out_specs = [
         rows_spec(SEQ_LEN, 3 * width),
         rows_spec(SEQ_LEN, width),
         rows_spec(NBLK * WIN, heads * QB),
+        const_spec((width_in, 3 * width)),
     ]
-    scratch = [pltpu.VMEM((width_in, 3 * width), BF16)]
-    scratch += [pltpu.VMEM((SEQ_LEN + 2 * MARGIN, width), BF16)] * 2
+    scratch = [pltpu.VMEM((SEQ_LEN + 2 * MARGIN, width), BF16)] * 2
     scratch += [pltpu.VMEM((NBLK * WIN, heads * QB), F32)]
     flops = 2 * total * width_in * 3 * width + 8 * total * WIN * width
     cost = pl.CostEstimate(flops=flops, bytes_accessed=total * (width_in + 6 * width) * 2, transcendentals=0)
-    in_specs = [rows_spec(SEQ_LEN, width_in), const_spec(w.shape), const_spec(bias.shape)]
     if first:
-        in_specs += [const_spec(gain.shape), const_spec(shift.shape)]
+        in_specs = [rows_spec(SEQ_LEN, width_in)] + [const_spec(v.shape) for v in (w, bias, gain, shift)]
         outs = [jax.ShapeDtypeStruct(rows.shape, BF16)] * 2 + outs
         out_specs = [rows_spec(SEQ_LEN, width_in)] * 2 + out_specs
         args = (rows, w, bias, gain, shift)
     else:
-        args = (rows, w, bias)
+        half_spec = pl.BlockSpec((3 * width_in // 2, width), lambda *_: (0, 0), pipeline_mode=pl.Buffered(1))
+        in_specs = [rows_spec(SEQ_LEN, width_in), half_spec, half_spec, const_spec(bias.shape)]
+        args = (rows, *w, bias)
 
     def body(*refs):
         (first_kernel if first else second_kernel)(heads, *refs)
@@ -197,7 +218,7 @@
             scratch_shapes=scratch,
         ),
         out_shape=outs,
-        compiler_params=params(),
+        compiler_params=params("attend_first" if first else "attend_second"),
         cost_estimate=cost,
         name="attend_first" if first else "attend_second",
     )(scal, *args)
@@ -256,9 +277,9 @@
 
 def up_kernel(
     per_seq, scal,
-    x, cot, ctx_a, ctx_b, wo_a, wo_b, wu_a, wu_b, bo, gain, shift, bias_a, bias_b,
-    mid_out, n2_out, hidden_out, pre_out, pack_own, pack_other,
-    acc_d, wo_s, ctx_s, branch, n2_half, pre_even, pre_odd,
+    x, cot, ctx_a, ctx_b, wo_a, wo_m, wo_t, wu_a, wu_m, wu_t, bo, gain, shift, bias_a, bias_b,
+    mid_out, n2_out, hidden_out, pre_out, pack_own, pack_other, wo_s, wu_b,
+    acc_d, ctx_s, branch, n2_half, pre_even, pre_odd,
 ):
     i = pl.program_id(0)
     clear(i, acc_d)
@@ -267,7 +288,11 @@
     @pl.when(i == 0)
     def _():
         wo_s[:width, :] = wo_a[...]
-        wo_s[width:, :] = wo_b[...]
+        side, half_rows = wo_m.shape[1], wu_m.shape[0]
+        for part, place_of in parts_in_order(scal, wo_m, wo_t):
+            wo_s[width:, pl.ds(pl.multiple_of(place_of * side, side), side)] = part[...]
+        for part, place_of in parts_in_order(scal, wu_m, wu_t):
+            wu_b[pl.ds(pl.multiple_of(place_of * half_rows, half_rows), half_rows), :] = part[...]
 
     rows = x.shape[0]
     ctx_s[:, :width] = ctx_a[...]
@@ -305,8 +330,8 @@
 
     @pl.when(i == pl.num_programs(0) - 1)
     def _():
-        put_blocks(scal[0], [pack_own], acc_d, slice(0, half))
-        put_blocks(scal[0], [pack_other], acc_d, slice(half, 2 * half))
+        put_blocks(scal[1], [pack_own], acc_d, slice(0, half))
+        put_blocks(scal[1], [pack_other], acc_d, slice(half, 2 * half))
 
 
 def call(kernel, name, grid, scalars, in_specs, outs, out_specs, scratch, flops, nbytes, args, alias=()):
@@ -317,29 +342,32 @@
             scratch_shapes=scratch,
         ),
         out_shape=[jax.ShapeDtypeStruct(s, t) for s, t in outs],
-        compiler_params=params(),
+        compiler_params=params(name),
         input_output_aliases=dict(alias),
         cost_estimate=pl.CostEstimate(flops=flops, bytes_accessed=nbytes, transcendentals=0),
         name=name,
     )(*scalars, *args)
 
 
-def up_block(scal, x, cot, ctx_a, ctx_b, wo, wu, bo, gain, shift, biases):
+def up_block(scal, x, cot, ctx_a, ctx_b, wo_a, wu_a, parts, bo, gain, shift, biases):
     total, d = x.shape
     width = ctx_a.shape[1]
-    half = wu[0].shape[1]
-    args = (x, cot, ctx_a, ctx_b, *wo, *wu, bo, gain, shift, *biases)
+    half = wu_a.shape[1]
+    args = (x, cot, ctx_a, ctx_b, wo_a, *parts[0], wu_a, *parts[1], bo, gain, shift, *biases)
     in_specs = [rows_spec(TU, d), rows_spec(TU, d), rows_spec(TU, width), rows_spec(TU, width)]
-    in_specs += [const_spec(a.shape) for a in args[4:]]
+    tail_spec = lambda v: pl.BlockSpec(
+        (width, v.shape[1]), lambda *_: (v.shape[0] // width - 1, 0), pipeline_mode=pl.Buffered(1)
+    )
+    in_specs += [tail_spec(v) if k in (1, 2) else const_spec(v.shape) for k, v in enumerate(args[4:])]
     pack = (BLOCKS, d // BLOCKS, half)
     outs = [
         ((total, d), F32), ((total, d), BF16), ((total, 2 * half), BF16), ((total, 2 * half), BF16),
-        (pack, BF16), (pack, BF16),
+        (pack, BF16), (pack, BF16), ((2 * width, d), BF16), ((d, half), BF16),
     ]
     out_specs = [rows_spec(TU, d), rows_spec(TU, d), rows_spec(TU, 2 * half), rows_spec(TU, 2 * half)]
-    out_specs += [const_spec(pack), const_spec(pack)]
+    out_specs += [const_spec(s) for s, _ in outs[4:]]
     scratch = [
-        pltpu.VMEM((d, 2 * half), F32), pltpu.VMEM((2 * width, d), BF16), pltpu.VMEM((TU, 2 * width), BF16),
+        pltpu.VMEM((d, 2 * half), F32), pltpu.VMEM((TU, 2 * width), BF16),
         pltpu.VMEM((TU, d), F32), pltpu.VMEM((TU, d), BF16), pltpu.VMEM((TU, FC), F32), pltpu.VMEM((TU, FC), F32),
     ]
 
@@ -354,18 +382,13 @@
 
 def down_kernel(
     scal,
-    cot, mid, n2_in, pre, ctx_a, ctx_b, wo_a, wo_b, wu_a, wu_b, wd_a, wd_b, gain,
+    cot, mid, n2_in, pre, ctx_a, ctx_b, wo_s, wu_a, wu_b, wd_a, wd_b, gain,
     gmid_out, gctx_a, gctx_b, keep_own, keep_other, send_own, send_other,
-    acc_own, acc_other, acc_small, wo_s, ctx_s, n2_t, gh_even, gh_odd, gpre, back_a, back_b,
+    acc_own, acc_other, acc_small, ctx_s, n2_t, gh_even, gh_odd, gpre, back_a, back_b,
 ):
     i = pl.program_id(0)
     clear(i, acc_own, acc_other, acc_small)
     width = ctx_a.shape[1]
-
-    @pl.when(i == 0)
-    def _():
-        wo_s[:width, :] = wo_a[...]
-        wo_s[width:, :] = wo_b[...]
 
     rows = cot.shape[0]
     ctx_s[:, :width] = ctx_a[...]
@@ -451,7 +474,7 @@
     total, d = cot.shape
     width = ctx_a.shape[1]
     half = wu[0].shape[1]
-    args = (cot, mid, n2, pre, ctx_a, ctx_b, *wo, *wu, *wd, gain)
+    args = (cot, mid, n2, pre, ctx_a, ctx_b, wo, *wu, *wd, gain)
     in_specs = [rows_spec(TB, d), rows_spec(TB, d), rows_spec(TB, d), rows_spec(TB, 2 * half)]
     in_specs += [rows_spec(TB, width), rows_spec(TB, width)]
     in_specs += [const_spec(a.shape) for a in args[6:]]
@@ -462,7 +485,7 @@
     out_specs += [const_spec(s) for s, _ in outs[3:]]
     scratch = [
         pltpu.VMEM((d + ONES, columns), F32), pltpu.VMEM((d + ONES, columns), F32),
-        pltpu.VMEM((32, d), F32), pltpu.VMEM((2 * width, d), BF16), pltpu.VMEM((TB, 2 * width), BF16),
+        pltpu.VMEM((32, d), F32), pltpu.VMEM((TB, 2 * width), BF16),
         pltpu.VMEM((d + ONES, TB), BF16),
         pltpu.VMEM((TB, FB), BF16), pltpu.VMEM((TB, FB), BF16), pltpu.VMEM((TB, 2 * half), BF16),
         pltpu.VMEM((TB, d), F32), pltpu.VMEM((TB, d), F32),
@@ -489,7 +512,7 @@
 
     @pl.when(pl.program_id(0) == 0)
     def _():
-        place(scal[0], (d0, d1), d_all, BF16)
+        place(scal[1], (d0, d1), d_all, BF16)
         down[...] = d_all[...].T.astype(F32)
 
 
@@ -571,13 +594,17 @@
         d = acc.shape[0]
         column = lambda v: jnp.broadcast_to(v[...], (EXTRA, d)).T[:, 0:1]
         gain_col, shift_col = column(gain), column(shift)
-        gain_grad, shift_grad = jnp.zeros((d, 1), F32), jnp.zeros((d, 1), F32)
+        gain_grad, shift_grad = jnp.zeros((d, EXTRA), F32), jnp.zeros((d, EXTRA), F32)
         for j in range(3):
-            at = slice(j * width, (j + 1) * width)
-            weight = w[j].astype(F32)
-            gain_grad += jnp.sum(weight * acc[:, at], axis=1, keepdims=True)
-            shift_grad += jnp.sum(weight * acc_b[:, at], axis=1, keepdims=True)
-            acc[:, at] = gain_col * acc[:, at] + shift_col * acc_b[:, at]
+            for c in range(0, width, EXTRA):
+                at = slice(j * width + c, j * width + c + EXTRA)
+                weight = w[:, at].astype(F32)
+                total, sums = acc[:, at], acc_b[:, at]
+                gain_grad += weight * total
+                shift_grad += weight * sums
+                acc[:, at] = gain_col * total + shift_col * sums
+        gain_grad = jnp.sum(gain_grad, axis=1, keepdims=True)
+        shift_grad = jnp.sum(shift_grad, axis=1, keepdims=True)
         put_vectors(acc, 3 * width, [jnp.concatenate([acc_b[:, :width], acc_b[:, 2 * width :]], axis=1)])
         lane = lax.broadcasted_iota(jnp.int32, (d, EXTRA), 1)
         extra = jnp.where(lane == 1, gain_grad, acc[:, 3 * width :])
@@ -618,14 +645,12 @@
 
 
 def last_kernel(per_seq, first, scal, x, gmid, gp_a, gp_b, w_a, w_b, gain, *refs):
-    gin, back_a, back_b, side_a, side_b = refs[-5:]
+    gin, back_a, back_b = refs[-3:]
     i = pl.program_id(0)
-    side_by_side(i, w_a, side_a)
-    side_by_side(i, w_b, side_b)
     rows = x.shape[0]
     tile = i + first
-    back_a[...] = dot_nt(gp_a[...], side_a[...])
-    back_b[...] = dot_nt(gp_b[...], side_b[...])
+    back_a[...] = dot_nt(gp_a[...], w_a[...])
+    back_b[...] = dot_nt(gp_b[...], w_b[...])
     for sub in subs(rows):
         keep = keep_of((SUB, x.shape[1]), (tile % per_seq) * rows + sub.start, tile // per_seq, scal)
         nn, r = normalize(x[sub, :].astype(F32) * keep)
@@ -653,7 +678,7 @@
         specs += [pl.BlockSpec(memory_space=pl.ANY)]
     return call(
         body, "input_gradient", tiles, (scal,), specs, [((total, d), F32)], [part_spec(part * tiles, d)],
-        [pltpu.VMEM((TM, d), F32)] * 2 + [pltpu.VMEM((d, width), BF16)] * 2,
+        [pltpu.VMEM((TM, d), F32)] * 2,
         4 * tiles * TM * d * width, tiles * TM * (10 * d + 4 * width), args, alias,
     )[0]
 
@@ -666,8 +691,8 @@
         out[at, :] = pieces[j // each][j % each, :, columns].astype(kind)
 
 
-def unpack_kernel(scal, u0, u1, q0, q1, up, out, *refs):
-    vectors, (bias_up, qkv, bias_q, gain, shift, u_side, q_all) = refs[:4], refs[4:]
+def unpack_kernel(scal, u0, u1, q0, q1, side_y, side_d, up, out, *refs):
+    vectors, (bias_up, qkv, bias_q, gain, shift, u_side, q_all, q_side) = refs[:4], refs[4:]
     me = scal[0]
     half, side = up.shape[1], out.shape[1] // 2
     rows = out.shape[0]
@@ -685,6 +710,8 @@
         qkv[j] = q_all[:, j * width : (j + 1) * width]
     sums = q_all[:, 3 * width :].T
     bias_q[...] = jnp.concatenate([sums[0:1, :width], sums[0:1, width:]], axis=0)
+    place(scal[1], (side_y, side_d), q_side, F32)
+    sums += q_side[...].T
     gain[...] = sums[1:2, :]
     shift[...] = sums[2:3, :]
 
@@ -692,7 +719,7 @@
 def unpack(scal, pieces, up, out, qkv):
     d = up[0]
     shapes = [up, out, *[(1, d)] * 4, (1, up[1]), qkv, (2, qkv[2]), (1, d), (1, d)]
-    natural = [(d, pieces[0].shape[2] - up[1]), (d, pieces[2].shape[2])]
+    natural = [(d, pieces[0].shape[2] - up[1]), (d, pieces[2].shape[2]), (d, EXTRA)]
     return call(
         unpack_kernel, "unpack", 1, (scal,), [const_spec(p.shape) for p in pieces], [(s, F32) for s in shapes],
         [const_spec(s) for s in shapes], [pltpu.VMEM(s, F32) for s in natural], 0,
@@ -715,7 +742,7 @@
         return swap(v, 1)
 
     def diagonal(v):
-        pairs = [(2 * i + j, 2 * (i ^ 8) + 1 - j) for i in range(dp) for j in range(2)]
+        pairs = [(2 * i + j, 2 * (i ^ 1) + 1 - j) for i in range(dp) for j in range(2)]
         return lax.ppermute(v, ("dp", "tensor"), pairs)
 
     def plus(first, *rest):
@@ -750,7 +777,7 @@
         if paired:
             label = ((index & 1) << 3) | ((index & 2) << 1) | ((index & 4) >> 1)
             label_q = ((index & 1) << 3) | (index & 4)
-        place_here = jnp.stack([label, label_q, here]).astype(jnp.int32)
+        place_here = jnp.stack([label, label_q, here, index & 1 if paired else jnp.int32(0)]).astype(jnp.int32)
         ends = [span[:, k] for span in (time_span, freq_span) for k in range(2)]
         scal = jnp.concatenate([place_here, lengths, *ends])
         row = lambda v: v.reshape(1, -1)
@@ -762,9 +789,10 @@
         def attend_b(rows, w, bias):
             return attention_forward(False, scal, rows, w, bias, None, None)
 
-        def up(ctx_a, ctx_b, wo, wu, biases):
+        def up(ctx_a, ctx_b, wo_a, wu_a, parts, biases):
             return up_block(
-                scal, inputs, cotangent, ctx_a, ctx_b, wo, wu, row(out_bias), row(gain_two), row(shift_two), biases
+                scal, inputs, cotangent, ctx_a, ctx_b, wo_a, wu_a, parts, row(out_bias), row(gain_two),
+                row(shift_two), biases,
             )
 
         def down(mid, n2, pre, ctx_a, ctx_b, wo, wu, wd):
@@ -791,89 +819,83 @@
                 rows = v.shape[0] // 2
                 return lax.dynamic_slice_in_dim(v, odd * rows, rows, 0)
 
-            def whole(mine, theirs):
-                return jnp.concatenate([jnp.where(odd == 0, mine, theirs), jnp.where(odd == 0, theirs, mine)], axis=0)
-
             biases = stack_biases(qkv_bias, up_bias)
             qkv_a = turned(qkv_weight)
-            qkv_rows = qkv_a.reshape(-1, qkv_a.shape[2])
-            (nn, n1, proj_a, ctx_a, probs_a), (qkv_half, out_half, biases_b), _ = window(
-                attend_a, (inputs, qkv_a, biases),
-                [(part_of(qkv_rows), across), (part_of(out_weight), across), (biases, across)],
-            )
-            qkv_b = whole(qkv_half, core(qkv_half)).reshape(qkv_a.shape)
-            (proj_b, ctx_b, probs_b), (up_half, out_theirs), (_, out_half) = window(
-                attend_b, (n1, qkv_b, biases_b), [(part_of(up_weight), across), (out_half, core)]
-            )
-            wo = (out_weight, whole(out_half, out_theirs))
-            wu = (up_weight, whole(up_half, core(up_half)))
-            (mid, n2, hidden, pre, d_own, d_other), (down_b,), _ = window(
-                up, (ctx_a, ctx_b, wo, wu, (biases, biases_b)), [(down_weight, across)]
-            )
+            side = d // 2
+            low, high = qkv_a.reshape(2, -1, side)
+            first_rows = jnp.where(
+                odd == 0,
+                jnp.concatenate([low, out_weight[:, :side]], axis=0),
+                jnp.concatenate([high, out_weight[:, side:]], axis=0),
+            )
+            (nn, n1, proj_a, ctx_a, probs_a, side_a), (first_half, biases_b), _ = window(
+                attend_a, (inputs, qkv_a, biases), [(first_rows, across), (biases, across)]
+            )
+            first_pair = (first_half, core(first_half))
+            (proj_b, ctx_b, probs_b, side_b), (up_half,), _ = window(
+                attend_b, (n1, first_pair, biases_b), [(part_of(up_weight), across)]
+            )
+            pairs = (first_pair, (up_half, core(up_half)))
+            (mid, n2, hidden, pre, d_own, d_other, wo, up_b), (down_b,), _ = window(
+                up, (ctx_a, ctx_b, out_weight, up_weight, pairs, (biases, biases_b)), [(down_weight, across)]
+            )
+            wu = (up_weight, up_b)
             wd = (down_weight, down_b)
             (gmid, gctx_a, gctx_b, u_own, u_other, u_send_own, u_send_other), (d_cross,), _ = window(
                 down, (mid, n2, pre, ctx_a, ctx_b, wo, wu, wd), [(d_other, across)]
             )
+            step = lambda distance: lambda v: swap(v, distance)
             u_other, u_own = plus(u_other, core(u_send_other)), plus(u_own, core(u_send_own))
             d_sum = plus(d_own, d_cross)
             d_sum = plus(lower(d_sum), core(upper(d_sum)))
-            step = lambda distance: lambda v: swap(v, distance)
             (gproj_b, q_other, q_send), (u_cross, d_in), _ = window(
-                back, (nn, proj_b, probs_b, gctx_b, qkv_b), [(u_other, across), (upper(d_sum), step(2))]
+                back, (nn, proj_b, probs_b, gctx_b, side_b), [(u_other, across), (upper(d_sum), step(4))]
             )
             u_sum = plus(u_own, u_cross)
             d_sum = plus(lower(d_sum), d_in)
             q_other = plus(q_other, core(q_send))
             (gproj_a, q_own, q_send), (u_in, d_in, q_cross), _ = window(
-                back, (nn, proj_a, probs_a, gctx_a, qkv_a),
-                [(upper(u_sum), step(2)), (upper(d_sum), step(4)), (q_other, across)],
+                back, (nn, proj_a, probs_a, gctx_a, side_a),
+                [(upper(u_sum), step(2)), (d_sum, step(8)), (q_other, across)],
             )
             u_sum = plus(lower(u_sum), u_in)
-            d_sum = plus(lower(d_sum), d_in)
+            d_sum = plus(d_sum, d_in)
             q_sum = plus(q_own, core(q_send), q_cross)
             input_grad, (u_in, d_in, q_in), _ = window(
-                last(0, 2), (gmid, gproj_a, gproj_b, qkv_a, qkv_b, None),
-                [(upper(u_sum), step(4)), (d_sum, step(8)), (q_sum, step(2))],
+                last(0, 2), (gmid, gproj_a, gproj_b, side_a, side_b, None),
+                [(upper(u_sum), step(4)), (d_sum, step(2)), (upper(q_sum), step(4))],
             )
             u_sum = plus(lower(u_sum), u_in)
             d_sum = plus(d_sum, d_in)
-            q_sum = plus(q_sum, q_in)
+            q_sum = plus(lower(q_sum), q_in)
             input_grad, (u_in, d_in, q_in), _ = window(
-                last(1, 2), (gmid, gproj_a, gproj_b, qkv_a, qkv_b, input_grad),
-                [(u_sum, step(8)), (d_sum, step(4)), (upper(q_sum), step(4))],
+                last(1, 2), (gmid, gproj_a, gproj_b, side_a, side_b, input_grad),
+                [(u_sum, step(8)), (d_sum, step(4)), (q_sum, step(2))],
             )
             u_sum = plus(u_sum, u_in)
             d_sum = join(d_sum, d_in)
-            q_sum = plus(lower(q_sum), q_in)
-            third = q_sum.shape[2] - EXTRA
-            q_sides = q_sum[:, :, third:]
+            q_sum = plus(q_sum, q_in)
             tiles = total // TM
             cuts = (0, tiles // 2, tiles * 3 // 4, tiles)
-            (layer_out,), (u_in, d_in, q_in, q_side_y, q_side_d), _ = window(
+            (layer_out,), (u_in, d_in, q_in), _ = window(
                 out(cuts[0], cuts[1] - cuts[0]), (mid, hidden, wd, None),
-                [(u_sum, step(4)), (d_sum, step(2)), (q_sum, step(8)), (q_sides, across), (q_sides, diagonal)],
+                [(u_sum, step(4)), (d_sum, core), (q_sum, step(8))],
             )
             u_sum = join(u_sum, u_in)
-            d_sum = join(d_sum, d_in)
-            lane = lax.broadcasted_iota(jnp.int32, q_sides.shape, 2)
-            f32 = lambda v: v.astype(F32)
-            q_in_side = f32(q_in[:, :, third:])
-            own = f32(q_sides) + q_in_side
-            both = own + (f32(q_side_y) + f32(q_side_d))
-            q_side = jnp.where((lane == 1) | (lane == 2), both, own).astype(BF16)
-            q_sum = jnp.concatenate([plus(q_sum[:, :, :third], q_in[:, :, :third]), q_side], axis=2)
-            (layer_out,), (u_in, d_in, q_in), _ = window(
-                out(cuts[1], cuts[2] - cuts[1]), (mid, hidden, wd, layer_out),
-                [(u_sum, step(2)), (d_sum, core), (q_sum, step(4))],
+            q_sum = plus(q_sum, q_in)
+            (layer_out, g_down), (u_in, q_in), _ = window(
+                out(cuts[1], cuts[2] - cuts[1]), (mid, hidden, wd, layer_out, d_sum, d_in),
+                [(u_sum, step(2)), (q_sum, step(4))],
             )
             u_sum = join(u_sum, u_in)
             q_sum = join(q_sum, q_in)
-            (layer_out, g_down), (u_in, q_in), _ = window(
-                out(cuts[2], cuts[3] - cuts[2]), (mid, hidden, wd, layer_out, d_sum, d_in),
-                [(u_sum, core), (q_sum, core)],
+            sides = q_sum[:, :, q_sum.shape[2] - EXTRA :]
+            (layer_out,), (u_in, q_in, side_y, side_d), _ = window(
+                out(cuts[2], cuts[3] - cuts[2]), (mid, hidden, wd, layer_out),
+                [(u_sum, core), (q_sum, core), (sides, across), (sides, diagonal)],
             )
             g_up, g_out, *shared_two, g_bu, g_qkv, g_qb, gain_grad, shift_grad = unpack(
-                scal, (u_sum, u_in, q_sum, q_in), up_weight.shape, out_weight.shape, qkv_a.shape
+                scal, (u_sum, u_in, q_sum, q_in, side_y, side_d), up_weight.shape, out_weight.shape, qkv_a.shape
             )
             g_qkv = turned(g_qkv)
             g_bu = g_bu.reshape(-1)
@@ -892,13 +914,15 @@
             qkv = [turned(w) for w in halves(qkv_weight, 2)]
             biases = [stack_biases(q, u) for q, u in zip(halves(qkv_bias, 1), halves(up_bias, 0))]
             wo, wu, wd = halves(out_weight, 0), halves(up_weight, 1), halves(down_weight, 0)
-            nn, n1, proj_a, ctx_a, probs_a = attend_a(inputs, qkv[0], biases[0])
-            proj_b, ctx_b, probs_b = attend_b(n1, qkv[1], biases[1])
-            mid, n2, hidden, pre, d_own, d_other = up(ctx_a, ctx_b, wo, wu, biases)
+            nn, n1, proj_a, ctx_a, probs_a, side_a = attend_a(inputs, qkv[0], biases[0])
+            halves_b = jnp.split(qkv[1].reshape(-1, qkv[1].shape[2]), 2, axis=0)
+            proj_b, ctx_b, probs_b, side_b = attend_b(n1, halves_b, biases[1])
+            parts = (jnp.split(wo[1], 2, axis=1), jnp.split(wu[1], 2, axis=0))
+            mid, n2, hidden, pre, d_own, d_other, wo, _ = up(ctx_a, ctx_b, wo[0], wu[0], parts, biases)
             gmid, gctx_a, gctx_b, *u_packs = down(mid, n2, pre, ctx_a, ctx_b, wo, wu, wd)
-            gproj_b, *q_other = back(nn, proj_b, probs_b, gctx_b, qkv[1])
-            gproj_a, *q_own = back(nn, proj_a, probs_a, gctx_a, qkv[0])
-            input_grad = last(0, 1)(gmid, gproj_a, gproj_b, *qkv, None)
+            gproj_b, *q_other = back(nn, proj_b, probs_b, gctx_b, side_b)
+            gproj_a, *q_own = back(nn, proj_a, probs_a, gctx_a, side_a)
+            input_grad = last(0, 1)(gmid, gproj_a, gproj_b, side_a, side_b, None)
             layer_out = out(0, total // TM)(mid, hidden, wd, None)[0]
             g_down = sums(natural(d_own), natural(d_other), 1).T
             u = natural(u_packs[0], u_packs[2]), natural(u_packs[1], u_packs[3])

time: 249 us -> 240 us (0.964)
  Pallas kernels: 191 us -> 188 us
    pallas_call x10, Pallas kernels: 166 us -> 162 us  [call(): pl.pallas_call(kernel, grid_spec=pltpu.PrefetchScalarGridSpec(num_scalar_...]
    concatenate x4 -> x0, other arithmetic: 2.71 us -> none  [the longest x3 2.69 us: whole(): jnp.concatenate([jnp.where(odd == 0, mine, theirs), jnp.where(odd == 0, t...]
    ppermute x25 -> x23, starting transfers between devices: 18 us -> 17.1 us  [swap(): return lax.ppermute(v, 'dp', [(i, i ^ distance) for i in range(dp)])]
    ppermute x9 -> x8, starting transfers between devices: 10.2 us -> 11.1 us  [across(): return lax.ppermute(v, 'tensor', [(0, 1), (1, 0)])]
    ppermute x25 -> x23, waiting for transfers between devices: 11.2 us -> 11.2 us  [swap(): return lax.ppermute(v, 'dp', [(i, i ^ distance) for i in range(dp)])]
  transfers between devices with their start and end apart: 35 -> 32, of which waited for: 10 -> 9; matrix products, arithmetic and copies ran while one was open for 1% -> 1% of each run, Pallas kernels for 75% -> 77%
where the time goes in v4:
time: 240 us; the launch traced here: 239 us
  Pallas kernels  188 us (78%)
  starting transfers between devices  28.3 us (12%)
  waiting for transfers between devices  12.1 us (5%)
  local copies, waits for them, and re-layouts  6.07 us (3%)
  other arithmetic  3.97 us (2%)
    pallas_call x10, Pallas kernels, call(): pl.pallas_call(kernel, grid_spec=pltpu.PrefetchScalarGridSpec(num_scalar_...  162 us
    pallas_call x2, Pallas kernels, attention_forward(): pl.pallas_call(body, grid_spec=pltpu.PrefetchScalarGridSpec(num_scalar_pr...  25.2 us
    ppermute x23, starting transfers between devices, swap(): return lax.ppermute(v, 'dp', [(i, i ^ distance) for i in range(dp)])  17.1 us
    ppermute x23, waiting for transfers between devices, swap(): return lax.ppermute(v, 'dp', [(i, i ^ distance) for i in range(dp)])  11.2 us
    ppermute x8, starting transfers between devices, across(): return lax.ppermute(v, 'tensor', [(0, 1), (1, 0)])  11.1 us
  transfers between devices with their start and end apart: 32, of which 9 were waited for; matrix products, arithmetic and copies ran while one was open for 1% of the time, Pallas kernels for 77%

profile of v4, /device:TPU:0, one launch (start us, length us, event | category | flops | bytes accessed | tf_op | source)
XLA Modules:
  0.0 239.2 jit_solution(15363698571930501808)
XLA Ops:
  4.4 3.0 %collective-permute-start.1 = (f32[6,256]{1,0:T(8,128)S(1)}, f32[6,256]{1,0:T(8,128)S(1)}, u32[]{:S(2)}, u32[]{:S(2)}) collective-permute-start(f32[6,256]{1,0:T(8,128)S(1)} %pad_maximum_fusion.4.refs_3_.refs_14_), channel_id=1, source_target_pairs={{0,1},{1,0},{2,3},{3,2},{4,5},{5,4},{6,7},{7,6},{8,9},{9,8},{10,11... | collective-permute-start | bytes 18440 | tf_op jit(solution)/shard_map/ppermute | solution.py:736
  8.1 13.8 %attend_first.1 = (bf16[4096,512]{1,0:T(8,128)(2,1)}, bf16[4096,512]{1,0:T(8,128)(2,1)}, bf16[4096,768]{1,0:T(8,128)(2,1)}, bf16[4096,256]{1,0:T(8,128)(2,1)}, b...) custom-call(s32[44]{0:T(128)} %concatenate.25.refs_0_.scal, bf16[4096,512]{1,0:T(8,128)(2,1)} %refs_1_.6, ...), custom_call_target="tpu_custom_call" | custom-call | flops 4026531840 | bytes 16777216 | tf_op jit(solution)/shard_map/attend_first/pallas_call | solution.py:211
  22.1 1.8 collective-permute-done.2.refs_3_.refs_7_
  23.9 1.9 collective-permute-start.3
  25.9 11.4 %attend_second.1 = (bf16[4096,768]{1,0:T(8,128)(2,1)}, bf16[4096,256]{1,0:T(8,128)(2,1)}, bf16[6144,256]{1,0:T(8,128)(2,1)}, bf16[512,768]{1,0:T(8,128)(2,1)}) custom-call(s32[44]{0:T(128)} %concatenate.25.refs_0_.scal, bf16[4096,512]{1,0:T(8,128)(2,1)} %get-tuple-element.224.refs_1_, bf16[1024,256]{1,0:T(8,128)(2,1)} %copy-done.18, ...), custom_call_target="tpu_custom_call" | custom-call | flops 4026531840 | bytes 16777216 | tf_op jit(solution)/shard_map/attend_second/pallas_call | solution.py:211
  38.1 1.9 collective-permute-done.4.refs_10_
  40.0 1.7 collective-permute-start.5
  41.8 36.6 %feed_up.1 = (f32[4096,512]{1,0:T(8,128)}, bf16[4096,512]{1,0:T(8,128)(2,1)}, bf16[4096,2048]{1,0:T(8,128)(2,1)}, bf16[4096,2048]{1,0:T(8,128)(2,1)}, bf16[16,32...) custom-call(s32[44]{0:T(128)} %concatenate.25.refs_0_.scal, ...), custom_call_target="tpu_custom_call" | custom-call | flops 19327352832 | bytes 71303168 | tf_op jit(solution)/shard_map/feed_up/pallas_call | solution.py:338
  81.6 42.3 %feed_back.1 = (bf16[4096,512]{1,0:T(8,128)(2,1)}, bf16[4096,256]{1,0:T(8,128)(2,1)S(1)}, bf16[4096,256]{1,0:T(8,128)(2,1)}, bf16[8,32,1408]{2,1,0:T(8,128)(2,1)...) custom-call(s32[44]{0:T(128)S(1)} %copy-done.4, ...), custom_call_target="tpu_custom_call" | custom-call | flops 30064771072 | bytes 50331648 | tf_op jit(solution)/shard_map/feed_back/pallas_call | solution.py:338
  128.9 1.6 collective-permute-start.11
  130.5 17.6 %attend_back.2 = (bf16[4096,768]{1,0:T(8,128)(2,1)}, bf16[8,32,896]{2,1,0:T(8,128)(2,1)}, bf16[8,32,896]{2,1,0:T(8,128)(2,1)}) custom-call(s32[44]{0:T(128)} %concatenate.25.refs_0_.scal, bf16[4096,512]{1,0:T(8,128)(2,1)} %get-tuple-element.309.refs_1_, bf16[4096,768]{1,0:T(8,128)(2,1)} %get-tuple-element.292.refs_2_, ...), custom_call_target="tpu_custom_call" | custom-call | flops 4831838208 | bytes 23068672 | tf_op jit(solution)/shard_map/attend_back/pallas_call | solution.py:338
  151.1 2.6 %collective-permute-start.14 = (bf16[4,32,1024]{2,1,0:T(8,128)(2,1)S(1)}, bf16[4,32,1024]{2,1,0:T(8,128)(2,1)S(1)}, u32[]{:S(2)}, u32[]{:S(2)}) collective-permute-start(bf16[4,32,1024]{2,1,0:T(8,128)(2,1)S(1)} %add_convert_fusion.10), channel_id=1, source_target_pairs={{0,16},{2,18},{4,20},{6,22},{8,24},{10,26},{12,28},{14,30},{16,0},... | collective-permute-start | bytes 786440 | tf_op jit(solution)/shard_map/ppermute | solution.py:739
  153.7 1.5 collective-permute-start.13
  155.2 17.8 %attend_back.3 = (bf16[4096,768]{1,0:T(8,128)(2,1)}, bf16[8,32,896]{2,1,0:T(8,128)(2,1)}, bf16[8,32,896]{2,1,0:T(8,128)(2,1)}) custom-call(s32[44]{0:T(128)} %concatenate.25.refs_0_.scal, bf16[4096,512]{1,0:T(8,128)(2,1)} %get-tuple-element.309.refs_1_, bf16[4096,768]{1,0:T(8,128)(2,1)} %get-tuple-element.310.refs_2_, ...), custom_call_target="tpu_custom_call" | custom-call | flops 4831838208 | bytes 23068672 | tf_op jit(solution)/shard_map/attend_back/pallas_call | solution.py:338
  173.3 1.8 collective-permute-done.16
  176.8 1.6 collective-permute-start.19
  178.9 10.4 %input_gradient.2.refs_8_ = f32[4096,512]{1,0:T(8,128)} custom-call(s32[44]{0:T(128)} %concatenate.25.refs_0_.scal, bf16[4096,512]{1,0:T(8,128)(2,1)} %refs_1_.6, bf16[4096,512]{1,0:T(8,128)(2,1)} %get-tuple-element.340.refs_2_, bf16[4096,768]{1,0:T(8,128)(2,1)} %get-tuple-element.341.refs_3_, bf16[4096,768]{1,0:T(8,128)(2,1)} %get-tuple-element.342.refs_4_, ...), custom_call_target="tpu_custom_call" | custom-call | flops 3221225472 | bytes 16777216 | tf_op jit(solution)/shard_map/input_gradient/pallas_call | solution.py:338
  191.9 10.4 %input_gradient.3 = f32[4096,512]{1,0:T(8,128)} custom-call(s32[44]{0:T(128)} %concatenate.25.refs_0_.scal, bf16[4096,512]{1,0:T(8,128)(2,1)} %refs_1_.6, bf16[4096,512]{1,0:T(8,128)(2,1)} %get-tuple-element.340.refs_2_, bf16[4096,768]{1,0:T(8,128)(2,1)} %get-tuple-element.341.refs_3_, ...), custom_call_target="tpu_custom_call", output_to_operand_aliasing={{}: (8, {})} | custom-call | flops 3221225472 | bytes 16777216 | tf_op jit(solution)/shard_map/input_gradient/pallas_call | solution.py:338
  202.5 1.7 collective-permute-start.23
  204.2 2.6 %collective-permute-start.25 = (bf16[4,32,896]{2,1,0:T(8,128)(2,1)S(1)}, bf16[4,32,896]{2,1,0:T(8,128)(2,1)S(1)}, u32[]{:S(2)}, u32[]{:S(2)}) collective-permute-start(bf16[4,32,896]{2,1,0:T(8,128)(2,1)S(1)} %add_convert_fusion.12), channel_id=1, source_target_pairs={{0,16},{2,18},{4,20},{6,22},{8,24},{10,26},{12,28},{14,30},{16,0},... | collective-permute-start | bytes 688136 | tf_op jit(solution)/shard_map/ppermute | solution.py:739
  206.8 10.1 %layer_out.3.before = bf16[4096,512]{1,0:T(8,128)(2,1)} custom-call(s32[44]{0:T(128)} %concatenate.25.refs_0_.scal, f32[4096,512]{1,0:T(8,128)} %get-tuple-element.377.mid, bf16[4096,2048]{1,0:T(8,128)(2,1)} %get-tuple-element.378.hidden, bf16[1024,512]{1,0:T(8,128)(2,1)} %wd_a.3, bf16[1024,512]{1,0:T(8,128)(2,1)} %copy-done.1, f32[1,512]{1,0:T(1,128)} %bitcast.37), custom_call_target="tpu_custom_call" | custom-call | flops 4294967296 | bytes 14680064 | tf_op jit(solution)/shard_map/layer_out/pallas_call | solution.py:338
  218.5 7.9 %layer_out.4 = (bf16[4096,512]{1,0:T(8,128)(2,1)}, f32[1024,512]{1,0:T(8,128)}) custom-call(s32[44]{0:T(128)} %concatenate.25.refs_0_.scal, f32[4096,512]{1,0:T(8,128)} %get-tuple-element.377.mid, bf16[4096,2048]{1,0:T(8,128)(2,1)} %get-tuple-element.378.hidden, bf16[1024,512]{1,0:T(8,128)(2,1)} %wd_a.3, ...), custom_call_target="tpu_custom_call", output_to_operand_aliasing={{0}: (6, {})} | custom-call | flops 2147483648 | bytes 7340032 | tf_op jit(solution)/shard_map/layer_out/pallas_call | solution.py:338
  229.8 6.5 %layer_out.5 = bf16[4096,512]{1,0:T(8,128)(2,1)} custom-call(s32[44]{0:T(128)} %concatenate.25.refs_0_.scal, f32[4096,512]{1,0:T(8,128)} %get-tuple-element.377.mid, bf16[4096,2048]{1,0:T(8,128)(2,1)} %get-tuple-element.378.hidden, bf16[1024,512]{1,0:T(8,128)(2,1)} %wd_a.3, bf16[1024,512]{1,0:T(8,128)(2,1)} %copy-done.1, ...), custom_call_target="tpu_custom_call", output_to_operand_aliasing={{}: (6, {})} | custom-call | flops 2147483648 | bytes 7340032 | tf_op jit(solution)/shard_map/layer_out/pallas_call | solution.py:338
  236.3 2.9 %unpack.1 = (f32[512,1024]{1,0:T(8,128)}, f32[256,512]{1,0:T(8,128)}, f32[1,512]{1,0:T(1,128)}, f32[1,512]{1,0:T(1,128)}, f32[1,512]{1,0:T(1,128)}, /*index=5*/f...) custom-call(s32[44]{0:T(128)S(1)} %copy-done.5, ...), custom_call_target="tpu_custom_call" | custom-call | bytes 7471104 | tf_op jit(solution)/shard_map/unpack/pallas_call | solution.py:338
  (131 shorter events, 26.7 us)
Async XLA Ops:
  4.4 17.6 %collective-permute-start.1 = (f32[6,256]{1,0:T(8,128)S(1)}, f32[6,256]{1,0:T(8,128)S(1)}, u32[]{:S(2)}, u32[]{:S(2)}) collective-permute-start(f32[6,256]{1,0:T(8,128)S(1)} %pad_maximum_fusion.4.refs_3_.refs_14_), channel_id=1, source_target_pairs={{0,1},{1,0},{2,3},{3,2},{4,5},{5,4},{6,7},{7,6},{8,9},{9,8},{10,11... | collective-permute-start | bytes 18440 | tf_op jit(solution)/shard_map/ppermute | solution.py:736
  7.4 14.5 %collective-permute-start = (bf16[1024,256]{1,0:T(8,128)(2,1)S(1)}, bf16[1024,256]{1,0:T(8,128)(2,1)S(1)}, u32[]{:S(2)}, u32[]{:S(2)}) collective-permute-start(bf16[1024,256]{1,0:T(8,128)(2,1)S(1)} %maximum_select_fusion), channel_id=1, source_target_pairs={{0,1},{1,0},{2,3},{3,2},{4,5},{5,4},{6,7},{7,6},{8,9},{9,8},{10,11... | collective-permute-start | bytes 1572872 | tf_op jit(solution)/shard_map/ppermute | solution.py:736
  23.9 14.2 %collective-permute-start.3 = (bf16[256,1024]{1,0:T(8,128)(2,1)S(1)}, bf16[256,1024]{1,0:T(8,128)(2,1)S(1)}, u32[]{:S(2)}, u32[]{:S(2)}) collective-permute-start(bf16[256,1024]{1,0:T(8,128)(2,1)S(1)} %constant_dynamic-slice_fusion), channel_id=1, source_target_pairs={{0,1},{1,0},{2,3},{3,2},{4,5},{5,4},{6,7},{7,6},{8,9},{9,8},{10,11... | collective-permute-start | bytes 1572872 | tf_op jit(solution)/shard_map/ppermute | solution.py:736
  40.0 38.4 %collective-permute-start.5 = (bf16[1024,512]{1,0:T(8,128)(2,1)S(1)}, bf16[1024,512]{1,0:T(8,128)(2,1)S(1)}, u32[]{:S(2)}, u32[]{:S(2)}) collective-permute-start(bf16[1024,512]{1,0:T(8,128)(2,1)S(1)} %copy-done), channel_id=1, source_target_pairs={{0,1},{1,0},{2,3},{3,2},{4,5},{5,4},{6,7},{7,6},{8,9},{9,8},{10,11... | collective-permute-start | bytes 3145736 | tf_op jit(solution)/shard_map/ppermute | solution.py:736
  78.5 45.4 %collective-permute-start.6 = (bf16[16,32,1024]{2,1,0:T(8,128)(2,1)}, bf16[16,32,1024]{2,1,0:T(8,128)(2,1)S(1)}, u32[]{:S(2)}, u32[]{:S(2)}) collective-permute-start(bf16[16,32,1024]{2,1,0:T(8,128)(2,1)} %get-tuple-element.279), channel_id=1, source_target_pairs={{0,1},{1,0},{2,3},{3,2},{4,5},{5,4},{6,7},{7,6},{8,9},{9,8},{10,11... | collective-permute-start | bytes 3145736 | tf_op jit(solution)/shard_map/ppermute | solution.py:736
  127.6 20.5 %collective-permute-start.10 = (bf16[8,32,1408]{2,1,0:T(8,128)(2,1)S(1)}, bf16[8,32,1408]{2,1,0:T(8,128)(2,1)S(1)}, u32[]{:S(2)}, u32[]{:S(2)}) collective-permute-start(bf16[8,32,1408]{2,1,0:T(8,128)(2,1)S(1)} %add_convert_fusion.2), channel_id=1, source_target_pairs={{0,1},{1,0},{2,3},{3,2},{4,5},{5,4},{6,7},{7,6},{8,9},{9,8},{10,11... | collective-permute-start | bytes 2162696 | tf_op jit(solution)/shard_map/ppermute | solution.py:736
  128.9 19.5 %collective-permute-start.7 = (bf16[8,32,1408]{2,1,0:T(8,128)(2,1)}, bf16[8,32,1408]{2,1,0:T(8,128)(2,1)S(1)}, u32[]{:S(2)}, u32[]{:S(2)}) collective-permute-start(bf16[8,32,1408]{2,1,0:T(8,128)(2,1)} %get-tuple-element.281), channel_id=1, source_target_pairs={{0,2},{2,0},{4,6},{6,4},{8,10},{10,8},{12,14},{14,12},{16,18},{18,... | collective-permute-start | bytes 2162696 | tf_op jit(solution)/shard_map/ppermute | solution.py:739
  128.9 19.2 %collective-permute-start.11 = (bf16[4,32,1024]{2,1,0:T(8,128)(2,1)S(1)}, bf16[4,32,1024]{2,1,0:T(8,128)(2,1)S(1)}, u32[]{:S(2)}, u32[]{:S(2)}) collective-permute-start(bf16[4,32,1024]{2,1,0:T(8,128)(2,1)S(1)} %slice.70), channel_id=1, source_target_pairs={{0,8},{2,10},{4,12},{6,14},{8,0},{10,2},{12,4},{14,6},{16,24},{18,... | collective-permute-start | bytes 786440 | tf_op jit(solution)/shard_map/ppermute | solution.py:739
  150.3 22.7 %collective-permute-start.15 = (bf16[8,32,896]{2,1,0:T(8,128)(2,1)S(1)}, bf16[8,32,896]{2,1,0:T(8,128)(2,1)S(1)}, u32[]{:S(2)}, u32[]{:S(2)}) collective-permute-start(bf16[8,32,896]{2,1,0:T(8,128)(2,1)S(1)} %add_convert_fusion.6), channel_id=1, source_target_pairs={{0,1},{1,0},{2,3},{3,2},{4,5},{5,4},{6,7},{7,6},{8,9},{9,8},{10,11... | collective-permute-start | bytes 1376264 | tf_op jit(solution)/shard_map/ppermute | solution.py:736
  151.1 21.9 %collective-permute-start.14 = (bf16[4,32,1024]{2,1,0:T(8,128)(2,1)S(1)}, bf16[4,32,1024]{2,1,0:T(8,128)(2,1)S(1)}, u32[]{:S(2)}, u32[]{:S(2)}) collective-permute-start(bf16[4,32,1024]{2,1,0:T(8,128)(2,1)S(1)} %add_convert_fusion.10), channel_id=1, source_target_pairs={{0,16},{2,18},{4,20},{6,22},{8,24},{10,26},{12,28},{14,30},{16,0},... | collective-permute-start | bytes 786440 | tf_op jit(solution)/shard_map/ppermute | solution.py:739
  153.7 19.3 %collective-permute-start.13 = (bf16[4,32,1408]{2,1,0:T(8,128)(2,1)S(1)}, bf16[4,32,1408]{2,1,0:T(8,128)(2,1)S(1)}, u32[]{:S(2)}, u32[]{:S(2)}) collective-permute-start(bf16[4,32,1408]{2,1,0:T(8,128)(2,1)S(1)} %slice.72), channel_id=1, source_target_pairs={{0,4},{2,6},{4,0},{6,2},{8,12},{10,14},{12,8},{14,10},{16,20},{18,... | collective-permute-start | bytes 1081352 | tf_op jit(solution)/shard_map/ppermute | solution.py:739
  176.3 13.0 %collective-permute-start.17 = (bf16[2,32,1408]{2,1,0:T(8,128)(2,1)S(1)}, bf16[2,32,1408]{2,1,0:T(8,128)(2,1)S(1)}, u32[]{:S(2)}, u32[]{:S(2)}) collective-permute-start(bf16[2,32,1408]{2,1,0:T(8,128)(2,1)S(1)} %slice.75), channel_id=1, source_target_pairs={{0,8},{2,10},{4,12},{6,14},{8,0},{10,2},{12,4},{14,6},{16,24},{18,... | collective-permute-start | bytes 540680 | tf_op jit(solution)/shard_map/ppermute | solution.py:739
  176.8 12.5 %collective-permute-start.19 = (bf16[4,32,896]{2,1,0:T(8,128)(2,1)S(1)}, bf16[4,32,896]{2,1,0:T(8,128)(2,1)S(1)}, u32[]{:S(2)}, u32[]{:S(2)}) collective-permute-start(bf16[4,32,896]{2,1,0:T(8,128)(2,1)S(1)} %slice.76), channel_id=1, source_target_pairs={{0,8},{2,10},{4,12},{6,14},{8,0},{10,2},{12,4},{14,6},{16,24},{18,... | collective-permute-start | bytes 688136 | tf_op jit(solution)/shard_map/ppermute | solution.py:739
  178.4 10.9 %collective-permute-start.18 = (bf16[4,32,1024]{2,1,0:T(8,128)(2,1)S(1)}, bf16[4,32,1024]{2,1,0:T(8,128)(2,1)S(1)}, u32[]{:S(2)}, u32[]{:S(2)}) collective-permute-start(bf16[4,32,1024]{2,1,0:T(8,128)(2,1)S(1)} %add_convert_fusion.9), channel_id=1, source_target_pairs={{0,4},{2,6},{4,0},{6,2},{8,12},{10,14},{12,8},{14,10},{16,20},{18,... | collective-permute-start | bytes 786440 | tf_op jit(solution)/shard_map/ppermute | solution.py:739
  189.5 12.7 %collective-permute-start.20 = (bf16[2,32,1408]{2,1,0:T(8,128)(2,1)S(1)}, bf16[2,32,1408]{2,1,0:T(8,128)(2,1)S(1)}, u32[]{:S(2)}, u32[]{:S(2)}) collective-permute-start(bf16[2,32,1408]{2,1,0:T(8,128)(2,1)S(1)} %add_convert_fusion.15), channel_id=1, source_target_pairs={{0,16},{2,18},{4,20},{6,22},{8,24},{10,26},{12,28},{14,30},{16,0},... | collective-permute-start | bytes 540680 | tf_op jit(solution)/shard_map/ppermute | solution.py:739
  189.9 12.3 %collective-permute-start.22 = (bf16[4,32,896]{2,1,0:T(8,128)(2,1)S(1)}, bf16[4,32,896]{2,1,0:T(8,128)(2,1)S(1)}, u32[]{:S(2)}, u32[]{:S(2)}) collective-permute-start(bf16[4,32,896]{2,1,0:T(8,128)(2,1)S(1)} %add_convert_fusion.13), channel_id=1, source_target_pairs={{0,4},{2,6},{4,0},{6,2},{8,12},{10,14},{12,8},{14,10},{16,20},{18,... | collective-permute-start | bytes 688136 | tf_op jit(solution)/shard_map/ppermute | solution.py:739
  191.4 10.9 %collective-permute-start.21 = (bf16[4,32,1024]{2,1,0:T(8,128)(2,1)S(1)}, bf16[4,32,1024]{2,1,0:T(8,128)(2,1)S(1)}, u32[]{:S(2)}, u32[]{:S(2)}) collective-permute-start(bf16[4,32,1024]{2,1,0:T(8,128)(2,1)S(1)} %add_convert_fusion.8), channel_id=1, source_target_pairs={{0,8},{2,10},{4,12},{6,14},{8,0},{10,2},{12,4},{14,6},{16,24},{18,... | collective-permute-start | bytes 786440 | tf_op jit(solution)/shard_map/ppermute | solution.py:739
  202.5 15.3 %collective-permute-start.24 = (bf16[8,32,1024]{2,1,0:T(8,128)(2,1)S(1)}, bf16[8,32,1024]{2,1,0:T(8,128)(2,1)S(1)}, u32[]{:S(2)}, u32[]{:S(2)}) collective-permute-start(bf16[8,32,1024]{2,1,0:T(8,128)(2,1)S(1)} %pad_maximum_fusion.1.d0), channel_id=1, source_target_pairs={{0,2},{2,0},{4,6},{6,4},{8,10},{10,8},{12,14},{14,12},{16,18},{18,... | collective-permute-start | bytes 1572872 | tf_op jit(solution)/shard_map/ppermute | solution.py:739
  202.5 14.3 %collective-permute-start.23 = (bf16[2,32,1408]{2,1,0:T(8,128)(2,1)S(1)}, bf16[2,32,1408]{2,1,0:T(8,128)(2,1)S(1)}, u32[]{:S(2)}, u32[]{:S(2)}) collective-permute-start(bf16[2,32,1408]{2,1,0:T(8,128)(2,1)S(1)} %add_convert_fusion.14), channel_id=1, source_target_pairs={{0,8},{2,10},{4,12},{6,14},{8,0},{10,2},{12,4},{14,6},{16,24},{18,... | collective-permute-start | bytes 540680 | tf_op jit(solution)/shard_map/ppermute | solution.py:739
  204.2 13.5 %collective-permute-start.25 = (bf16[4,32,896]{2,1,0:T(8,128)(2,1)S(1)}, bf16[4,32,896]{2,1,0:T(8,128)(2,1)S(1)}, u32[]{:S(2)}, u32[]{:S(2)}) collective-permute-start(bf16[4,32,896]{2,1,0:T(8,128)(2,1)S(1)} %add_convert_fusion.12), channel_id=1, source_target_pairs={{0,16},{2,18},{4,20},{6,22},{8,24},{10,26},{12,28},{14,30},{16,0},... | collective-permute-start | bytes 688136 | tf_op jit(solution)/shard_map/ppermute | solution.py:739
  217.8 9.7 %collective-permute-start.26 = (bf16[4,32,1408]{2,1,0:T(8,128)(2,1)S(1)}, bf16[4,32,1408]{2,1,0:T(8,128)(2,1)S(1)}, u32[]{:S(2)}, u32[]{:S(2)}) collective-permute-start(bf16[4,32,1408]{2,1,0:T(8,128)(2,1)S(1)} %pad_maximum_fusion.3), channel_id=1, source_target_pairs={{0,4},{2,6},{4,0},{6,2},{8,12},{10,14},{12,8},{14,10},{16,20},{18,... | collective-permute-start | bytes 1081352 | tf_op jit(solution)/shard_map/ppermute | solution.py:739
  218.5 8.0 %collective-permute-start.27 = (bf16[4,32,896]{2,1,0:T(8,128)(2,1)S(1)}, bf16[4,32,896]{2,1,0:T(8,128)(2,1)S(1)}, u32[]{:S(2)}, u32[]{:S(2)}) collective-permute-start(bf16[4,32,896]{2,1,0:T(8,128)(2,1)S(1)} %add_convert_fusion.11), channel_id=1, source_target_pairs={{0,8},{2,10},{4,12},{6,14},{8,0},{10,2},{12,4},{14,6},{16,24},{18,... | collective-permute-start | bytes 688136 | tf_op jit(solution)/shard_map/ppermute | solution.py:739
  227.8 8.5 %collective-permute-start.28 = (bf16[8,32,1408]{2,1,0:T(8,128)(2,1)S(1)}, bf16[8,32,1408]{2,1,0:T(8,128)(2,1)S(1)}, u32[]{:S(2)}, u32[]{:S(2)}) collective-permute-start(bf16[8,32,1408]{2,1,0:T(8,128)(2,1)S(1)} %pad_maximum_fusion.u0), channel_id=1, source_target_pairs={{0,2},{2,0},{4,6},{6,4},{8,10},{10,8},{12,14},{14,12},{16,18},{18,... | collective-permute-start | bytes 2162696 | tf_op jit(solution)/shard_map/ppermute | solution.py:739
  227.8 8.4 %collective-permute-start.29 = (bf16[8,32,896]{2,1,0:T(8,128)(2,1)S(1)}, bf16[8,32,896]{2,1,0:T(8,128)(2,1)S(1)}, u32[]{:S(2)}, u32[]{:S(2)}) collective-permute-start(bf16[8,32,896]{2,1,0:T(8,128)(2,1)S(1)} %pad_maximum_fusion.2.q0), channel_id=1, source_target_pairs={{0,2},{2,0},{4,6},{6,4},{8,10},{10,8},{12,14},{14,12},{16,18},{18,... | collective-permute-start | bytes 1376264 | tf_op jit(solution)/shard_map/ppermute | solution.py:739
  (31 other events, 330.1 us)

commit v5 on v4

--- a/solution.py
+++ b/solution.py
@@ -10,8 +10,8 @@
 LEFT = 10
 RIGHT = 2
 QB = 64
-MARGIN = 16
-WIN = QB + 2 * MARGIN
+MARGIN = 14
+WIN = QB + 16
 NBLK = SEQ_LEN // QB
 EPS = 1e-05
 LN_ROWS = 256
@@ -76,10 +76,10 @@
 
 def attend(length, proj, kpad, vpad, scores, ctx, probs_out, heads):
     width = heads * HEAD_DIM
-    edge = jnp.zeros((MARGIN, width), BF16)
+    edge = jnp.zeros((WIN - QB, width), BF16)
     for pad, j in ((kpad, 1), (vpad, 2)):
-        pad[0:MARGIN, :] = edge
-        pad[MARGIN + SEQ_LEN :, :] = edge
+        pad[0 : WIN - QB, :] = edge
+        pad[SEQ_LEN:, :] = edge
         pad[MARGIN : MARGIN + SEQ_LEN, :] = proj[:, j * width : (j + 1) * width]
     mask = head_mask(HEAD_DIM**-0.5, heads)
     key = lax.broadcasted_iota(jnp.int32, (WIN, heads * QB), 0)
@@ -165,7 +165,7 @@
 
 
 NEEDS = {
-    "attend_first": 60, "attend_second": 60, "feed_up": 60, "feed_back": 44, "attend_back": 60,
+    "attend_first": 60, "attend_second": 60, "feed_up": 49, "feed_back": 42, "attend_back": 60,
     "input_gradient": 60, "layer_out": 57, "unpack": 20,
 }
 
@@ -191,7 +191,7 @@
         rows_spec(NBLK * WIN, heads * QB),
         const_spec((width_in, 3 * width)),
     ]
-    scratch = [pltpu.VMEM((SEQ_LEN + 2 * MARGIN, width), BF16)] * 2
+    scratch = [pltpu.VMEM((SEQ_LEN + WIN - QB, width), BF16)] * 2
     scratch += [pltpu.VMEM((NBLK * WIN, heads * QB), F32)]
     flops = 2 * total * width_in * 3 * width + 8 * total * WIN * width
     cost = pl.CostEstimate(flops=flops, bytes_accessed=total * (width_in + 6 * width) * 2, transcendentals=0)
@@ -275,11 +275,20 @@
     return jnp.concatenate([biases[r : r + 1, :] for r in rows], axis=1)
 
 
+def assemble(scal, wo_a, wo_m, wo_t, wu_m, wu_t, wo_s, wu_b):
+    width, side, rows = wo_a.shape[0], wo_m.shape[1], wu_m.shape[0]
+    wo_s[:width, :] = wo_a[...]
+    for part, place_of in parts_in_order(scal, wo_m, wo_t):
+        wo_s[width:, pl.ds(pl.multiple_of(place_of * side, side), side)] = part[...]
+    for part, place_of in parts_in_order(scal, wu_m, wu_t):
+        wu_b[pl.ds(pl.multiple_of(place_of * rows, rows), rows), :] = part[...]
+
+
 def up_kernel(
     per_seq, scal,
     x, cot, ctx_a, ctx_b, wo_a, wo_m, wo_t, wu_a, wu_m, wu_t, bo, gain, shift, bias_a, bias_b,
-    mid_out, n2_out, hidden_out, pre_out, pack_own, pack_other, wo_s, wu_b,
-    acc_d, ctx_s, branch, n2_half, pre_even, pre_odd,
+    mid_out, n2_out, hidden_out, pre_out, pack_own, pack_other,
+    acc_d, wo_s, wu_b, ctx_s, branch, n2_half, pre_even, pre_odd,
 ):
     i = pl.program_id(0)
     clear(i, acc_d)
@@ -287,12 +296,7 @@
 
     @pl.when(i == 0)
     def _():
-        wo_s[:width, :] = wo_a[...]
-        side, half_rows = wo_m.shape[1], wu_m.shape[0]
-        for part, place_of in parts_in_order(scal, wo_m, wo_t):
-            wo_s[width:, pl.ds(pl.multiple_of(place_of * side, side), side)] = part[...]
-        for part, place_of in parts_in_order(scal, wu_m, wu_t):
-            wu_b[pl.ds(pl.multiple_of(place_of * half_rows, half_rows), half_rows), :] = part[...]
+        assemble(scal, wo_a, wo_m, wo_t, wu_m, wu_t, wo_s, wu_b)
 
     rows = x.shape[0]
     ctx_s[:, :width] = ctx_a[...]
@@ -349,25 +353,29 @@
     )(*scalars, *args)
 
 
+def tail_spec(v, rows):
+    return pl.BlockSpec(
+        (rows, v.shape[1]), lambda *_: (v.shape[0] // rows - 1, 0), pipeline_mode=pl.Buffered(1)
+    )
+
+
 def up_block(scal, x, cot, ctx_a, ctx_b, wo_a, wu_a, parts, bo, gain, shift, biases):
     total, d = x.shape
     width = ctx_a.shape[1]
     half = wu_a.shape[1]
     args = (x, cot, ctx_a, ctx_b, wo_a, *parts[0], wu_a, *parts[1], bo, gain, shift, *biases)
     in_specs = [rows_spec(TU, d), rows_spec(TU, d), rows_spec(TU, width), rows_spec(TU, width)]
-    tail_spec = lambda v: pl.BlockSpec(
-        (width, v.shape[1]), lambda *_: (v.shape[0] // width - 1, 0), pipeline_mode=pl.Buffered(1)
-    )
-    in_specs += [tail_spec(v) if k in (1, 2) else const_spec(v.shape) for k, v in enumerate(args[4:])]
+    in_specs += [tail_spec(v, width) if k in (1, 2) else const_spec(v.shape) for k, v in enumerate(args[4:])]
     pack = (BLOCKS, d // BLOCKS, half)
     outs = [
         ((total, d), F32), ((total, d), BF16), ((total, 2 * half), BF16), ((total, 2 * half), BF16),
-        (pack, BF16), (pack, BF16), ((2 * width, d), BF16), ((d, half), BF16),
+        (pack, BF16), (pack, BF16),
     ]
     out_specs = [rows_spec(TU, d), rows_spec(TU, d), rows_spec(TU, 2 * half), rows_spec(TU, 2 * half)]
     out_specs += [const_spec(s) for s, _ in outs[4:]]
     scratch = [
-        pltpu.VMEM((d, 2 * half), F32), pltpu.VMEM((TU, 2 * width), BF16),
+        pltpu.VMEM((d, 2 * half), F32), pltpu.VMEM((2 * width, d), BF16), pltpu.VMEM((d, half), BF16),
+        pltpu.VMEM((TU, 2 * width), BF16),
         pltpu.VMEM((TU, d), F32), pltpu.VMEM((TU, d), BF16), pltpu.VMEM((TU, FC), F32), pltpu.VMEM((TU, FC), F32),
     ]
 
@@ -382,13 +390,18 @@
 
 def down_kernel(
     scal,
-    cot, mid, n2_in, pre, ctx_a, ctx_b, wo_s, wu_a, wu_b, wd_a, wd_b, gain,
+    cot, mid, n2_in, pre, ctx_a, ctx_b, wo_a, wo_m, wo_t, wu_a, wu_m, wu_t, wd_a, wd_b, gain,
     gmid_out, gctx_a, gctx_b, keep_own, keep_other, send_own, send_other,
-    acc_own, acc_other, acc_small, ctx_s, n2_t, gh_even, gh_odd, gpre, back_a, back_b,
+    acc_own, acc_other, acc_small, wo_s, wu_b, ctx_s, n2_t, gh_even, gh_odd, gpre, back_a, back_b,
 ):
     i = pl.program_id(0)
     clear(i, acc_own, acc_other, acc_small)
     width = ctx_a.shape[1]
+
+    @pl.when(i == 0)
+    def _():
+        assemble(scal, wo_a, wo_m, wo_t, wu_m, wu_t, wo_s, wu_b)
+
 
     rows = cot.shape[0]
     ctx_s[:, :width] = ctx_a[...]
@@ -470,14 +483,14 @@
             put_blocks(scal[0], [keep, send], acc, slice(None))
 
 
-def down_block(scal, cot, mid, n2, pre, ctx_a, ctx_b, wo, wu, wd, gain):
+def down_block(scal, cot, mid, n2, pre, ctx_a, ctx_b, wo_a, wu_a, parts, wd, gain):
     total, d = cot.shape
     width = ctx_a.shape[1]
-    half = wu[0].shape[1]
-    args = (cot, mid, n2, pre, ctx_a, ctx_b, wo, *wu, *wd, gain)
+    half = wu_a.shape[1]
+    args = (cot, mid, n2, pre, ctx_a, ctx_b, wo_a, *parts[0], wu_a, *parts[1], *wd, gain)
     in_specs = [rows_spec(TB, d), rows_spec(TB, d), rows_spec(TB, d), rows_spec(TB, 2 * half)]
     in_specs += [rows_spec(TB, width), rows_spec(TB, width)]
-    in_specs += [const_spec(a.shape) for a in args[6:]]
+    in_specs += [tail_spec(v, width) if k in (1, 2) else const_spec(v.shape) for k, v in enumerate(args[6:])]
     columns = half + d // 2 + EXTRA
     pack = (BLOCKS // 2, d // BLOCKS, columns)
     outs = [((total, d), BF16), ((total, width), BF16), ((total, width), BF16), *[(pack, BF16)] * 4]
@@ -485,7 +498,8 @@
     out_specs += [const_spec(s) for s, _ in outs[3:]]
     scratch = [
         pltpu.VMEM((d + ONES, columns), F32), pltpu.VMEM((d + ONES, columns), F32),
-        pltpu.VMEM((32, d), F32), pltpu.VMEM((TB, 2 * width), BF16),
+        pltpu.VMEM((32, d), F32), pltpu.VMEM((2 * width, d), BF16), pltpu.VMEM((d, half), BF16),
+        pltpu.VMEM((TB, 2 * width), BF16),
         pltpu.VMEM((d + ONES, TB), BF16),
         pltpu.VMEM((TB, FB), BF16), pltpu.VMEM((TB, FB), BF16), pltpu.VMEM((TB, 2 * half), BF16),
         pltpu.VMEM((TB, d), F32), pltpu.VMEM((TB, d), F32),
@@ -550,14 +564,14 @@
     s = pl.program_id(0)
     clear(s, acc, acc_b)
     width = heads * HEAD_DIM
-    edge = jnp.zeros((MARGIN, width), BF16)
+    edge = jnp.zeros((WIN - QB, width), BF16)
     for pad, j in ((kpad, 1), (vpad, 2)):
-        pad[0:MARGIN, :] = edge
-        pad[MARGIN + SEQ_LEN :, :] = edge
+        pad[0 : WIN - QB, :] = edge
+        pad[SEQ_LEN:, :] = edge
         pad[MARGIN : MARGIN + SEQ_LEN, :] = proj[:, j * width : (j + 1) * width]
     mask = head_mask(1.0, heads)
-    dk[0 : 2 * MARGIN, :] = jnp.zeros((2 * MARGIN, width), F32)
-    dv[0 : 2 * MARGIN, :] = jnp.zeros((2 * MARGIN, width), F32)
+    dk[0 : (WIN - QB), :] = jnp.zeros(((WIN - QB), width), F32)
+    dv[0 : (WIN - QB), :] = jnp.zeros(((WIN - QB), width), F32)
     scale = HEAD_DIM**-0.5
 
     def rows(b):
@@ -581,8 +595,8 @@
         key_term = dot_nn(gscore[own(b), :], spread(proj[rows(b), 0:width], mask, heads)) * scale
         value_term = dot_nn(probs[own(b), :], spread(gctx[rows(b), :], mask, heads))
         for total, term in ((dk, key_term), (dv, value_term)):
-            total[b * QB : b * QB + 2 * MARGIN, :] += term[: 2 * MARGIN]
-            total[b * QB + 2 * MARGIN : b * QB + WIN, :] = term[2 * MARGIN :]
+            total[b * QB : b * QB + (WIN - QB), :] += term[: (WIN - QB)]
+            total[b * QB + (WIN - QB) : b * QB + WIN, :] = term[(WIN - QB) :]
     gproj[:, width : 2 * width] = dk[MARGIN : MARGIN + SEQ_LEN, :].astype(BF16)
     gproj[:, 2 * width :] = dv[MARGIN : MARGIN + SEQ_LEN, :].astype(BF16)
     gp_all = gproj[...]
@@ -621,7 +635,7 @@
     def body(*refs):
         attend_back_kernel(heads, *refs)
 
-    pad = SEQ_LEN + 2 * MARGIN
+    pad = SEQ_LEN + WIN - QB
     columns = 3 * width + EXTRA
     pack = (BLOCKS // 2, d // BLOCKS, columns)
     return call(
@@ -795,8 +809,8 @@
                 row(shift_two), biases,
             )
 
-        def down(mid, n2, pre, ctx_a, ctx_b, wo, wu, wd):
-            return down_block(scal, cotangent, mid, n2, pre, ctx_a, ctx_b, wo, wu, wd, row(gain_two))
+        def down(mid, n2, pre, ctx_a, ctx_b, wo_a, wu_a, parts, wd):
+            return down_block(scal, cotangent, mid, n2, pre, ctx_a, ctx_b, wo_a, wu_a, parts, wd, row(gain_two))
 
         def back(nn, proj, probs, gctx, w):
             return attention_backward(scal, nn, proj, probs, gctx, w, row(gain_one), row(shift_one))
@@ -836,13 +850,12 @@
                 attend_b, (n1, first_pair, biases_b), [(part_of(up_weight), across)]
             )
             pairs = (first_pair, (up_half, core(up_half)))
-            (mid, n2, hidden, pre, d_own, d_other, wo, up_b), (down_b,), _ = window(
+            (mid, n2, hidden, pre, d_own, d_other), (down_b,), _ = window(
                 up, (ctx_a, ctx_b, out_weight, up_weight, pairs, (biases, biases_b)), [(down_weight, across)]
             )
-            wu = (up_weight, up_b)
             wd = (down_weight, down_b)
             (gmid, gctx_a, gctx_b, u_own, u_other, u_send_own, u_send_other), (d_cross,), _ = window(
-                down, (mid, n2, pre, ctx_a, ctx_b, wo, wu, wd), [(d_other, across)]
+                down, (mid, n2, pre, ctx_a, ctx_b, out_weight, up_weight, pairs, wd), [(d_other, across)]
             )
             step = lambda distance: lambda v: swap(v, distance)
             u_other, u_own = plus(u_other, core(u_send_other)), plus(u_own, core(u_send_own))
@@ -860,14 +873,14 @@
             )
             u_sum = plus(lower(u_sum), u_in)
             d_sum = plus(d_sum, d_in)
-            q_sum = plus(q_own, core(q_send), q_cross)
+            q_terms = (q_own, core(q_send), q_cross)
             input_grad, (u_in, d_in, q_in), _ = window(
                 last(0, 2), (gmid, gproj_a, gproj_b, side_a, side_b, None),
-                [(upper(u_sum), step(4)), (d_sum, step(2)), (upper(q_sum), step(4))],
+                [(upper(u_sum), step(4)), (d_sum, step(2)), (plus(*map(upper, q_terms)), step(4))],
             )
             u_sum = plus(lower(u_sum), u_in)
             d_sum = plus(d_sum, d_in)
-            q_sum = plus(lower(q_sum), q_in)
+            q_sum = plus(*map(lower, q_terms), q_in)
             input_grad, (u_in, d_in, q_in), _ = window(
                 last(1, 2), (gmid, gproj_a, gproj_b, side_a, side_b, input_grad),
                 [(u_sum, step(8)), (d_sum, step(4)), (q_sum, step(2))],
@@ -876,7 +889,7 @@
             d_sum = join(d_sum, d_in)
             q_sum = plus(q_sum, q_in)
             tiles = total // TM
-            cuts = (0, tiles // 2, tiles * 3 // 4, tiles)
+            cuts = (0, tiles * 5 // 8, tiles * 7 // 8, tiles)
             (layer_out,), (u_in, d_in, q_in), _ = window(
                 out(cuts[0], cuts[1] - cuts[0]), (mid, hidden, wd, None),
                 [(u_sum, step(4)), (d_sum, core), (q_sum, step(8))],
@@ -918,8 +931,8 @@
             halves_b = jnp.split(qkv[1].reshape(-1, qkv[1].shape[2]), 2, axis=0)
             proj_b, ctx_b, probs_b, side_b = attend_b(n1, halves_b, biases[1])
             parts = (jnp.split(wo[1], 2, axis=1), jnp.split(wu[1], 2, axis=0))
-            mid, n2, hidden, pre, d_own, d_other, wo, _ = up(ctx_a, ctx_b, wo[0], wu[0], parts, biases)
-            gmid, gctx_a, gctx_b, *u_packs = down(mid, n2, pre, ctx_a, ctx_b, wo, wu, wd)
+            mid, n2, hidden, pre, d_own, d_other = up(ctx_a, ctx_b, wo[0], wu[0], parts, biases)
+            gmid, gctx_a, gctx_b, *u_packs = down(mid, n2, pre, ctx_a, ctx_b, wo[0], wu[0], parts, wd)
             gproj_b, *q_other = back(nn, proj_b, probs_b, gctx_b, side_b)
             gproj_a, *q_own = back(nn, proj_a, probs_a, gctx_a, side_a)
             input_grad = last(0, 1)(gmid, gproj_a, gproj_b, side_a, side_b, None)

time: 240 us -> 239 us (level)
  Pallas kernels: 188 us -> 185 us
    pallas_call x10, Pallas kernels: 162 us -> 160 us  [call(): pl.pallas_call(kernel, grid_spec=pltpu.PrefetchScalarGridSpec(num_scalar_...]
  transfers between devices with their start and end apart: 32 -> 32, of which waited for: 9 -> 8; matrix products, arithmetic and copies ran while one was open for 1% -> 1% of each run, Pallas kernels for 77% -> 77%
where the time goes in v5:
time: 239 us; the launch traced here: 238 us
  Pallas kernels  185 us (77%)
  starting transfers between devices  28.6 us (12%)
  waiting for transfers between devices  10.3 us (4%)
  local copies, waits for them, and re-layouts  7.57 us (3%)
  other arithmetic  4.98 us (2%)
    pallas_call x10, Pallas kernels, call(): pl.pallas_call(kernel, grid_spec=pltpu.PrefetchScalarGridSpec(num_scalar_...  160 us
    pallas_call x2, Pallas kernels, attention_forward(): pl.pallas_call(body, grid_spec=pltpu.PrefetchScalarGridSpec(num_scalar_pr...  25.1 us
    ppermute x23, starting transfers between devices, swap(): return lax.ppermute(v, 'dp', [(i, i ^ distance) for i in range(dp)])  17.6 us
    ppermute x8, starting transfers between devices, across(): return lax.ppermute(v, 'tensor', [(0, 1), (1, 0)])  11 us
    ppermute x23, waiting for transfers between devices, swap(): return lax.ppermute(v, 'dp', [(i, i ^ distance) for i in range(dp)])  9.3 us
  transfers between devices with their start and end apart: 32, of which 8 were waited for; matrix products, arithmetic and copies ran while one was open for 1% of the time, Pallas kernels for 77%

profile of v5, /device:TPU:0, one launch (start us, length us, event | category | flops | bytes accessed | tf_op | source)
XLA Modules:
  0.0 237.8 jit_solution(12017519517454694421)
XLA Ops:
  4.4 3.0 %collective-permute-start.1 = (f32[6,256]{1,0:T(8,128)S(1)}, f32[6,256]{1,0:T(8,128)S(1)}, u32[]{:S(2)}, u32[]{:S(2)}) collective-permute-start(f32[6,256]{1,0:T(8,128)S(1)} %pad_maximum_fusion.4.refs_3_.refs_14_), channel_id=1, source_target_pairs={{0,1},{1,0},{2,3},{3,2},{4,5},{5,4},{6,7},{7,6},{8,9},{9,8},{10,11... | collective-permute-start | bytes 18440 | tf_op jit(solution)/shard_map/ppermute | solution.py:750
  8.1 13.9 %attend_first.1 = (bf16[4096,512]{1,0:T(8,128)(2,1)}, bf16[4096,512]{1,0:T(8,128)(2,1)}, bf16[4096,768]{1,0:T(8,128)(2,1)}, bf16[4096,256]{1,0:T(8,128)(2,1)}, b...) custom-call(s32[44]{0:T(128)} %concatenate.25.refs_0_.scal, bf16[4096,512]{1,0:T(8,128)(2,1)} %refs_1_.6, ...), custom_call_target="tpu_custom_call" | custom-call | flops 3892314112 | bytes 16777216 | tf_op jit(solution)/shard_map/attend_first/pallas_call | solution.py:211
  22.3 1.7 collective-permute-done.2.refs_3_.refs_7_.wo_t
  24.0 1.9 collective-permute-start.3
  26.0 11.2 %attend_second.1 = (bf16[4096,768]{1,0:T(8,128)(2,1)}, bf16[4096,256]{1,0:T(8,128)(2,1)}, bf16[5120,256]{1,0:T(8,128)(2,1)}, bf16[512,768]{1,0:T(8,128)(2,1)}) custom-call(s32[44]{0:T(128)} %concatenate.25.refs_0_.scal, bf16[4096,512]{1,0:T(8,128)(2,1)} %get-tuple-element.223.refs_1_, bf16[1024,256]{1,0:T(8,128)(2,1)} %copy-done.9, ...), custom_call_target="tpu_custom_call" | custom-call | flops 3892314112 | bytes 16777216 | tf_op jit(solution)/shard_map/attend_second/pallas_call | solution.py:211
  38.2 1.9 collective-permute-done.4.refs_10_.wu_t
  40.1 1.7 collective-permute-start.5
  44.7 34.7 %feed_up.1 = (f32[4096,512]{1,0:T(8,128)}, bf16[4096,512]{1,0:T(8,128)(2,1)}, bf16[4096,2048]{1,0:T(8,128)(2,1)}, bf16[4096,2048]{1,0:T(8,128)(2,1)}, bf16[16,32...) custom-call(s32[44]{0:T(128)S(1)} %copy-done.5, bf16[4096,512]{1,0:T(8,128)(2,1)} %refs_1_.6, ...), custom_call_target="tpu_custom_call" | custom-call | flops 19327352832 | bytes 71303168 | tf_op jit(solution)/shard_map/feed_up/pallas_call | solution.py:342
  80.8 41.7 %feed_back.1 = (bf16[4096,512]{1,0:T(8,128)(2,1)}, bf16[4096,256]{1,0:T(8,128)(2,1)S(1)}, bf16[4096,256]{1,0:T(8,128)(2,1)}, bf16[8,32,1408]{2,1,0:T(8,128)(2,1)...) custom-call(s32[44]{0:T(128)S(1)} %copy-done.5, ...), custom_call_target="tpu_custom_call" | custom-call | flops 30064771072 | bytes 50331648 | tf_op jit(solution)/shard_map/feed_back/pallas_call | solution.py:342
  126.2 1.8 collective-permute-start.10
  128.0 1.6 collective-permute-start.11
  129.6 17.3 %attend_back.2 = (bf16[4096,768]{1,0:T(8,128)(2,1)}, bf16[8,32,896]{2,1,0:T(8,128)(2,1)}, bf16[8,32,896]{2,1,0:T(8,128)(2,1)}) custom-call(s32[44]{0:T(128)} %concatenate.25.refs_0_.scal, bf16[4096,512]{1,0:T(8,128)(2,1)} %get-tuple-element.307.refs_1_, bf16[4096,768]{1,0:T(8,128)(2,1)} %get-tuple-element.290.refs_2_, ...), custom_call_target="tpu_custom_call" | custom-call | flops 4563402752 | bytes 23068672 | tf_op jit(solution)/shard_map/attend_back/pallas_call | solution.py:342
  149.6 2.6 %collective-permute-start.14 = (bf16[4,32,1024]{2,1,0:T(8,128)(2,1)S(1)}, bf16[4,32,1024]{2,1,0:T(8,128)(2,1)S(1)}, u32[]{:S(2)}, u32[]{:S(2)}) collective-permute-start(bf16[4,32,1024]{2,1,0:T(8,128)(2,1)S(1)} %add_convert_fusion.9), channel_id=1, source_target_pairs={{0,16},{2,18},{4,20},{6,22},{8,24},{10,26},{12,28},{14,30},{16,0},... | collective-permute-start | bytes 786440 | tf_op jit(solution)/shard_map/ppermute | solution.py:753
  153.7 17.5 %attend_back.3 = (bf16[4096,768]{1,0:T(8,128)(2,1)}, bf16[8,32,896]{2,1,0:T(8,128)(2,1)}, bf16[8,32,896]{2,1,0:T(8,128)(2,1)}) custom-call(s32[44]{0:T(128)} %concatenate.25.refs_0_.scal, bf16[4096,512]{1,0:T(8,128)(2,1)} %get-tuple-element.307.refs_1_, bf16[4096,768]{1,0:T(8,128)(2,1)} %get-tuple-element.308.refs_2_, ...), custom_call_target="tpu_custom_call" | custom-call | flops 4563402752 | bytes 23068672 | tf_op jit(solution)/shard_map/attend_back/pallas_call | solution.py:342
  171.5 1.8 collective-permute-done.16
  174.9 1.6 collective-permute-start.19
  177.0 10.4 %input_gradient.2.refs_8_ = f32[4096,512]{1,0:T(8,128)} custom-call(s32[44]{0:T(128)} %concatenate.25.refs_0_.scal, bf16[4096,512]{1,0:T(8,128)(2,1)} %refs_1_.6, bf16[4096,512]{1,0:T(8,128)(2,1)} %get-tuple-element.338.refs_2_, bf16[4096,768]{1,0:T(8,128)(2,1)} %get-tuple-element.339.refs_3_, bf16[4096,768]{1,0:T(8,128)(2,1)} %get-tuple-element.340.refs_4_, ...), custom_call_target="tpu_custom_call" | custom-call | flops 3221225472 | bytes 16777216 | tf_op jit(solution)/shard_map/input_gradient/pallas_call | solution.py:342
  190.0 10.4 %input_gradient.3 = f32[4096,512]{1,0:T(8,128)} custom-call(s32[44]{0:T(128)} %concatenate.25.refs_0_.scal, bf16[4096,512]{1,0:T(8,128)(2,1)} %refs_1_.6, bf16[4096,512]{1,0:T(8,128)(2,1)} %get-tuple-element.338.refs_2_, bf16[4096,768]{1,0:T(8,128)(2,1)} %get-tuple-element.339.refs_3_, ...), custom_call_target="tpu_custom_call", output_to_operand_aliasing={{}: (8, {})} | custom-call | flops 3221225472 | bytes 16777216 | tf_op jit(solution)/shard_map/input_gradient/pallas_call | solution.py:342
  200.7 1.6 collective-permute-start.23
  202.3 2.6 %collective-permute-start.25 = (bf16[4,32,896]{2,1,0:T(8,128)(2,1)S(1)}, bf16[4,32,896]{2,1,0:T(8,128)(2,1)S(1)}, u32[]{:S(2)}, u32[]{:S(2)}) collective-permute-start(bf16[4,32,896]{2,1,0:T(8,128)(2,1)S(1)} %add_convert_fusion.11), channel_id=1, source_target_pairs={{0,16},{2,18},{4,20},{6,22},{8,24},{10,26},{12,28},{14,30},{16,0},... | collective-permute-start | bytes 688136 | tf_op jit(solution)/shard_map/ppermute | solution.py:753
  204.9 12.0 %layer_out.3.before = bf16[4096,512]{1,0:T(8,128)(2,1)} custom-call(s32[44]{0:T(128)} %concatenate.25.refs_0_.scal, f32[4096,512]{1,0:T(8,128)} %get-tuple-element.375.mid, bf16[4096,2048]{1,0:T(8,128)(2,1)} %get-tuple-element.376.hidden, bf16[1024,512]{1,0:T(8,128)(2,1)} %wd_a.3, bf16[1024,512]{1,0:T(8,128)(2,1)} %copy-done.1, f32[1,512]{1,0:T(1,128)} %bitcast.39), custom_call_target="tpu_custom_call" | custom-call | flops 5368709120 | bytes 18350080 | tf_op jit(solution)/shard_map/layer_out/pallas_call | solution.py:342
  218.1 7.9 %layer_out.4 = (bf16[4096,512]{1,0:T(8,128)(2,1)}, f32[1024,512]{1,0:T(8,128)}) custom-call(s32[44]{0:T(128)} %concatenate.25.refs_0_.scal, f32[4096,512]{1,0:T(8,128)} %get-tuple-element.375.mid, bf16[4096,2048]{1,0:T(8,128)(2,1)} %get-tuple-element.376.hidden, bf16[1024,512]{1,0:T(8,128)(2,1)} %wd_a.3, ...), custom_call_target="tpu_custom_call", output_to_operand_aliasing={{0}: (6, {})} | custom-call | flops 2147483648 | bytes 7340032 | tf_op jit(solution)/shard_map/layer_out/pallas_call | solution.py:342
  229.6 5.2 %layer_out.5 = bf16[4096,512]{1,0:T(8,128)(2,1)} custom-call(s32[44]{0:T(128)} %concatenate.25.refs_0_.scal, f32[4096,512]{1,0:T(8,128)} %get-tuple-element.375.mid, bf16[4096,2048]{1,0:T(8,128)(2,1)} %get-tuple-element.376.hidden, bf16[1024,512]{1,0:T(8,128)(2,1)} %wd_a.3, bf16[1024,512]{1,0:T(8,128)(2,1)} %copy-done.1, ...), custom_call_target="tpu_custom_call", output_to_operand_aliasing={{}: (6, {})} | custom-call | flops 1073741824 | bytes 3670016 | tf_op jit(solution)/shard_map/layer_out/pallas_call | solution.py:342
  234.9 2.9 %unpack.1 = (f32[512,1024]{1,0:T(8,128)}, f32[256,512]{1,0:T(8,128)}, f32[1,512]{1,0:T(1,128)}, f32[1,512]{1,0:T(1,128)}, f32[1,512]{1,0:T(1,128)}, /*index=5*/f...) custom-call(s32[44]{0:T(128)S(1)} %copy-done.6, ...), custom_call_target="tpu_custom_call" | custom-call | bytes 7471104 | tf_op jit(solution)/shard_map/unpack/pallas_call | solution.py:342
  (144 shorter events, 27.5 us)
Async XLA Ops:
  4.4 17.6 %collective-permute-start.1 = (f32[6,256]{1,0:T(8,128)S(1)}, f32[6,256]{1,0:T(8,128)S(1)}, u32[]{:S(2)}, u32[]{:S(2)}) collective-permute-start(f32[6,256]{1,0:T(8,128)S(1)} %pad_maximum_fusion.4.refs_3_.refs_14_), channel_id=1, source_target_pairs={{0,1},{1,0},{2,3},{3,2},{4,5},{5,4},{6,7},{7,6},{8,9},{9,8},{10,11... | collective-permute-start | bytes 18440 | tf_op jit(solution)/shard_map/ppermute | solution.py:750
  7.4 14.6 %collective-permute-start = (bf16[1024,256]{1,0:T(8,128)(2,1)S(1)}, bf16[1024,256]{1,0:T(8,128)(2,1)S(1)}, u32[]{:S(2)}, u32[]{:S(2)}) collective-permute-start(bf16[1024,256]{1,0:T(8,128)(2,1)S(1)} %maximum_select_fusion), channel_id=1, source_target_pairs={{0,1},{1,0},{2,3},{3,2},{4,5},{5,4},{6,7},{7,6},{8,9},{9,8},{10,11... | collective-permute-start | bytes 1572872 | tf_op jit(solution)/shard_map/ppermute | solution.py:750
  24.0 14.2 %collective-permute-start.3 = (bf16[256,1024]{1,0:T(8,128)(2,1)S(1)}, bf16[256,1024]{1,0:T(8,128)(2,1)S(1)}, u32[]{:S(2)}, u32[]{:S(2)}) collective-permute-start(bf16[256,1024]{1,0:T(8,128)(2,1)S(1)} %constant_dynamic-slice_fusion), channel_id=1, source_target_pairs={{0,1},{1,0},{2,3},{3,2},{4,5},{5,4},{6,7},{7,6},{8,9},{9,8},{10,11... | collective-permute-start | bytes 1572872 | tf_op jit(solution)/shard_map/ppermute | solution.py:750
  40.1 39.3 %collective-permute-start.5 = (bf16[1024,512]{1,0:T(8,128)(2,1)S(1)}, bf16[1024,512]{1,0:T(8,128)(2,1)S(1)}, u32[]{:S(2)}, u32[]{:S(2)}) collective-permute-start(bf16[1024,512]{1,0:T(8,128)(2,1)S(1)} %copy-done), channel_id=1, source_target_pairs={{0,1},{1,0},{2,3},{3,2},{4,5},{5,4},{6,7},{7,6},{8,9},{9,8},{10,11... | collective-permute-start | bytes 3145736 | tf_op jit(solution)/shard_map/ppermute | solution.py:750
  79.4 43.1 %collective-permute-start.6 = (bf16[16,32,1024]{2,1,0:T(8,128)(2,1)S(1)}, bf16[16,32,1024]{2,1,0:T(8,128)(2,1)S(1)}, u32[]{:S(2)}, u32[]{:S(2)}) collective-permute-start(bf16[16,32,1024]{2,1,0:T(8,128)(2,1)S(1)} %get-tuple-element.277), channel_id=1, source_target_pairs={{0,1},{1,0},{2,3},{3,2},{4,5},{5,4},{6,7},{7,6},{8,9},{9,8},{10,11... | collective-permute-start | bytes 3145736 | tf_op jit(solution)/shard_map/ppermute | solution.py:750
  126.2 20.7 %collective-permute-start.10 = (bf16[8,32,1408]{2,1,0:T(8,128)(2,1)S(1)}, bf16[8,32,1408]{2,1,0:T(8,128)(2,1)S(1)}, u32[]{:S(2)}, u32[]{:S(2)}) collective-permute-start(bf16[8,32,1408]{2,1,0:T(8,128)(2,1)S(1)} %add_convert_fusion.2), channel_id=1, source_target_pairs={{0,1},{1,0},{2,3},{3,2},{4,5},{5,4},{6,7},{7,6},{8,9},{9,8},{10,11... | collective-permute-start | bytes 2162696 | tf_op jit(solution)/shard_map/ppermute | solution.py:750
  128.0 19.2 %collective-permute-start.7 = (bf16[8,32,1408]{2,1,0:T(8,128)(2,1)S(1)}, bf16[8,32,1408]{2,1,0:T(8,128)(2,1)}, u32[]{:S(2)}, u32[]{:S(2)}) collective-permute-start(bf16[8,32,1408]{2,1,0:T(8,128)(2,1)S(1)} %get-tuple-element.279), channel_id=1, source_target_pairs={{0,2},{2,0},{4,6},{6,4},{8,10},{10,8},{12,14},{14,12},{16,18},{18,... | collective-permute-start | bytes 2162696 | tf_op jit(solution)/shard_map/ppermute | solution.py:753
  128.0 18.8 %collective-permute-start.11 = (bf16[4,32,1024]{2,1,0:T(8,128)(2,1)S(1)}, bf16[4,32,1024]{2,1,0:T(8,128)(2,1)S(1)}, u32[]{:S(2)}, u32[]{:S(2)}) collective-permute-start(bf16[4,32,1024]{2,1,0:T(8,128)(2,1)S(1)} %slice.86), channel_id=1, source_target_pairs={{0,8},{2,10},{4,12},{6,14},{8,0},{10,2},{12,4},{14,6},{16,24},{18,... | collective-permute-start | bytes 786440 | tf_op jit(solution)/shard_map/ppermute | solution.py:753
  149.1 22.1 %collective-permute-start.15 = (bf16[8,32,896]{2,1,0:T(8,128)(2,1)S(1)}, bf16[8,32,896]{2,1,0:T(8,128)(2,1)S(1)}, u32[]{:S(2)}, u32[]{:S(2)}) collective-permute-start(bf16[8,32,896]{2,1,0:T(8,128)(2,1)S(1)} %add_convert_fusion.5), channel_id=1, source_target_pairs={{0,1},{1,0},{2,3},{3,2},{4,5},{5,4},{6,7},{7,6},{8,9},{9,8},{10,11... | collective-permute-start | bytes 1376264 | tf_op jit(solution)/shard_map/ppermute | solution.py:750
  149.6 21.6 %collective-permute-start.14 = (bf16[4,32,1024]{2,1,0:T(8,128)(2,1)S(1)}, bf16[4,32,1024]{2,1,0:T(8,128)(2,1)S(1)}, u32[]{:S(2)}, u32[]{:S(2)}) collective-permute-start(bf16[4,32,1024]{2,1,0:T(8,128)(2,1)S(1)} %add_convert_fusion.9), channel_id=1, source_target_pairs={{0,16},{2,18},{4,20},{6,22},{8,24},{10,26},{12,28},{14,30},{16,0},... | collective-permute-start | bytes 786440 | tf_op jit(solution)/shard_map/ppermute | solution.py:753
  152.2 19.0 %collective-permute-start.13 = (bf16[4,32,1408]{2,1,0:T(8,128)(2,1)S(1)}, bf16[4,32,1408]{2,1,0:T(8,128)(2,1)S(1)}, u32[]{:S(2)}, u32[]{:S(2)}) collective-permute-start(bf16[4,32,1408]{2,1,0:T(8,128)(2,1)S(1)} %slice.88), channel_id=1, source_target_pairs={{0,4},{2,6},{4,0},{6,2},{8,12},{10,14},{12,8},{14,10},{16,20},{18,... | collective-permute-start | bytes 1081352 | tf_op jit(solution)/shard_map/ppermute | solution.py:753
  174.4 13.0 %collective-permute-start.17 = (bf16[2,32,1408]{2,1,0:T(8,128)(2,1)S(1)}, bf16[2,32,1408]{2,1,0:T(8,128)(2,1)S(1)}, u32[]{:S(2)}, u32[]{:S(2)}) collective-permute-start(bf16[2,32,1408]{2,1,0:T(8,128)(2,1)S(1)} %slice.91), channel_id=1, source_target_pairs={{0,8},{2,10},{4,12},{6,14},{8,0},{10,2},{12,4},{14,6},{16,24},{18,... | collective-permute-start | bytes 540680 | tf_op jit(solution)/shard_map/ppermute | solution.py:753
  174.9 12.5 %collective-permute-start.19 = (bf16[4,32,896]{2,1,0:T(8,128)(2,1)S(1)}, bf16[4,32,896]{2,1,0:T(8,128)(2,1)S(1)}, u32[]{:S(2)}, u32[]{:S(2)}) collective-permute-start(bf16[4,32,896]{2,1,0:T(8,128)(2,1)S(1)} %add_convert_fusion.13), channel_id=1, source_target_pairs={{0,8},{2,10},{4,12},{6,14},{8,0},{10,2},{12,4},{14,6},{16,24},{18,... | collective-permute-start | bytes 688136 | tf_op jit(solution)/shard_map/ppermute | solution.py:753
  176.4 10.9 %collective-permute-start.18 = (bf16[4,32,1024]{2,1,0:T(8,128)(2,1)S(1)}, bf16[4,32,1024]{2,1,0:T(8,128)(2,1)S(1)}, u32[]{:S(2)}, u32[]{:S(2)}) collective-permute-start(bf16[4,32,1024]{2,1,0:T(8,128)(2,1)S(1)} %add_convert_fusion.8), channel_id=1, source_target_pairs={{0,4},{2,6},{4,0},{6,2},{8,12},{10,14},{12,8},{14,10},{16,20},{18,... | collective-permute-start | bytes 786440 | tf_op jit(solution)/shard_map/ppermute | solution.py:753
  187.6 12.7 %collective-permute-start.20 = (bf16[2,32,1408]{2,1,0:T(8,128)(2,1)S(1)}, bf16[2,32,1408]{2,1,0:T(8,128)(2,1)S(1)}, u32[]{:S(2)}, u32[]{:S(2)}) collective-permute-start(bf16[2,32,1408]{2,1,0:T(8,128)(2,1)S(1)} %add_convert_fusion.15), channel_id=1, source_target_pairs={{0,16},{2,18},{4,20},{6,22},{8,24},{10,26},{12,28},{14,30},{16,0},... | collective-permute-start | bytes 540680 | tf_op jit(solution)/shard_map/ppermute | solution.py:753
  188.0 12.3 %collective-permute-start.22 = (bf16[4,32,896]{2,1,0:T(8,128)(2,1)S(1)}, bf16[4,32,896]{2,1,0:T(8,128)(2,1)S(1)}, u32[]{:S(2)}, u32[]{:S(2)}) collective-permute-start(bf16[4,32,896]{2,1,0:T(8,128)(2,1)S(1)} %add_convert_fusion.12), channel_id=1, source_target_pairs={{0,4},{2,6},{4,0},{6,2},{8,12},{10,14},{12,8},{14,10},{16,20},{18,... | collective-permute-start | bytes 688136 | tf_op jit(solution)/shard_map/ppermute | solution.py:753
  189.5 10.9 %collective-permute-start.21 = (bf16[4,32,1024]{2,1,0:T(8,128)(2,1)S(1)}, bf16[4,32,1024]{2,1,0:T(8,128)(2,1)S(1)}, u32[]{:S(2)}, u32[]{:S(2)}) collective-permute-start(bf16[4,32,1024]{2,1,0:T(8,128)(2,1)S(1)} %add_convert_fusion.7), channel_id=1, source_target_pairs={{0,8},{2,10},{4,12},{6,14},{8,0},{10,2},{12,4},{14,6},{16,24},{18,... | collective-permute-start | bytes 786440 | tf_op jit(solution)/shard_map/ppermute | solution.py:753
  200.6 16.3 %collective-permute-start.24 = (bf16[8,32,1024]{2,1,0:T(8,128)(2,1)S(1)}, bf16[8,32,1024]{2,1,0:T(8,128)(2,1)S(1)}, u32[]{:S(2)}, u32[]{:S(2)}) collective-permute-start(bf16[8,32,1024]{2,1,0:T(8,128)(2,1)S(1)} %pad_maximum_fusion.1.d0), channel_id=1, source_target_pairs={{0,2},{2,0},{4,6},{6,4},{8,10},{10,8},{12,14},{14,12},{16,18},{18,... | collective-permute-start | bytes 1572872 | tf_op jit(solution)/shard_map/ppermute | solution.py:753
  200.7 16.2 %collective-permute-start.23 = (bf16[2,32,1408]{2,1,0:T(8,128)(2,1)S(1)}, bf16[2,32,1408]{2,1,0:T(8,128)(2,1)S(1)}, u32[]{:S(2)}, u32[]{:S(2)}) collective-permute-start(bf16[2,32,1408]{2,1,0:T(8,128)(2,1)S(1)} %add_convert_fusion.14), channel_id=1, source_target_pairs={{0,8},{2,10},{4,12},{6,14},{8,0},{10,2},{12,4},{14,6},{16,24},{18,... | collective-permute-start | bytes 540680 | tf_op jit(solution)/shard_map/ppermute | solution.py:753
  202.3 14.6 %collective-permute-start.25 = (bf16[4,32,896]{2,1,0:T(8,128)(2,1)S(1)}, bf16[4,32,896]{2,1,0:T(8,128)(2,1)S(1)}, u32[]{:S(2)}, u32[]{:S(2)}) collective-permute-start(bf16[4,32,896]{2,1,0:T(8,128)(2,1)S(1)} %add_convert_fusion.11), channel_id=1, source_target_pairs={{0,16},{2,18},{4,20},{6,22},{8,24},{10,26},{12,28},{14,30},{16,0},... | collective-permute-start | bytes 688136 | tf_op jit(solution)/shard_map/ppermute | solution.py:753
  217.1 10.3 %collective-permute-start.26 = (bf16[4,32,1408]{2,1,0:T(8,128)(2,1)S(1)}, bf16[4,32,1408]{2,1,0:T(8,128)(2,1)S(1)}, u32[]{:S(2)}, u32[]{:S(2)}) collective-permute-start(bf16[4,32,1408]{2,1,0:T(8,128)(2,1)S(1)} %pad_maximum_fusion.3), channel_id=1, source_target_pairs={{0,4},{2,6},{4,0},{6,2},{8,12},{10,14},{12,8},{14,10},{16,20},{18,... | collective-permute-start | bytes 1081352 | tf_op jit(solution)/shard_map/ppermute | solution.py:753
  217.7 8.4 %collective-permute-start.27 = (bf16[4,32,896]{2,1,0:T(8,128)(2,1)S(1)}, bf16[4,32,896]{2,1,0:T(8,128)(2,1)S(1)}, u32[]{:S(2)}, u32[]{:S(2)}) collective-permute-start(bf16[4,32,896]{2,1,0:T(8,128)(2,1)S(1)} %add_convert_fusion.10), channel_id=1, source_target_pairs={{0,8},{2,10},{4,12},{6,14},{8,0},{10,2},{12,4},{14,6},{16,24},{18,... | collective-permute-start | bytes 688136 | tf_op jit(solution)/shard_map/ppermute | solution.py:753
  227.5 7.3 %collective-permute-start.28 = (bf16[8,32,1408]{2,1,0:T(8,128)(2,1)S(1)}, bf16[8,32,1408]{2,1,0:T(8,128)(2,1)S(1)}, u32[]{:S(2)}, u32[]{:S(2)}) collective-permute-start(bf16[8,32,1408]{2,1,0:T(8,128)(2,1)S(1)} %pad_maximum_fusion.u0), channel_id=1, source_target_pairs={{0,2},{2,0},{4,6},{6,4},{8,10},{10,8},{12,14},{14,12},{16,18},{18,... | collective-permute-start | bytes 2162696 | tf_op jit(solution)/shard_map/ppermute | solution.py:753
  227.6 7.2 %collective-permute-start.29 = (bf16[8,32,896]{2,1,0:T(8,128)(2,1)S(1)}, bf16[8,32,896]{2,1,0:T(8,128)(2,1)S(1)}, u32[]{:S(2)}, u32[]{:S(2)}) collective-permute-start(bf16[8,32,896]{2,1,0:T(8,128)(2,1)S(1)} %pad_maximum_fusion.2.q0), channel_id=1, source_target_pairs={{0,2},{2,0},{4,6},{6,4},{8,10},{10,8},{12,14},{14,12},{16,18},{18,... | collective-permute-start | bytes 1376264 | tf_op jit(solution)/shard_map/ppermute | solution.py:753
  (38 other events, 445.1 us)

commit v6 on v5

--- a/solution.py
+++ b/solution.py
@@ -269,12 +269,6 @@
     acc[:rows, first:] = jnp.concatenate(vectors + [jnp.zeros((spare, rows), F32)], axis=0).T
 
 
-def bias_chunk(biases, first, count):
-    width = biases.shape[1]
-    rows = range(2 + first // width, 2 + (first + count) // width)
-    return jnp.concatenate([biases[r : r + 1, :] for r in rows], axis=1)
-
-
 def assemble(scal, wo_a, wo_m, wo_t, wu_m, wu_t, wo_s, wu_b):
     width, side, rows = wo_a.shape[0], wo_m.shape[1], wu_m.shape[0]
     wo_s[:width, :] = wo_a[...]
@@ -322,7 +316,7 @@
     for n, (part, c) in enumerate(chunks):
         if n + 1 < len(chunks):
             up(n + 1)
-        bias = bias_chunk((bias_a, bias_b)[part], c * FC, FC) * 0.5
+        bias = (bias_a, bias_b)[part][:, c * FC : (c + 1) * FC] * 0.5
         ts = slice(part * half + c * FC, part * half + (c + 1) * FC)
         for sub in subs(rows):
             v = pres[n % 2][sub, :] + bias
@@ -792,10 +786,9 @@
             label = ((index & 1) << 3) | ((index & 2) << 1) | ((index & 4) >> 1)
             label_q = ((index & 1) << 3) | (index & 4)
         place_here = jnp.stack([label, label_q, here, index & 1 if paired else jnp.int32(0)]).astype(jnp.int32)
-        ends = [span[:, k] for span in (time_span, freq_span) for k in range(2)]
+        ends = [span.T.reshape(-1) for span in (time_span, freq_span)]
         scal = jnp.concatenate([place_here, lengths, *ends])
         row = lambda v: v.reshape(1, -1)
-        stack_biases = lambda b, u: jnp.concatenate([b, u.reshape(-1, b.shape[1])], axis=0)
 
         def attend_a(rows, w, bias):
             return attention_forward(True, scal, rows, w, bias, row(gain_one), row(shift_one))
@@ -833,7 +826,6 @@
                 rows = v.shape[0] // 2
                 return lax.dynamic_slice_in_dim(v, odd * rows, rows, 0)
 
-            biases = stack_biases(qkv_bias, up_bias)
             qkv_a = turned(qkv_weight)
             side = d // 2
             low, high = qkv_a.reshape(2, -1, side)
@@ -842,16 +834,16 @@
                 jnp.concatenate([low, out_weight[:, :side]], axis=0),
                 jnp.concatenate([high, out_weight[:, side:]], axis=0),
             )
-            (nn, n1, proj_a, ctx_a, probs_a, side_a), (first_half, biases_b), _ = window(
-                attend_a, (inputs, qkv_a, biases), [(first_rows, across), (biases, across)]
+            (nn, n1, proj_a, ctx_a, probs_a, side_a), (first_half, bias_b), _ = window(
+                attend_a, (inputs, qkv_a, qkv_bias), [(first_rows, across), (qkv_bias, across)]
             )
             first_pair = (first_half, core(first_half))
-            (proj_b, ctx_b, probs_b, side_b), (up_half,), _ = window(
-                attend_b, (n1, first_pair, biases_b), [(part_of(up_weight), across)]
+            (proj_b, ctx_b, probs_b, side_b), (up_half, up_bias_b), _ = window(
+                attend_b, (n1, first_pair, bias_b), [(part_of(up_weight), across), (row(up_bias), across)]
             )
             pairs = (first_pair, (up_half, core(up_half)))
             (mid, n2, hidden, pre, d_own, d_other), (down_b,), _ = window(
-                up, (ctx_a, ctx_b, out_weight, up_weight, pairs, (biases, biases_b)), [(down_weight, across)]
+                up, (ctx_a, ctx_b, out_weight, up_weight, pairs, (row(up_bias), up_bias_b)), [(down_weight, across)]
             )
             wd = (down_weight, down_b)
             (gmid, gctx_a, gctx_b, u_own, u_other, u_send_own, u_send_other), (d_cross,), _ = window(
@@ -925,13 +917,14 @@
 
             natural = lambda *packs: jnp.concatenate(packs, axis=0).reshape(d, -1)
             qkv = [turned(w) for w in halves(qkv_weight, 2)]
-            biases = [stack_biases(q, u) for q, u in zip(halves(qkv_bias, 1), halves(up_bias, 0))]
+            biases = halves(qkv_bias, 1)
+            up_biases = [row(b) for b in halves(up_bias, 0)]
             wo, wu, wd = halves(out_weight, 0), halves(up_weight, 1), halves(down_weight, 0)
             nn, n1, proj_a, ctx_a, probs_a, side_a = attend_a(inputs, qkv[0], biases[0])
             halves_b = jnp.split(qkv[1].reshape(-1, qkv[1].shape[2]), 2, axis=0)
             proj_b, ctx_b, probs_b, side_b = attend_b(n1, halves_b, biases[1])
             parts = (jnp.split(wo[1], 2, axis=1), jnp.split(wu[1], 2, axis=0))
-            mid, n2, hidden, pre, d_own, d_other = up(ctx_a, ctx_b, wo[0], wu[0], parts, biases)
+            mid, n2, hidden, pre, d_own, d_other = up(ctx_a, ctx_b, wo[0], wu[0], parts, up_biases)
             gmid, gctx_a, gctx_b, *u_packs = down(mid, n2, pre, ctx_a, ctx_b, wo[0], wu[0], parts, wd)
             gproj_b, *q_other = back(nn, proj_b, probs_b, gctx_b, side_b)
             gproj_a, *q_own = back(nn, proj_a, probs_a, gctx_a, side_a)

time: 239 us -> 237 us (level)
    ppermute x8 -> x9, starting transfers between devices: 11 us -> 11.2 us  [across(): return lax.ppermute(v, 'tensor', [(0, 1), (1, 0)])]
  transfers between devices with their start and end apart: 32 -> 33, of which waited for: 8 -> 8; matrix products, arithmetic and copies ran while one was open for 1% -> 1% of each run, Pallas kernels for 77% -> 77%
where the time goes in v6:
time: 237 us; the launch traced here: 236 us
  Pallas kernels  185 us (78%)
  starting transfers between devices  28.7 us (12%)
  waiting for transfers between devices  10.4 us (4%)
  local copies, waits for them, and re-layouts  6.33 us (3%)
  other arithmetic  4.29 us (2%)
    pallas_call x10, Pallas kernels, call(): pl.pallas_call(kernel, grid_spec=pltpu.PrefetchScalarGridSpec(num_scalar_...  160 us
    pallas_call x2, Pallas kernels, attention_forward(): pl.pallas_call(body, grid_spec=pltpu.PrefetchScalarGridSpec(num_scalar_pr...  25.1 us
    ppermute x23, starting transfers between devices, swap(): return lax.ppermute(v, 'dp', [(i, i ^ distance) for i in range(dp)])  17.6 us
    ppermute x9, starting transfers between devices, across(): return lax.ppermute(v, 'tensor', [(0, 1), (1, 0)])  11.2 us
    ppermute x23, waiting for transfers between devices, swap(): return lax.ppermute(v, 'dp', [(i, i ^ distance) for i in range(dp)])  9.38 us
  transfers between devices with their start and end apart: 33, of which 8 were waited for; matrix products, arithmetic and copies ran while one was open for 1% of the time, Pallas kernels for 77%

profile of v6, /device:TPU:0, one launch (start us, length us, event | category | flops | bytes accessed | tf_op | source)
XLA Modules:
  0.0 236.0 jit_solution(2245125074400952804)
XLA Ops:
  3.0 3.0 %collective-permute-start = (bf16[1024,256]{1,0:T(8,128)(2,1)S(1)}, bf16[1024,256]{1,0:T(8,128)(2,1)S(1)}, u32[]{:S(2)}, u32[]{:S(2)}) collective-permute-start(bf16[1024,256]{1,0:T(8,128)(2,1)S(1)} %maximum_select_fusion), channel_id=1, source_target_pairs={{0,1},{1,0},{2,3},{3,2},{4,5},{5,4},{6,7},{7,6},{8,9},{9,8},{10,11... | collective-permute-start | bytes 1572872 | tf_op jit(solution)/shard_map/ppermute | solution.py:744
  6.9 13.9 %attend_first.1 = (bf16[4096,512]{1,0:T(8,128)(2,1)}, bf16[4096,512]{1,0:T(8,128)(2,1)}, bf16[4096,768]{1,0:T(8,128)(2,1)}, bf16[4096,256]{1,0:T(8,128)(2,1)}, b...) custom-call(s32[44]{0:T(128)} %concatenate.22.refs_0_.scal, bf16[4096,512]{1,0:T(8,128)(2,1)} %refs_1_.6, ...), custom_call_target="tpu_custom_call" | custom-call | flops 3892314112 | bytes 16777216 | tf_op jit(solution)/shard_map/attend_first/pallas_call | solution.py:211
  21.0 1.8 collective-permute-done.2.refs_3_.refs_7_.wo_t
  22.9 2.0 collective-permute-start.3
  25.0 11.2 %attend_second.1 = (bf16[4096,768]{1,0:T(8,128)(2,1)}, bf16[4096,256]{1,0:T(8,128)(2,1)}, bf16[5120,256]{1,0:T(8,128)(2,1)}, bf16[512,768]{1,0:T(8,128)(2,1)}) custom-call(s32[44]{0:T(128)} %concatenate.22.refs_0_.scal, bf16[4096,512]{1,0:T(8,128)(2,1)} %get-tuple-element.225.refs_1_, bf16[1024,256]{1,0:T(8,128)(2,1)} %copy-done.7, ...), custom_call_target="tpu_custom_call" | custom-call | flops 3892314112 | bytes 16777216 | tf_op jit(solution)/shard_map/attend_second/pallas_call | solution.py:211
  37.2 1.9 collective-permute-done.5.refs_10_.wu_t
  39.1 1.7 collective-permute-start.6
  43.0 34.6 %feed_up.1 = (f32[4096,512]{1,0:T(8,128)}, bf16[4096,512]{1,0:T(8,128)(2,1)}, bf16[4096,2048]{1,0:T(8,128)(2,1)}, bf16[4096,2048]{1,0:T(8,128)(2,1)}, bf16[16,32...) custom-call(s32[44]{0:T(128)S(1)} %copy-done.5, bf16[4096,512]{1,0:T(8,128)(2,1)} %refs_1_.6, ...), custom_call_target="tpu_custom_call" | custom-call | flops 19327352832 | bytes 71303168 | tf_op jit(solution)/shard_map/feed_up/pallas_call | solution.py:336
  79.0 41.7 %feed_back.1 = (bf16[4096,512]{1,0:T(8,128)(2,1)}, bf16[4096,256]{1,0:T(8,128)(2,1)S(1)}, bf16[4096,256]{1,0:T(8,128)(2,1)}, bf16[8,32,1408]{2,1,0:T(8,128)(2,1)...) custom-call(s32[44]{0:T(128)S(1)} %copy-done.5, ...), custom_call_target="tpu_custom_call" | custom-call | flops 30064771072 | bytes 50331648 | tf_op jit(solution)/shard_map/feed_back/pallas_call | solution.py:336
  124.4 1.8 collective-permute-start.11
  126.2 1.6 collective-permute-start.12
  127.8 17.3 %attend_back.2 = (bf16[4096,768]{1,0:T(8,128)(2,1)}, bf16[8,32,896]{2,1,0:T(8,128)(2,1)}, bf16[8,32,896]{2,1,0:T(8,128)(2,1)}) custom-call(s32[44]{0:T(128)} %concatenate.22.refs_0_.scal, bf16[4096,512]{1,0:T(8,128)(2,1)} %get-tuple-element.311.refs_1_, bf16[4096,768]{1,0:T(8,128)(2,1)} %get-tuple-element.294.refs_2_, ...), custom_call_target="tpu_custom_call" | custom-call | flops 4563402752 | bytes 23068672 | tf_op jit(solution)/shard_map/attend_back/pallas_call | solution.py:336
  147.8 2.6 %collective-permute-start.15 = (bf16[4,32,1024]{2,1,0:T(8,128)(2,1)S(1)}, bf16[4,32,1024]{2,1,0:T(8,128)(2,1)S(1)}, u32[]{:S(2)}, u32[]{:S(2)}) collective-permute-start(bf16[4,32,1024]{2,1,0:T(8,128)(2,1)S(1)} %add_convert_fusion.9), channel_id=1, source_target_pairs={{0,16},{2,18},{4,20},{6,22},{8,24},{10,26},{12,28},{14,30},{16,0},... | collective-permute-start | bytes 786440 | tf_op jit(solution)/shard_map/ppermute | solution.py:747
  151.9 17.5 %attend_back.3 = (bf16[4096,768]{1,0:T(8,128)(2,1)}, bf16[8,32,896]{2,1,0:T(8,128)(2,1)}, bf16[8,32,896]{2,1,0:T(8,128)(2,1)}) custom-call(s32[44]{0:T(128)} %concatenate.22.refs_0_.scal, bf16[4096,512]{1,0:T(8,128)(2,1)} %get-tuple-element.311.refs_1_, bf16[4096,768]{1,0:T(8,128)(2,1)} %get-tuple-element.312.refs_2_, ...), custom_call_target="tpu_custom_call" | custom-call | flops 4563402752 | bytes 23068672 | tf_op jit(solution)/shard_map/attend_back/pallas_call | solution.py:336
  169.7 1.8 collective-permute-done.17
  173.1 1.6 collective-permute-start.20
  175.2 10.4 %input_gradient.2.refs_8_ = f32[4096,512]{1,0:T(8,128)} custom-call(s32[44]{0:T(128)} %concatenate.22.refs_0_.scal, bf16[4096,512]{1,0:T(8,128)(2,1)} %refs_1_.6, bf16[4096,512]{1,0:T(8,128)(2,1)} %get-tuple-element.342.refs_2_, bf16[4096,768]{1,0:T(8,128)(2,1)} %get-tuple-element.343.refs_3_, bf16[4096,768]{1,0:T(8,128)(2,1)} %get-tuple-element.344.refs_4_, ...), custom_call_target="tpu_custom_call" | custom-call | flops 3221225472 | bytes 16777216 | tf_op jit(solution)/shard_map/input_gradient/pallas_call | solution.py:336
  188.2 10.4 %input_gradient.3 = f32[4096,512]{1,0:T(8,128)} custom-call(s32[44]{0:T(128)} %concatenate.22.refs_0_.scal, bf16[4096,512]{1,0:T(8,128)(2,1)} %refs_1_.6, bf16[4096,512]{1,0:T(8,128)(2,1)} %get-tuple-element.342.refs_2_, bf16[4096,768]{1,0:T(8,128)(2,1)} %get-tuple-element.343.refs_3_, ...), custom_call_target="tpu_custom_call", output_to_operand_aliasing={{}: (8, {})} | custom-call | flops 3221225472 | bytes 16777216 | tf_op jit(solution)/shard_map/input_gradient/pallas_call | solution.py:336
  198.9 1.7 collective-permute-start.24
  200.5 2.6 %collective-permute-start.26 = (bf16[4,32,896]{2,1,0:T(8,128)(2,1)S(1)}, bf16[4,32,896]{2,1,0:T(8,128)(2,1)S(1)}, u32[]{:S(2)}, u32[]{:S(2)}) collective-permute-start(bf16[4,32,896]{2,1,0:T(8,128)(2,1)S(1)} %add_convert_fusion.11), channel_id=1, source_target_pairs={{0,16},{2,18},{4,20},{6,22},{8,24},{10,26},{12,28},{14,30},{16,0},... | collective-permute-start | bytes 688136 | tf_op jit(solution)/shard_map/ppermute | solution.py:747
  203.1 12.0 %layer_out.3.before = bf16[4096,512]{1,0:T(8,128)(2,1)} custom-call(s32[44]{0:T(128)} %concatenate.22.refs_0_.scal, f32[4096,512]{1,0:T(8,128)} %get-tuple-element.379.mid, bf16[4096,2048]{1,0:T(8,128)(2,1)} %get-tuple-element.380.hidden, bf16[1024,512]{1,0:T(8,128)(2,1)} %wd_a.3, bf16[1024,512]{1,0:T(8,128)(2,1)} %copy-done.1, f32[1,512]{1,0:T(1,128)} %bitcast.36), custom_call_target="tpu_custom_call" | custom-call | flops 5368709120 | bytes 18350080 | tf_op jit(solution)/shard_map/layer_out/pallas_call | solution.py:336
  216.3 7.9 %layer_out.4 = (bf16[4096,512]{1,0:T(8,128)(2,1)}, f32[1024,512]{1,0:T(8,128)}) custom-call(s32[44]{0:T(128)} %concatenate.22.refs_0_.scal, f32[4096,512]{1,0:T(8,128)} %get-tuple-element.379.mid, bf16[4096,2048]{1,0:T(8,128)(2,1)} %get-tuple-element.380.hidden, bf16[1024,512]{1,0:T(8,128)(2,1)} %wd_a.3, ...), custom_call_target="tpu_custom_call", output_to_operand_aliasing={{0}: (6, {})} | custom-call | flops 2147483648 | bytes 7340032 | tf_op jit(solution)/shard_map/layer_out/pallas_call | solution.py:336
  227.8 5.2 %layer_out.5 = bf16[4096,512]{1,0:T(8,128)(2,1)} custom-call(s32[44]{0:T(128)} %concatenate.22.refs_0_.scal, f32[4096,512]{1,0:T(8,128)} %get-tuple-element.379.mid, bf16[4096,2048]{1,0:T(8,128)(2,1)} %get-tuple-element.380.hidden, bf16[1024,512]{1,0:T(8,128)(2,1)} %wd_a.3, bf16[1024,512]{1,0:T(8,128)(2,1)} %copy-done.1, ...), custom_call_target="tpu_custom_call", output_to_operand_aliasing={{}: (6, {})} | custom-call | flops 1073741824 | bytes 3670016 | tf_op jit(solution)/shard_map/layer_out/pallas_call | solution.py:336
  233.0 2.9 %unpack.1 = (f32[512,1024]{1,0:T(8,128)}, f32[256,512]{1,0:T(8,128)}, f32[1,512]{1,0:T(1,128)}, f32[1,512]{1,0:T(1,128)}, f32[1,512]{1,0:T(1,128)}, /*index=5*/f...) custom-call(s32[44]{0:T(128)S(1)} %copy-done.6, ...), custom_call_target="tpu_custom_call" | custom-call | bytes 7471104 | tf_op jit(solution)/shard_map/unpack/pallas_call | solution.py:336
  (143 shorter events, 25.7 us)
Async XLA Ops:
  3.0 17.8 %collective-permute-start = (bf16[1024,256]{1,0:T(8,128)(2,1)S(1)}, bf16[1024,256]{1,0:T(8,128)(2,1)S(1)}, u32[]{:S(2)}, u32[]{:S(2)}) collective-permute-start(bf16[1024,256]{1,0:T(8,128)(2,1)S(1)} %maximum_select_fusion), channel_id=1, source_target_pairs={{0,1},{1,0},{2,3},{3,2},{4,5},{5,4},{6,7},{7,6},{8,9},{9,8},{10,11... | collective-permute-start | bytes 1572872 | tf_op jit(solution)/shard_map/ppermute | solution.py:744
  6.0 14.8 %collective-permute-start.1 = (f32[2,256]{1,0:T(2,128)S(1)}, f32[2,256]{1,0:T(2,128)S(1)}, u32[]{:S(2)}, u32[]{:S(2)}) collective-permute-start(f32[2,256]{1,0:T(2,128)S(1)} %copy-done.25), channel_id=1, source_target_pairs={{0,1},{1,0},{2,3},{3,2},{4,5},{5,4},{6,7},{7,6},{8,9},{9,8},{10,11... | collective-permute-start | bytes 6152 | tf_op jit(solution)/shard_map/ppermute | solution.py:744
  22.9 14.3 %collective-permute-start.3 = (bf16[256,1024]{1,0:T(8,128)(2,1)S(1)}, bf16[256,1024]{1,0:T(8,128)(2,1)S(1)}, u32[]{:S(2)}, u32[]{:S(2)}) collective-permute-start(bf16[256,1024]{1,0:T(8,128)(2,1)S(1)} %constant_dynamic-slice_fusion), channel_id=1, source_target_pairs={{0,1},{1,0},{2,3},{3,2},{4,5},{5,4},{6,7},{7,6},{8,9},{9,8},{10,11... | collective-permute-start | bytes 1572872 | tf_op jit(solution)/shard_map/ppermute | solution.py:744
  24.9 12.3 %collective-permute-start.4 = (f32[1,1024]{1,0:T(1,128)S(1)}, f32[1,1024]{1,0:T(1,128)S(1)}, u32[]{:S(2)}, u32[]{:S(2)}) collective-permute-start(f32[1,1024]{1,0:T(1,128)S(1)} %bitcast.28), channel_id=1, source_target_pairs={{0,1},{1,0},{2,3},{3,2},{4,5},{5,4},{6,7},{7,6},{8,9},{9,8},{10,11... | collective-permute-start | bytes 12296 | tf_op jit(solution)/shard_map/ppermute | solution.py:744
  39.1 38.5 %collective-permute-start.6 = (bf16[1024,512]{1,0:T(8,128)(2,1)S(1)}, bf16[1024,512]{1,0:T(8,128)(2,1)S(1)}, u32[]{:S(2)}, u32[]{:S(2)}) collective-permute-start(bf16[1024,512]{1,0:T(8,128)(2,1)S(1)} %copy-done), channel_id=1, source_target_pairs={{0,1},{1,0},{2,3},{3,2},{4,5},{5,4},{6,7},{7,6},{8,9},{9,8},{10,11... | collective-permute-start | bytes 3145736 | tf_op jit(solution)/shard_map/ppermute | solution.py:744
  77.6 43.2 %collective-permute-start.7 = (bf16[16,32,1024]{2,1,0:T(8,128)(2,1)S(1)}, bf16[16,32,1024]{2,1,0:T(8,128)(2,1)S(1)}, u32[]{:S(2)}, u32[]{:S(2)}) collective-permute-start(bf16[16,32,1024]{2,1,0:T(8,128)(2,1)S(1)} %get-tuple-element.281), channel_id=1, source_target_pairs={{0,1},{1,0},{2,3},{3,2},{4,5},{5,4},{6,7},{7,6},{8,9},{9,8},{10,11... | collective-permute-start | bytes 3145736 | tf_op jit(solution)/shard_map/ppermute | solution.py:744
  124.4 20.6 %collective-permute-start.11 = (bf16[8,32,1408]{2,1,0:T(8,128)(2,1)S(1)}, bf16[8,32,1408]{2,1,0:T(8,128)(2,1)S(1)}, u32[]{:S(2)}, u32[]{:S(2)}) collective-permute-start(bf16[8,32,1408]{2,1,0:T(8,128)(2,1)S(1)} %add_convert_fusion.2), channel_id=1, source_target_pairs={{0,1},{1,0},{2,3},{3,2},{4,5},{5,4},{6,7},{7,6},{8,9},{9,8},{10,11... | collective-permute-start | bytes 2162696 | tf_op jit(solution)/shard_map/ppermute | solution.py:744
  126.2 19.2 %collective-permute-start.8 = (bf16[8,32,1408]{2,1,0:T(8,128)(2,1)S(1)}, bf16[8,32,1408]{2,1,0:T(8,128)(2,1)}, u32[]{:S(2)}, u32[]{:S(2)}) collective-permute-start(bf16[8,32,1408]{2,1,0:T(8,128)(2,1)S(1)} %get-tuple-element.283), channel_id=1, source_target_pairs={{0,2},{2,0},{4,6},{6,4},{8,10},{10,8},{12,14},{14,12},{16,18},{18,... | collective-permute-start | bytes 2162696 | tf_op jit(solution)/shard_map/ppermute | solution.py:747
  126.2 18.8 %collective-permute-start.12 = (bf16[4,32,1024]{2,1,0:T(8,128)(2,1)S(1)}, bf16[4,32,1024]{2,1,0:T(8,128)(2,1)S(1)}, u32[]{:S(2)}, u32[]{:S(2)}) collective-permute-start(bf16[4,32,1024]{2,1,0:T(8,128)(2,1)S(1)} %slice.70), channel_id=1, source_target_pairs={{0,8},{2,10},{4,12},{6,14},{8,0},{10,2},{12,4},{14,6},{16,24},{18,... | collective-permute-start | bytes 786440 | tf_op jit(solution)/shard_map/ppermute | solution.py:747
  147.3 22.1 %collective-permute-start.16 = (bf16[8,32,896]{2,1,0:T(8,128)(2,1)S(1)}, bf16[8,32,896]{2,1,0:T(8,128)(2,1)S(1)}, u32[]{:S(2)}, u32[]{:S(2)}) collective-permute-start(bf16[8,32,896]{2,1,0:T(8,128)(2,1)S(1)} %add_convert_fusion.5), channel_id=1, source_target_pairs={{0,1},{1,0},{2,3},{3,2},{4,5},{5,4},{6,7},{7,6},{8,9},{9,8},{10,11... | collective-permute-start | bytes 1376264 | tf_op jit(solution)/shard_map/ppermute | solution.py:744
  147.8 21.6 %collective-permute-start.15 = (bf16[4,32,1024]{2,1,0:T(8,128)(2,1)S(1)}, bf16[4,32,1024]{2,1,0:T(8,128)(2,1)S(1)}, u32[]{:S(2)}, u32[]{:S(2)}) collective-permute-start(bf16[4,32,1024]{2,1,0:T(8,128)(2,1)S(1)} %add_convert_fusion.9), channel_id=1, source_target_pairs={{0,16},{2,18},{4,20},{6,22},{8,24},{10,26},{12,28},{14,30},{16,0},... | collective-permute-start | bytes 786440 | tf_op jit(solution)/shard_map/ppermute | solution.py:747
  150.4 19.0 %collective-permute-start.14 = (bf16[4,32,1408]{2,1,0:T(8,128)(2,1)S(1)}, bf16[4,32,1408]{2,1,0:T(8,128)(2,1)S(1)}, u32[]{:S(2)}, u32[]{:S(2)}) collective-permute-start(bf16[4,32,1408]{2,1,0:T(8,128)(2,1)S(1)} %slice.72), channel_id=1, source_target_pairs={{0,4},{2,6},{4,0},{6,2},{8,12},{10,14},{12,8},{14,10},{16,20},{18,... | collective-permute-start | bytes 1081352 | tf_op jit(solution)/shard_map/ppermute | solution.py:747
  172.5 13.0 %collective-permute-start.18 = (bf16[2,32,1408]{2,1,0:T(8,128)(2,1)S(1)}, bf16[2,32,1408]{2,1,0:T(8,128)(2,1)S(1)}, u32[]{:S(2)}, u32[]{:S(2)}) collective-permute-start(bf16[2,32,1408]{2,1,0:T(8,128)(2,1)S(1)} %slice.75), channel_id=1, source_target_pairs={{0,8},{2,10},{4,12},{6,14},{8,0},{10,2},{12,4},{14,6},{16,24},{18,... | collective-permute-start | bytes 540680 | tf_op jit(solution)/shard_map/ppermute | solution.py:747
  173.1 12.5 %collective-permute-start.20 = (bf16[4,32,896]{2,1,0:T(8,128)(2,1)S(1)}, bf16[4,32,896]{2,1,0:T(8,128)(2,1)S(1)}, u32[]{:S(2)}, u32[]{:S(2)}) collective-permute-start(bf16[4,32,896]{2,1,0:T(8,128)(2,1)S(1)} %add_convert_fusion.13), channel_id=1, source_target_pairs={{0,8},{2,10},{4,12},{6,14},{8,0},{10,2},{12,4},{14,6},{16,24},{18,... | collective-permute-start | bytes 688136 | tf_op jit(solution)/shard_map/ppermute | solution.py:747
  174.6 10.9 %collective-permute-start.19 = (bf16[4,32,1024]{2,1,0:T(8,128)(2,1)S(1)}, bf16[4,32,1024]{2,1,0:T(8,128)(2,1)S(1)}, u32[]{:S(2)}, u32[]{:S(2)}) collective-permute-start(bf16[4,32,1024]{2,1,0:T(8,128)(2,1)S(1)} %add_convert_fusion.8), channel_id=1, source_target_pairs={{0,4},{2,6},{4,0},{6,2},{8,12},{10,14},{12,8},{14,10},{16,20},{18,... | collective-permute-start | bytes 786440 | tf_op jit(solution)/shard_map/ppermute | solution.py:747
  185.8 12.7 %collective-permute-start.21 = (bf16[2,32,1408]{2,1,0:T(8,128)(2,1)S(1)}, bf16[2,32,1408]{2,1,0:T(8,128)(2,1)S(1)}, u32[]{:S(2)}, u32[]{:S(2)}) collective-permute-start(bf16[2,32,1408]{2,1,0:T(8,128)(2,1)S(1)} %add_convert_fusion.15), channel_id=1, source_target_pairs={{0,16},{2,18},{4,20},{6,22},{8,24},{10,26},{12,28},{14,30},{16,0},... | collective-permute-start | bytes 540680 | tf_op jit(solution)/shard_map/ppermute | solution.py:747
  186.2 12.3 %collective-permute-start.23 = (bf16[4,32,896]{2,1,0:T(8,128)(2,1)S(1)}, bf16[4,32,896]{2,1,0:T(8,128)(2,1)S(1)}, u32[]{:S(2)}, u32[]{:S(2)}) collective-permute-start(bf16[4,32,896]{2,1,0:T(8,128)(2,1)S(1)} %add_convert_fusion.12), channel_id=1, source_target_pairs={{0,4},{2,6},{4,0},{6,2},{8,12},{10,14},{12,8},{14,10},{16,20},{18,... | collective-permute-start | bytes 688136 | tf_op jit(solution)/shard_map/ppermute | solution.py:747
  187.7 10.8 %collective-permute-start.22 = (bf16[4,32,1024]{2,1,0:T(8,128)(2,1)S(1)}, bf16[4,32,1024]{2,1,0:T(8,128)(2,1)S(1)}, u32[]{:S(2)}, u32[]{:S(2)}) collective-permute-start(bf16[4,32,1024]{2,1,0:T(8,128)(2,1)S(1)} %add_convert_fusion.7), channel_id=1, source_target_pairs={{0,8},{2,10},{4,12},{6,14},{8,0},{10,2},{12,4},{14,6},{16,24},{18,... | collective-permute-start | bytes 786440 | tf_op jit(solution)/shard_map/ppermute | solution.py:747
  198.8 16.3 %collective-permute-start.25 = (bf16[8,32,1024]{2,1,0:T(8,128)(2,1)S(1)}, bf16[8,32,1024]{2,1,0:T(8,128)(2,1)S(1)}, u32[]{:S(2)}, u32[]{:S(2)}) collective-permute-start(bf16[8,32,1024]{2,1,0:T(8,128)(2,1)S(1)} %pad_maximum_fusion.1.d0), channel_id=1, source_target_pairs={{0,2},{2,0},{4,6},{6,4},{8,10},{10,8},{12,14},{14,12},{16,18},{18,... | collective-permute-start | bytes 1572872 | tf_op jit(solution)/shard_map/ppermute | solution.py:747
  198.9 16.2 %collective-permute-start.24 = (bf16[2,32,1408]{2,1,0:T(8,128)(2,1)S(1)}, bf16[2,32,1408]{2,1,0:T(8,128)(2,1)S(1)}, u32[]{:S(2)}, u32[]{:S(2)}) collective-permute-start(bf16[2,32,1408]{2,1,0:T(8,128)(2,1)S(1)} %add_convert_fusion.14), channel_id=1, source_target_pairs={{0,8},{2,10},{4,12},{6,14},{8,0},{10,2},{12,4},{14,6},{16,24},{18,... | collective-permute-start | bytes 540680 | tf_op jit(solution)/shard_map/ppermute | solution.py:747
  200.5 14.6 %collective-permute-start.26 = (bf16[4,32,896]{2,1,0:T(8,128)(2,1)S(1)}, bf16[4,32,896]{2,1,0:T(8,128)(2,1)S(1)}, u32[]{:S(2)}, u32[]{:S(2)}) collective-permute-start(bf16[4,32,896]{2,1,0:T(8,128)(2,1)S(1)} %add_convert_fusion.11), channel_id=1, source_target_pairs={{0,16},{2,18},{4,20},{6,22},{8,24},{10,26},{12,28},{14,30},{16,0},... | collective-permute-start | bytes 688136 | tf_op jit(solution)/shard_map/ppermute | solution.py:747
  215.2 10.3 %collective-permute-start.27 = (bf16[4,32,1408]{2,1,0:T(8,128)(2,1)S(1)}, bf16[4,32,1408]{2,1,0:T(8,128)(2,1)S(1)}, u32[]{:S(2)}, u32[]{:S(2)}) collective-permute-start(bf16[4,32,1408]{2,1,0:T(8,128)(2,1)S(1)} %pad_maximum_fusion.3), channel_id=1, source_target_pairs={{0,4},{2,6},{4,0},{6,2},{8,12},{10,14},{12,8},{14,10},{16,20},{18,... | collective-permute-start | bytes 1081352 | tf_op jit(solution)/shard_map/ppermute | solution.py:747
  215.8 8.4 %collective-permute-start.28 = (bf16[4,32,896]{2,1,0:T(8,128)(2,1)S(1)}, bf16[4,32,896]{2,1,0:T(8,128)(2,1)S(1)}, u32[]{:S(2)}, u32[]{:S(2)}) collective-permute-start(bf16[4,32,896]{2,1,0:T(8,128)(2,1)S(1)} %add_convert_fusion.10), channel_id=1, source_target_pairs={{0,8},{2,10},{4,12},{6,14},{8,0},{10,2},{12,4},{14,6},{16,24},{18,... | collective-permute-start | bytes 688136 | tf_op jit(solution)/shard_map/ppermute | solution.py:747
  225.7 7.3 %collective-permute-start.29 = (bf16[8,32,1408]{2,1,0:T(8,128)(2,1)S(1)}, bf16[8,32,1408]{2,1,0:T(8,128)(2,1)S(1)}, u32[]{:S(2)}, u32[]{:S(2)}) collective-permute-start(bf16[8,32,1408]{2,1,0:T(8,128)(2,1)S(1)} %pad_maximum_fusion.u0), channel_id=1, source_target_pairs={{0,2},{2,0},{4,6},{6,4},{8,10},{10,8},{12,14},{14,12},{16,18},{18,... | collective-permute-start | bytes 2162696 | tf_op jit(solution)/shard_map/ppermute | solution.py:747
  (38 other events, 437.5 us)

commit v7 on v6

--- a/solution.py
+++ b/solution.py
@@ -165,7 +165,7 @@
 
 
 NEEDS = {
-    "attend_first": 60, "attend_second": 60, "feed_up": 49, "feed_back": 42, "attend_back": 60,
+    "attend_first": 60, "attend_second": 48, "feed_up": 47, "feed_back": 40, "attend_back": 60,
     "input_gradient": 60, "layer_out": 57, "unpack": 20,
 }
 

time: 237 us -> 235 us (level)
  transfers between devices with their start and end apart: 33 -> 33, of which waited for: 8 -> 7; matrix products, arithmetic and copies ran while one was open for 1% -> 1% of each run, Pallas kernels for 77% -> 77%
where the time goes in v7:
time: 235 us
  Pallas kernels  183 us (78%)
  starting transfers between devices  28.7 us (12%)
  waiting for transfers between devices  10.5 us (4%)
  local copies, waits for them, and re-layouts  7.74 us (3%)
  other arithmetic  3.18 us (1%)
    pallas_call x10, Pallas kernels, call(): pl.pallas_call(kernel, grid_spec=pltpu.PrefetchScalarGridSpec(num_scalar_...  159 us
    pallas_call x2, Pallas kernels, attention_forward(): pl.pallas_call(body, grid_spec=pltpu.PrefetchScalarGridSpec(num_scalar_pr...  24.3 us
    ppermute x23, starting transfers between devices, swap(): return lax.ppermute(v, 'dp', [(i, i ^ distance) for i in range(dp)])  17.5 us
    ppermute x9, starting transfers between devices, across(): return lax.ppermute(v, 'tensor', [(0, 1), (1, 0)])  11.2 us
    ppermute x23, waiting for transfers between devices, swap(): return lax.ppermute(v, 'dp', [(i, i ^ distance) for i in range(dp)])  10.5 us
  transfers between devices with their start and end apart: 33, of which 7 were waited for; matrix products, arithmetic and copies ran while one was open for 1% of the time, Pallas kernels for 77%

profile of v7, /device:TPU:0, one launch (start us, length us, event | category | flops | bytes accessed | tf_op | source)
XLA Modules:
  0.0 234.6 jit_solution(297506754221170912)
XLA Ops:
  3.0 3.0 %collective-permute-start = (bf16[1024,256]{1,0:T(8,128)(2,1)S(1)}, bf16[1024,256]{1,0:T(8,128)(2,1)S(1)}, u32[]{:S(2)}, u32[]{:S(2)}) collective-permute-start(bf16[1024,256]{1,0:T(8,128)(2,1)S(1)} %maximum_select_fusion), channel_id=1, source_target_pairs={{0,1},{1,0},{2,3},{3,2},{4,5},{5,4},{6,7},{7,6},{8,9},{9,8},{10,11... | collective-permute-start | bytes 1572872 | tf_op jit(solution)/shard_map/ppermute | solution.py:744
  6.9 13.9 %attend_first.1 = (bf16[4096,512]{1,0:T(8,128)(2,1)}, bf16[4096,512]{1,0:T(8,128)(2,1)}, bf16[4096,768]{1,0:T(8,128)(2,1)}, bf16[4096,256]{1,0:T(8,128)(2,1)}, b...) custom-call(s32[44]{0:T(128)} %concatenate.22.refs_0_.scal, bf16[4096,512]{1,0:T(8,128)(2,1)} %refs_1_.6, ...), custom_call_target="tpu_custom_call" | custom-call | flops 3892314112 | bytes 16777216 | tf_op jit(solution)/shard_map/attend_first/pallas_call | solution.py:211
  20.9 1.8 collective-permute-done.2.refs_3_.refs_7_.wo_t
  22.8 2.0 collective-permute-start.3
  24.9 10.4 %attend_second.1 = (bf16[4096,768]{1,0:T(8,128)(2,1)}, bf16[4096,256]{1,0:T(8,128)(2,1)S(1)}, bf16[5120,256]{1,0:T(8,128)(2,1)}, bf16[512,768]{1,0:T(8,128)(2,1)S(1)}) custom-call(s32[44]{0:T(128)S(1)} %copy-done.5, bf16[4096,512]{1,0:T(8,128)(2,1)} %get-tuple-element.225.refs_1_, bf16[1024,256]{1,0:T(8,128)(2,1)S(1)} %collective-permute-done.refs_2_.refs_6_.wo_m, ...), custom_call_target="tpu_custom_call" | custom-call | flops 3892314112 | bytes 16777216 | tf_op jit(solution)/shard_map/attend_second/pallas_call | solution.py:211
  37.6 1.9 collective-permute-done.5.refs_10_.wu_t
  39.5 1.9 collective-permute-start.6
  42.5 33.5 %feed_up.1 = (f32[4096,512]{1,0:T(8,128)}, bf16[4096,512]{1,0:T(8,128)(2,1)}, bf16[4096,2048]{1,0:T(8,128)(2,1)}, bf16[4096,2048]{1,0:T(8,128)(2,1)}, bf16[16,32...) custom-call(s32[44]{0:T(128)S(1)} %copy-done.5, bf16[4096,512]{1,0:T(8,128)(2,1)} %refs_1_.6, ...), custom_call_target="tpu_custom_call" | custom-call | flops 19327352832 | bytes 71303168 | tf_op jit(solution)/shard_map/feed_up/pallas_call | solution.py:336
  77.5 41.9 %feed_back.1 = (bf16[4096,512]{1,0:T(8,128)(2,1)}, bf16[4096,256]{1,0:T(8,128)(2,1)S(1)}, bf16[4096,256]{1,0:T(8,128)(2,1)S(1)}, bf16[8,32,1408]{2,1,0:T(8,128)(...) custom-call(s32[44]{0:T(128)S(1)} %copy-done.5, ...), custom_call_target="tpu_custom_call" | custom-call | flops 30064771072 | bytes 50331648 | tf_op jit(solution)/shard_map/feed_back/pallas_call | solution.py:336
  123.1 1.8 collective-permute-start.11
  124.8 1.6 collective-permute-start.12
  126.4 17.2 %attend_back.2 = (bf16[4096,768]{1,0:T(8,128)(2,1)}, bf16[8,32,896]{2,1,0:T(8,128)(2,1)}, bf16[8,32,896]{2,1,0:T(8,128)(2,1)}) custom-call(s32[44]{0:T(128)} %concatenate.22.refs_0_.scal, bf16[4096,512]{1,0:T(8,128)(2,1)} %get-tuple-element.311.refs_1_, bf16[4096,768]{1,0:T(8,128)(2,1)} %get-tuple-element.294.refs_2_, ...), custom_call_target="tpu_custom_call" | custom-call | flops 4563402752 | bytes 23068672 | tf_op jit(solution)/shard_map/attend_back/pallas_call | solution.py:336
  146.5 2.6 %collective-permute-start.15 = (bf16[4,32,1024]{2,1,0:T(8,128)(2,1)S(1)}, bf16[4,32,1024]{2,1,0:T(8,128)(2,1)S(1)}, u32[]{:S(2)}, u32[]{:S(2)}) collective-permute-start(bf16[4,32,1024]{2,1,0:T(8,128)(2,1)S(1)} %add_convert_fusion.9), channel_id=1, source_target_pairs={{0,16},{2,18},{4,20},{6,22},{8,24},{10,26},{12,28},{14,30},{16,0},... | collective-permute-start | bytes 786440 | tf_op jit(solution)/shard_map/ppermute | solution.py:747
  150.6 17.5 %attend_back.3 = (bf16[4096,768]{1,0:T(8,128)(2,1)}, bf16[8,32,896]{2,1,0:T(8,128)(2,1)}, bf16[8,32,896]{2,1,0:T(8,128)(2,1)}) custom-call(s32[44]{0:T(128)} %concatenate.22.refs_0_.scal, bf16[4096,512]{1,0:T(8,128)(2,1)} %get-tuple-element.311.refs_1_, bf16[4096,768]{1,0:T(8,128)(2,1)} %get-tuple-element.312.refs_2_, ...), custom_call_target="tpu_custom_call" | custom-call | flops 4563402752 | bytes 23068672 | tf_op jit(solution)/shard_map/attend_back/pallas_call | solution.py:336
  168.4 1.8 collective-permute-done.17
  171.7 1.6 collective-permute-start.20
  173.9 10.4 %input_gradient.2.refs_8_ = f32[4096,512]{1,0:T(8,128)} custom-call(s32[44]{0:T(128)} %concatenate.22.refs_0_.scal, bf16[4096,512]{1,0:T(8,128)(2,1)} %refs_1_.6, bf16[4096,512]{1,0:T(8,128)(2,1)} %get-tuple-element.342.refs_2_, bf16[4096,768]{1,0:T(8,128)(2,1)} %get-tuple-element.343.refs_3_, bf16[4096,768]{1,0:T(8,128)(2,1)} %get-tuple-element.344.refs_4_, ...), custom_call_target="tpu_custom_call" | custom-call | flops 3221225472 | bytes 16777216 | tf_op jit(solution)/shard_map/input_gradient/pallas_call | solution.py:336
  186.9 10.4 %input_gradient.3 = f32[4096,512]{1,0:T(8,128)} custom-call(s32[44]{0:T(128)} %concatenate.22.refs_0_.scal, bf16[4096,512]{1,0:T(8,128)(2,1)} %refs_1_.6, bf16[4096,512]{1,0:T(8,128)(2,1)} %get-tuple-element.342.refs_2_, bf16[4096,768]{1,0:T(8,128)(2,1)} %get-tuple-element.343.refs_3_, ...), custom_call_target="tpu_custom_call", output_to_operand_aliasing={{}: (8, {})} | custom-call | flops 3221225472 | bytes 16777216 | tf_op jit(solution)/shard_map/input_gradient/pallas_call | solution.py:336
  197.5 1.6 collective-permute-start.24
  199.2 2.6 %collective-permute-start.26 = (bf16[4,32,896]{2,1,0:T(8,128)(2,1)S(1)}, bf16[4,32,896]{2,1,0:T(8,128)(2,1)S(1)}, u32[]{:S(2)}, u32[]{:S(2)}) collective-permute-start(bf16[4,32,896]{2,1,0:T(8,128)(2,1)S(1)} %add_convert_fusion.11), channel_id=1, source_target_pairs={{0,16},{2,18},{4,20},{6,22},{8,24},{10,26},{12,28},{14,30},{16,0},... | collective-permute-start | bytes 688136 | tf_op jit(solution)/shard_map/ppermute | solution.py:747
  201.8 12.0 %layer_out.3.before = bf16[4096,512]{1,0:T(8,128)(2,1)} custom-call(s32[44]{0:T(128)} %concatenate.22.refs_0_.scal, f32[4096,512]{1,0:T(8,128)} %get-tuple-element.379.mid, bf16[4096,2048]{1,0:T(8,128)(2,1)} %get-tuple-element.380.hidden, bf16[1024,512]{1,0:T(8,128)(2,1)} %wd_a.3, bf16[1024,512]{1,0:T(8,128)(2,1)} %copy-done.1, f32[1,512]{1,0:T(1,128)} %bitcast.36), custom_call_target="tpu_custom_call" | custom-call | flops 5368709120 | bytes 18350080 | tf_op jit(solution)/shard_map/layer_out/pallas_call | solution.py:336
  215.0 7.9 %layer_out.4 = (bf16[4096,512]{1,0:T(8,128)(2,1)}, f32[1024,512]{1,0:T(8,128)}) custom-call(s32[44]{0:T(128)} %concatenate.22.refs_0_.scal, f32[4096,512]{1,0:T(8,128)} %get-tuple-element.379.mid, bf16[4096,2048]{1,0:T(8,128)(2,1)} %get-tuple-element.380.hidden, bf16[1024,512]{1,0:T(8,128)(2,1)} %wd_a.3, ...), custom_call_target="tpu_custom_call", output_to_operand_aliasing={{0}: (6, {})} | custom-call | flops 2147483648 | bytes 7340032 | tf_op jit(solution)/shard_map/layer_out/pallas_call | solution.py:336
  226.5 5.2 %layer_out.5 = bf16[4096,512]{1,0:T(8,128)(2,1)} custom-call(s32[44]{0:T(128)} %concatenate.22.refs_0_.scal, f32[4096,512]{1,0:T(8,128)} %get-tuple-element.379.mid, bf16[4096,2048]{1,0:T(8,128)(2,1)} %get-tuple-element.380.hidden, bf16[1024,512]{1,0:T(8,128)(2,1)} %wd_a.3, bf16[1024,512]{1,0:T(8,128)(2,1)} %copy-done.1, ...), custom_call_target="tpu_custom_call", output_to_operand_aliasing={{}: (6, {})} | custom-call | flops 1073741824 | bytes 3670016 | tf_op jit(solution)/shard_map/layer_out/pallas_call | solution.py:336
  231.7 2.9 %unpack.1 = (f32[512,1024]{1,0:T(8,128)}, f32[256,512]{1,0:T(8,128)}, f32[1,512]{1,0:T(1,128)}, f32[1,512]{1,0:T(1,128)}, f32[1,512]{1,0:T(1,128)}, /*index=5*/f...) custom-call(s32[44]{0:T(128)S(1)} %copy-done.6, ...), custom_call_target="tpu_custom_call" | custom-call | bytes 7471104 | tf_op jit(solution)/shard_map/unpack/pallas_call | solution.py:336
  (139 shorter events, 25.8 us)
Async XLA Ops:
  3.0 17.8 %collective-permute-start = (bf16[1024,256]{1,0:T(8,128)(2,1)S(1)}, bf16[1024,256]{1,0:T(8,128)(2,1)S(1)}, u32[]{:S(2)}, u32[]{:S(2)}) collective-permute-start(bf16[1024,256]{1,0:T(8,128)(2,1)S(1)} %maximum_select_fusion), channel_id=1, source_target_pairs={{0,1},{1,0},{2,3},{3,2},{4,5},{5,4},{6,7},{7,6},{8,9},{9,8},{10,11... | collective-permute-start | bytes 1572872 | tf_op jit(solution)/shard_map/ppermute | solution.py:744
  6.0 14.7 %collective-permute-start.1 = (f32[2,256]{1,0:T(2,128)S(1)}, f32[2,256]{1,0:T(2,128)S(1)}, u32[]{:S(2)}, u32[]{:S(2)}) collective-permute-start(f32[2,256]{1,0:T(2,128)S(1)} %copy-done.24), channel_id=1, source_target_pairs={{0,1},{1,0},{2,3},{3,2},{4,5},{5,4},{6,7},{7,6},{8,9},{9,8},{10,11... | collective-permute-start | bytes 6152 | tf_op jit(solution)/shard_map/ppermute | solution.py:744
  22.8 14.8 %collective-permute-start.3 = (bf16[256,1024]{1,0:T(8,128)(2,1)S(1)}, bf16[256,1024]{1,0:T(8,128)(2,1)S(1)}, u32[]{:S(2)}, u32[]{:S(2)}) collective-permute-start(bf16[256,1024]{1,0:T(8,128)(2,1)S(1)} %constant_dynamic-slice_fusion), channel_id=1, source_target_pairs={{0,1},{1,0},{2,3},{3,2},{4,5},{5,4},{6,7},{7,6},{8,9},{9,8},{10,11... | collective-permute-start | bytes 1572872 | tf_op jit(solution)/shard_map/ppermute | solution.py:744
  24.8 12.8 %collective-permute-start.4 = (f32[1,1024]{1,0:T(1,128)S(1)}, f32[1,1024]{1,0:T(1,128)S(1)}, u32[]{:S(2)}, u32[]{:S(2)}) collective-permute-start(f32[1,1024]{1,0:T(1,128)S(1)} %bitcast.28), channel_id=1, source_target_pairs={{0,1},{1,0},{2,3},{3,2},{4,5},{5,4},{6,7},{7,6},{8,9},{9,8},{10,11... | collective-permute-start | bytes 12296 | tf_op jit(solution)/shard_map/ppermute | solution.py:744
  39.5 36.5 %collective-permute-start.6 = (bf16[1024,512]{1,0:T(8,128)(2,1)S(1)}, bf16[1024,512]{1,0:T(8,128)(2,1)S(1)}, u32[]{:S(2)}, u32[]{:S(2)}) collective-permute-start(bf16[1024,512]{1,0:T(8,128)(2,1)S(1)} %copy-done), channel_id=1, source_target_pairs={{0,1},{1,0},{2,3},{3,2},{4,5},{5,4},{6,7},{7,6},{8,9},{9,8},{10,11... | collective-permute-start | bytes 3145736 | tf_op jit(solution)/shard_map/ppermute | solution.py:744
  76.1 43.3 %collective-permute-start.7 = (bf16[16,32,1024]{2,1,0:T(8,128)(2,1)S(1)}, bf16[16,32,1024]{2,1,0:T(8,128)(2,1)S(1)}, u32[]{:S(2)}, u32[]{:S(2)}) collective-permute-start(bf16[16,32,1024]{2,1,0:T(8,128)(2,1)S(1)} %get-tuple-element.281), channel_id=1, source_target_pairs={{0,1},{1,0},{2,3},{3,2},{4,5},{5,4},{6,7},{7,6},{8,9},{9,8},{10,11... | collective-permute-start | bytes 3145736 | tf_op jit(solution)/shard_map/ppermute | solution.py:744
  123.1 20.6 %collective-permute-start.11 = (bf16[8,32,1408]{2,1,0:T(8,128)(2,1)S(1)}, bf16[8,32,1408]{2,1,0:T(8,128)(2,1)S(1)}, u32[]{:S(2)}, u32[]{:S(2)}) collective-permute-start(bf16[8,32,1408]{2,1,0:T(8,128)(2,1)S(1)} %add_convert_fusion.2), channel_id=1, source_target_pairs={{0,1},{1,0},{2,3},{3,2},{4,5},{5,4},{6,7},{7,6},{8,9},{9,8},{10,11... | collective-permute-start | bytes 2162696 | tf_op jit(solution)/shard_map/ppermute | solution.py:744
  124.8 19.2 %collective-permute-start.8 = (bf16[8,32,1408]{2,1,0:T(8,128)(2,1)}, bf16[8,32,1408]{2,1,0:T(8,128)(2,1)S(1)}, u32[]{:S(2)}, u32[]{:S(2)}) collective-permute-start(bf16[8,32,1408]{2,1,0:T(8,128)(2,1)} %get-tuple-element.283), channel_id=1, source_target_pairs={{0,2},{2,0},{4,6},{6,4},{8,10},{10,8},{12,14},{14,12},{16,18},{18,... | collective-permute-start | bytes 2162696 | tf_op jit(solution)/shard_map/ppermute | solution.py:747
  124.8 18.8 %collective-permute-start.12 = (bf16[4,32,1024]{2,1,0:T(8,128)(2,1)S(1)}, bf16[4,32,1024]{2,1,0:T(8,128)(2,1)S(1)}, u32[]{:S(2)}, u32[]{:S(2)}) collective-permute-start(bf16[4,32,1024]{2,1,0:T(8,128)(2,1)S(1)} %slice.70), channel_id=1, source_target_pairs={{0,8},{2,10},{4,12},{6,14},{8,0},{10,2},{12,4},{14,6},{16,24},{18,... | collective-permute-start | bytes 786440 | tf_op jit(solution)/shard_map/ppermute | solution.py:747
  145.9 22.2 %collective-permute-start.16 = (bf16[8,32,896]{2,1,0:T(8,128)(2,1)S(1)}, bf16[8,32,896]{2,1,0:T(8,128)(2,1)S(1)}, u32[]{:S(2)}, u32[]{:S(2)}) collective-permute-start(bf16[8,32,896]{2,1,0:T(8,128)(2,1)S(1)} %add_convert_fusion.5), channel_id=1, source_target_pairs={{0,1},{1,0},{2,3},{3,2},{4,5},{5,4},{6,7},{7,6},{8,9},{9,8},{10,11... | collective-permute-start | bytes 1376264 | tf_op jit(solution)/shard_map/ppermute | solution.py:744
  146.5 21.6 %collective-permute-start.15 = (bf16[4,32,1024]{2,1,0:T(8,128)(2,1)S(1)}, bf16[4,32,1024]{2,1,0:T(8,128)(2,1)S(1)}, u32[]{:S(2)}, u32[]{:S(2)}) collective-permute-start(bf16[4,32,1024]{2,1,0:T(8,128)(2,1)S(1)} %add_convert_fusion.9), channel_id=1, source_target_pairs={{0,16},{2,18},{4,20},{6,22},{8,24},{10,26},{12,28},{14,30},{16,0},... | collective-permute-start | bytes 786440 | tf_op jit(solution)/shard_map/ppermute | solution.py:747
  149.1 19.0 %collective-permute-start.14 = (bf16[4,32,1408]{2,1,0:T(8,128)(2,1)S(1)}, bf16[4,32,1408]{2,1,0:T(8,128)(2,1)S(1)}, u32[]{:S(2)}, u32[]{:S(2)}) collective-permute-start(bf16[4,32,1408]{2,1,0:T(8,128)(2,1)S(1)} %slice.72), channel_id=1, source_target_pairs={{0,4},{2,6},{4,0},{6,2},{8,12},{10,14},{12,8},{14,10},{16,20},{18,... | collective-permute-start | bytes 1081352 | tf_op jit(solution)/shard_map/ppermute | solution.py:747
  171.2 13.0 %collective-permute-start.18 = (bf16[2,32,1408]{2,1,0:T(8,128)(2,1)S(1)}, bf16[2,32,1408]{2,1,0:T(8,128)(2,1)S(1)}, u32[]{:S(2)}, u32[]{:S(2)}) collective-permute-start(bf16[2,32,1408]{2,1,0:T(8,128)(2,1)S(1)} %slice.75), channel_id=1, source_target_pairs={{0,8},{2,10},{4,12},{6,14},{8,0},{10,2},{12,4},{14,6},{16,24},{18,... | collective-permute-start | bytes 540680 | tf_op jit(solution)/shard_map/ppermute | solution.py:747
  171.7 12.5 %collective-permute-start.20 = (bf16[4,32,896]{2,1,0:T(8,128)(2,1)S(1)}, bf16[4,32,896]{2,1,0:T(8,128)(2,1)S(1)}, u32[]{:S(2)}, u32[]{:S(2)}) collective-permute-start(bf16[4,32,896]{2,1,0:T(8,128)(2,1)S(1)} %add_convert_fusion.13), channel_id=1, source_target_pairs={{0,8},{2,10},{4,12},{6,14},{8,0},{10,2},{12,4},{14,6},{16,24},{18,... | collective-permute-start | bytes 688136 | tf_op jit(solution)/shard_map/ppermute | solution.py:747
  173.3 10.9 %collective-permute-start.19 = (bf16[4,32,1024]{2,1,0:T(8,128)(2,1)S(1)}, bf16[4,32,1024]{2,1,0:T(8,128)(2,1)S(1)}, u32[]{:S(2)}, u32[]{:S(2)}) collective-permute-start(bf16[4,32,1024]{2,1,0:T(8,128)(2,1)S(1)} %add_convert_fusion.8), channel_id=1, source_target_pairs={{0,4},{2,6},{4,0},{6,2},{8,12},{10,14},{12,8},{14,10},{16,20},{18,... | collective-permute-start | bytes 786440 | tf_op jit(solution)/shard_map/ppermute | solution.py:747
  184.5 12.7 %collective-permute-start.21 = (bf16[2,32,1408]{2,1,0:T(8,128)(2,1)S(1)}, bf16[2,32,1408]{2,1,0:T(8,128)(2,1)S(1)}, u32[]{:S(2)}, u32[]{:S(2)}) collective-permute-start(bf16[2,32,1408]{2,1,0:T(8,128)(2,1)S(1)} %add_convert_fusion.15), channel_id=1, source_target_pairs={{0,16},{2,18},{4,20},{6,22},{8,24},{10,26},{12,28},{14,30},{16,0},... | collective-permute-start | bytes 540680 | tf_op jit(solution)/shard_map/ppermute | solution.py:747
  184.9 12.3 %collective-permute-start.23 = (bf16[4,32,896]{2,1,0:T(8,128)(2,1)S(1)}, bf16[4,32,896]{2,1,0:T(8,128)(2,1)S(1)}, u32[]{:S(2)}, u32[]{:S(2)}) collective-permute-start(bf16[4,32,896]{2,1,0:T(8,128)(2,1)S(1)} %add_convert_fusion.12), channel_id=1, source_target_pairs={{0,4},{2,6},{4,0},{6,2},{8,12},{10,14},{12,8},{14,10},{16,20},{18,... | collective-permute-start | bytes 688136 | tf_op jit(solution)/shard_map/ppermute | solution.py:747
  186.4 10.9 %collective-permute-start.22 = (bf16[4,32,1024]{2,1,0:T(8,128)(2,1)S(1)}, bf16[4,32,1024]{2,1,0:T(8,128)(2,1)S(1)}, u32[]{:S(2)}, u32[]{:S(2)}) collective-permute-start(bf16[4,32,1024]{2,1,0:T(8,128)(2,1)S(1)} %add_convert_fusion.7), channel_id=1, source_target_pairs={{0,8},{2,10},{4,12},{6,14},{8,0},{10,2},{12,4},{14,6},{16,24},{18,... | collective-permute-start | bytes 786440 | tf_op jit(solution)/shard_map/ppermute | solution.py:747
  197.5 16.3 %collective-permute-start.25 = (bf16[8,32,1024]{2,1,0:T(8,128)(2,1)S(1)}, bf16[8,32,1024]{2,1,0:T(8,128)(2,1)S(1)}, u32[]{:S(2)}, u32[]{:S(2)}) collective-permute-start(bf16[8,32,1024]{2,1,0:T(8,128)(2,1)S(1)} %pad_maximum_fusion.1.d0), channel_id=1, source_target_pairs={{0,2},{2,0},{4,6},{6,4},{8,10},{10,8},{12,14},{14,12},{16,18},{18,... | collective-permute-start | bytes 1572872 | tf_op jit(solution)/shard_map/ppermute | solution.py:747
  197.5 16.2 %collective-permute-start.24 = (bf16[2,32,1408]{2,1,0:T(8,128)(2,1)S(1)}, bf16[2,32,1408]{2,1,0:T(8,128)(2,1)S(1)}, u32[]{:S(2)}, u32[]{:S(2)}) collective-permute-start(bf16[2,32,1408]{2,1,0:T(8,128)(2,1)S(1)} %add_convert_fusion.14), channel_id=1, source_target_pairs={{0,8},{2,10},{4,12},{6,14},{8,0},{10,2},{12,4},{14,6},{16,24},{18,... | collective-permute-start | bytes 540680 | tf_op jit(solution)/shard_map/ppermute | solution.py:747
  199.2 14.6 %collective-permute-start.26 = (bf16[4,32,896]{2,1,0:T(8,128)(2,1)S(1)}, bf16[4,32,896]{2,1,0:T(8,128)(2,1)S(1)}, u32[]{:S(2)}, u32[]{:S(2)}) collective-permute-start(bf16[4,32,896]{2,1,0:T(8,128)(2,1)S(1)} %add_convert_fusion.11), channel_id=1, source_target_pairs={{0,16},{2,18},{4,20},{6,22},{8,24},{10,26},{12,28},{14,30},{16,0},... | collective-permute-start | bytes 688136 | tf_op jit(solution)/shard_map/ppermute | solution.py:747
  213.9 10.3 %collective-permute-start.27 = (bf16[4,32,1408]{2,1,0:T(8,128)(2,1)S(1)}, bf16[4,32,1408]{2,1,0:T(8,128)(2,1)S(1)}, u32[]{:S(2)}, u32[]{:S(2)}) collective-permute-start(bf16[4,32,1408]{2,1,0:T(8,128)(2,1)S(1)} %pad_maximum_fusion.3), channel_id=1, source_target_pairs={{0,4},{2,6},{4,0},{6,2},{8,12},{10,14},{12,8},{14,10},{16,20},{18,... | collective-permute-start | bytes 1081352 | tf_op jit(solution)/shard_map/ppermute | solution.py:747
  214.5 8.4 %collective-permute-start.28 = (bf16[4,32,896]{2,1,0:T(8,128)(2,1)S(1)}, bf16[4,32,896]{2,1,0:T(8,128)(2,1)S(1)}, u32[]{:S(2)}, u32[]{:S(2)}) collective-permute-start(bf16[4,32,896]{2,1,0:T(8,128)(2,1)S(1)} %add_convert_fusion.10), channel_id=1, source_target_pairs={{0,8},{2,10},{4,12},{6,14},{8,0},{10,2},{12,4},{14,6},{16,24},{18,... | collective-permute-start | bytes 688136 | tf_op jit(solution)/shard_map/ppermute | solution.py:747
  224.4 7.3 %collective-permute-start.29 = (bf16[8,32,1408]{2,1,0:T(8,128)(2,1)S(1)}, bf16[8,32,1408]{2,1,0:T(8,128)(2,1)S(1)}, u32[]{:S(2)}, u32[]{:S(2)}) collective-permute-start(bf16[8,32,1408]{2,1,0:T(8,128)(2,1)S(1)} %pad_maximum_fusion.u0), channel_id=1, source_target_pairs={{0,2},{2,0},{4,6},{6,4},{8,10},{10,8},{12,14},{14,12},{16,18},{18,... | collective-permute-start | bytes 2162696 | tf_op jit(solution)/shard_map/ppermute | solution.py:747
  (36 other events, 355.8 us)
